TPU v7x, 32 devices: a whole 2x2x4 slice. The times are simulated.
32 devices in a mesh: shard: 4 (over y, x), ctx: 2 (over z_hi), tp: 4 (over z_lo, core).
Axes of the slice: x: 2, y: 2, z: 4 (z_hi: 2, z_lo: 2; z = z_hi * 2 + z_lo), core: 2. Of those that a mesh axis runs over, the one named last changes fastest.
Arguments:
- tokens_in: bfloat16 [2, 4, 384, 2048], P(None, 'shard', 'ctx'), may hold values from -6 to 6
- cotangent: bfloat16 [2, 4, 384, 2048], P(None, 'shard', 'ctx'), may hold values from -6 to 6
- expert_ids: int32 [2, 4, 384, 4], P(None, 'shard', 'ctx'), may hold values from 0 to 7, all different within a row; in each aligned block of 192 rows (0 to 191, 192 to 383, ..., all dimensions but the last counted through in order) at most 128 rows name the same one
- prefix_len: int32 [2, 4], P(None, 'shard'), may hold values from 0 to 384
- attn_gain: bfloat16 [2048], P('shard'), may hold values from 0.5 to 1.5
- qkv_weight: bfloat16 [3, 2048, 2048], P(None, 'shard', 'tp'), may hold values from -0.125 to 0.125
- qkv_bias: bfloat16 [3, 16, 128], P(None, 'tp'), may hold values from -1 to 1
- out_weight: bfloat16 [2048, 2048], P('tp', 'shard'), may hold values from -2 to 2
- ffn_gain: bfloat16 [2048], P('shard'), may hold values from 0.5 to 1.5
- router_weight: bfloat16 [2048, 8], P('shard'), may hold values from -0.0625 to 0.0625
- expert_gate: bfloat16 [8, 2048, 1408], P(None, 'shard', 'tp'), may hold values from -0.125 to 0.125
- expert_up: bfloat16 [8, 2048, 1408], P(None, 'shard', 'tp'), may hold values from -0.125 to 0.125
- expert_down: bfloat16 [8, 1408, 2048], P(None, 'tp', 'shard'), may hold values from -0.625 to 0.625
- shared_gate: bfloat16 [2048, 5632], P('shard', 'tp'), may hold values from -0.125 to 0.125
- shared_up: bfloat16 [2048, 5632], P('shard', 'tp'), may hold values from -0.125 to 0.125
- shared_down: bfloat16 [5632, 2048], P('tp', 'shard'), may hold values from -0.15625 to 0.15625
- shared_switch: bfloat16 [2048], P('shard'), may hold values from -0.125 to 0.125
Outputs:
- layer_out: bfloat16 [2, 4, 384, 2048], P(None, 'shard', 'ctx')
- tokens_grad: float32 [2, 4, 384, 2048], P(None, 'shard', 'ctx')
- attn_gain_grad: float32 [2048], P(('shard', 'ctx'))
- qkv_weight_grad: float32 [3, 2048, 2048], P(None, ('shard', 'ctx'), 'tp')
- qkv_bias_grad: float32 [3, 16, 128], P(None, 'tp', ('shard', 'ctx'))
- out_weight_grad: float32 [2048, 2048], P('tp', ('shard', 'ctx'))
- ffn_gain_grad: float32 [2048], P(('shard', 'ctx'))
- router_grad: float32 [2048, 8], P(('shard', 'ctx'))
- expert_gate_grad: float32 [8, 2048, 1408], P(None, ('shard', 'ctx'), 'tp')
- expert_up_grad: float32 [8, 2048, 1408], P(None, ('shard', 'ctx'), 'tp')
- expert_down_grad: float32 [8, 1408, 2048], P(None, 'tp', ('shard', 'ctx'))
- shared_gate_grad: float32 [2048, 5632], P(('shard', 'ctx'), 'tp')
- shared_up_grad: float32 [2048, 5632], P(('shard', 'ctx'), 'tp')
- shared_down_grad: float32 [5632, 2048], P('tp', ('shard', 'ctx'))
- switch_grad: float32 [2048], P(('shard', 'ctx'))
Inputs may be any that keep to these rules, and one draw needn't show every extreme that they name: `expert_ids`: each token names 4 different experts. Among the 192 positions of a sequence that one index of ctx holds, no expert is named by more than 128 tokens, and one expert by exactly 128.
All inputs are finite; a program needn't handle non-finite values.
Results may differ from a plain program's by a relative error of at most 0.04.
Values may be sent and summed in bfloat16 or wider, within the bound.
No kernel may reach another device: no remote copies, remote signals or barrier semaphores. Data moves between devices by JAX's collectives and lax.ppermute only.
A program may use at most 320 MiB of HBM per device.

v0:
```python
import jax
import jax.numpy as jnp
from jax import lax
from jax.sharding import PartitionSpec as P

epsilon = 1e-06
rope_base = 1000000.0
highest = lax.Precision.HIGHEST


def rms_scale(values, gain_vec):
    factor = lax.rsqrt(jnp.mean(values * values, axis=-1, keepdims=True) + epsilon)
    return values * factor * gain_vec


def swiglu(gate_in, up_in):
    return jax.nn.silu(gate_in) * up_in


def rope_tables(length, head_dim):
    half_dim = head_dim // 2
    frequency = rope_base ** (-(jnp.arange(half_dim, dtype=jnp.float32) * 2.0) / head_dim)
    places = jnp.arange(length, dtype=jnp.float32)[:, None] * frequency[None, :]
    return (jnp.cos(places)[:, None, :], jnp.sin(places)[:, None, :])


def rotate(values, cosine, sine_table):
    half_dim = values.shape[-1] // 2
    first_half = values[..., :half_dim]
    second_half = values[..., half_dim:]
    return jnp.concatenate(
        [
            first_half * cosine - second_half * sine_table,
            second_half * cosine + first_half * sine_table,
        ],
        axis=-1,
    )


def visible(length, prefix_value):
    places = jnp.arange(length, dtype=jnp.int32)
    return (places[None, :] <= places[:, None]) | (places[None, :] < prefix_value)


def attend_scores(query_rows, key_rows, allowed, score_scale):
    raw_scores = (
        jnp.einsum("qhd,khd->hqk", query_rows, key_rows, preferred_element_type=jnp.float32)
        * score_scale
    )
    return jnp.where(allowed[None], raw_scores, -1000000000.0)


def dispatch(id_rows, experts, slot_room):
    token_count = id_rows.shape[0]
    pick_count = id_rows.shape[1]
    flat_ids = id_rows.reshape(-1)
    expert_marks = (flat_ids[:, None] == jnp.arange(experts, dtype=jnp.int32)[None, :]).astype(
        jnp.int32
    )
    expert_rank = jnp.sum((jnp.cumsum(expert_marks, axis=0) - 1) * expert_marks, axis=1)
    slot_index = flat_ids * slot_room + expert_rank
    token_owner = jnp.arange(token_count * pick_count, dtype=jnp.int32) // pick_count
    slot_owner = (
        jnp.full((experts * slot_room,), token_count, jnp.int32).at[slot_index].set(token_owner)
    )
    return (slot_index, slot_owner)


def collect(shards):
    return (
        lax.all_gather(shards[0], "shard", axis=0, tiled=True),
        lax.all_gather(shards[1], "shard", axis=1, tiled=True),
        lax.all_gather(shards[2], "shard", axis=1, tiled=True),
        lax.all_gather(shards[3], "shard", axis=0, tiled=True),
        lax.all_gather(shards[4], "shard", axis=0, tiled=True),
        lax.all_gather(shards[5], "shard", axis=1, tiled=True),
        lax.all_gather(shards[6], "shard", axis=1, tiled=True),
        lax.all_gather(shards[7], "shard", axis=2, tiled=True),
        lax.all_gather(shards[8], "shard", axis=0, tiled=True),
        lax.all_gather(shards[9], "shard", axis=0, tiled=True),
        lax.all_gather(shards[10], "shard", axis=1, tiled=True),
        lax.all_gather(shards[11], "shard", axis=0, tiled=True),
    )


def reduce_grads(grad_list):
    return (
        lax.psum_scatter(
            grad_list[0].astype(jnp.bfloat16), ("shard", "ctx"), scatter_dimension=0, tiled=True
        ).astype(jnp.float32),
        lax.psum_scatter(
            grad_list[1].astype(jnp.bfloat16), ("shard", "ctx"), scatter_dimension=1, tiled=True
        ).astype(jnp.float32),
        lax.psum_scatter(
            grad_list[2].astype(jnp.bfloat16), ("shard", "ctx"), scatter_dimension=2, tiled=True
        ).astype(jnp.float32),
        lax.psum_scatter(
            grad_list[3].astype(jnp.bfloat16), ("shard", "ctx"), scatter_dimension=1, tiled=True
        ).astype(jnp.float32),
        lax.psum_scatter(
            grad_list[4].astype(jnp.bfloat16), ("shard", "ctx"), scatter_dimension=0, tiled=True
        ).astype(jnp.float32),
        lax.psum_scatter(
            grad_list[5].astype(jnp.bfloat16), ("shard", "ctx"), scatter_dimension=0, tiled=True
        ).astype(jnp.float32),
        lax.psum_scatter(
            grad_list[6].astype(jnp.bfloat16), ("shard", "ctx"), scatter_dimension=1, tiled=True
        ).astype(jnp.float32),
        lax.psum_scatter(
            grad_list[7].astype(jnp.bfloat16), ("shard", "ctx"), scatter_dimension=1, tiled=True
        ).astype(jnp.float32),
        lax.psum_scatter(
            grad_list[8].astype(jnp.bfloat16), ("shard", "ctx"), scatter_dimension=2, tiled=True
        ).astype(jnp.float32),
        lax.psum_scatter(
            grad_list[9].astype(jnp.bfloat16), ("shard", "ctx"), scatter_dimension=0, tiled=True
        ).astype(jnp.float32),
        lax.psum_scatter(
            grad_list[10].astype(jnp.bfloat16), ("shard", "ctx"), scatter_dimension=0, tiled=True
        ).astype(jnp.float32),
        lax.psum_scatter(
            grad_list[11].astype(jnp.bfloat16), ("shard", "ctx"), scatter_dimension=1, tiled=True
        ).astype(jnp.float32),
        lax.psum_scatter(
            grad_list[12].astype(jnp.bfloat16), ("shard", "ctx"), scatter_dimension=0, tiled=True
        ).astype(jnp.float32),
    )


def micro_step(full_weights, qkv_bias, tokens_row, cotan_row, ids_row, prefix_value):
    (
        attn_gain,
        qkv_weight,
        out_weight,
        ffn_gain,
        router_weight,
        expert_gate,
        expert_up,
        expert_down,
        shared_gate,
        shared_up,
        shared_down,
        shared_switch,
    ) = full_weights
    token_count = tokens_row.shape[0]
    width = tokens_row.shape[1]
    length = token_count * lax.axis_size("ctx")
    local_heads = qkv_bias.shape[1]
    head_dim = qkv_bias.shape[2]
    experts = router_weight.shape[1]
    pick_count = ids_row.shape[1]
    slot_room = token_count * pick_count * 4 // (3 * experts)
    score_scale = head_dim ** (-0.5)
    inputs = tokens_row.astype(jnp.float32)
    first_gain = attn_gain.astype(jnp.float32)
    normed_float, first_pull = jax.vjp(rms_scale, inputs, first_gain)
    normed_one = normed_float.astype(jnp.bfloat16)
    bias_rows = qkv_bias.reshape(3, 1, local_heads * head_dim).astype(jnp.float32)
    projected = (
        jnp.einsum("sd,kde->kse", normed_one, qkv_weight, preferred_element_type=jnp.float32)
        + bias_rows
    )
    projected = projected.astype(jnp.bfloat16).reshape(3, token_count, local_heads, head_dim)
    by_heads = lax.all_to_all(projected, "ctx", split_axis=2, concat_axis=1, tiled=True)
    cosine, sine_table = rope_tables(length, head_dim)
    query_rows = rotate(by_heads[0].astype(jnp.float32), cosine, sine_table).astype(jnp.bfloat16)
    key_rows = rotate(by_heads[1].astype(jnp.float32), cosine, sine_table).astype(jnp.bfloat16)
    value_rows = by_heads[2]
    allowed = visible(length, prefix_value)
    scores = attend_scores(query_rows, key_rows, allowed, score_scale)
    score_top = jnp.max(scores, axis=-1, keepdims=True)
    raised = jnp.exp(scores - score_top)
    score_total = jnp.sum(raised, axis=-1, keepdims=True)
    log_total = score_top + jnp.log(score_total)
    probs_low = (raised / score_total).astype(jnp.bfloat16)
    attended = jnp.einsum(
        "hqk,khd->qhd", probs_low, value_rows, preferred_element_type=jnp.float32
    ).astype(jnp.bfloat16)
    head_rows = lax.all_to_all(attended, "ctx", split_axis=0, concat_axis=1, tiled=True).reshape(
        token_count, local_heads * head_dim
    )
    attn_part = jnp.dot(head_rows, out_weight, preferred_element_type=jnp.float32)
    attn_total = lax.psum(attn_part, "tp")
    hidden_res = inputs + attn_total
    second_gain = ffn_gain.astype(jnp.float32)
    second_float, second_pull = jax.vjp(rms_scale, hidden_res, second_gain)
    normed_two = second_float.astype(jnp.bfloat16)
    logits = jnp.dot(normed_two, router_weight, preferred_element_type=jnp.float32)
    router_probs = jax.nn.softmax(logits, axis=-1)
    expert_marks = (
        ids_row[:, :, None] == jnp.arange(experts, dtype=jnp.int32)[None, None, :]
    ).astype(jnp.float32)
    gate_values = jnp.sum(expert_marks * router_probs[:, None, :], axis=-1)
    slot_index, slot_owner = dispatch(ids_row, experts, slot_room)
    padded_two = jnp.concatenate([normed_two, jnp.zeros((1, width), jnp.bfloat16)], axis=0)
    expert_rows = padded_two[slot_owner].reshape(experts, slot_room, width)
    gate_pre = jnp.einsum(
        "ecd,edf->ecf", expert_rows, expert_gate, preferred_element_type=jnp.float32
    )
    up_pre = jnp.einsum("ecd,edf->ecf", expert_rows, expert_up, preferred_element_type=jnp.float32)
    act_float, act_pull = jax.vjp(swiglu, gate_pre, up_pre)
    expert_act = act_float.astype(jnp.bfloat16)
    expert_res = jnp.einsum(
        "ecf,efd->ecd", expert_act, expert_down, preferred_element_type=jnp.float32
    ).reshape(experts * slot_room, width)
    picked = expert_res[slot_index].reshape(token_count, pick_count, width)
    mixture = jnp.sum(gate_values[:, :, None] * picked, axis=1)
    shared_pre = jnp.dot(normed_two, shared_gate, preferred_element_type=jnp.float32)
    shared_lin = jnp.dot(normed_two, shared_up, preferred_element_type=jnp.float32)
    shared_float, shared_pull = jax.vjp(swiglu, shared_pre, shared_lin)
    shared_act = shared_float.astype(jnp.bfloat16)
    shared_res = jnp.dot(shared_act, shared_down, preferred_element_type=jnp.float32)
    switch = jax.nn.sigmoid(jnp.dot(normed_two, shared_switch, preferred_element_type=jnp.float32))
    ffn_total = lax.psum(
        (mixture + switch[:, None] * shared_res).astype(jnp.bfloat16), "tp"
    ).astype(jnp.float32)
    layer_out = (hidden_res + ffn_total).astype(jnp.bfloat16)
    upstream = cotan_row.astype(jnp.float32)
    padded_up = jnp.concatenate([upstream, jnp.zeros((1, width), jnp.float32)], axis=0)
    slot_gates = (
        jnp.zeros((experts * slot_room,), jnp.float32).at[slot_index].set(gate_values.reshape(-1))
    )
    res_grad = (
        (slot_gates[:, None] * padded_up[slot_owner])
        .astype(jnp.bfloat16)
        .reshape(experts, slot_room, width)
    )
    gate_grads = jnp.sum(picked * upstream[:, None, :], axis=-1)
    switch_part = jnp.sum(upstream * shared_res, axis=-1)
    act_grad = jnp.einsum(
        "ecd,efd->ecf", res_grad, expert_down, preferred_element_type=jnp.float32
    ).astype(jnp.bfloat16)
    gate_pre_grad, up_pre_grad = act_pull(act_grad.astype(jnp.float32))
    gate_pre_low = gate_pre_grad.astype(jnp.bfloat16)
    up_pre_low = up_pre_grad.astype(jnp.bfloat16)
    expert_gate_grad = jnp.einsum(
        "ecd,ecf->edf", expert_rows, gate_pre_low, preferred_element_type=jnp.float32
    )
    expert_up_grad = jnp.einsum(
        "ecd,ecf->edf", expert_rows, up_pre_low, preferred_element_type=jnp.float32
    )
    expert_down_grad = jnp.einsum(
        "ecf,ecd->efd", expert_act, res_grad, preferred_element_type=jnp.float32
    )
    row_grads = jnp.einsum(
        "ecf,edf->ecd", gate_pre_low, expert_gate, preferred_element_type=jnp.float32
    ) + jnp.einsum("ecf,edf->ecd", up_pre_low, expert_up, preferred_element_type=jnp.float32)
    normed_grad = (
        jnp.zeros((token_count + 1, width), jnp.float32)
        .at[slot_owner]
        .add(row_grads.reshape(experts * slot_room, width))[:token_count]
    )
    shared_res_grad = (switch[:, None] * upstream).astype(jnp.bfloat16)
    shared_act_grad = jnp.dot(
        shared_res_grad, shared_down.T, preferred_element_type=jnp.float32
    ).astype(jnp.bfloat16)
    shared_pre_grad, shared_lin_grad = shared_pull(shared_act_grad.astype(jnp.float32))
    shared_pre_low = shared_pre_grad.astype(jnp.bfloat16)
    shared_lin_low = shared_lin_grad.astype(jnp.bfloat16)
    shared_down_grad = jnp.dot(shared_act.T, shared_res_grad, preferred_element_type=jnp.float32)
    shared_gate_grad = jnp.dot(normed_two.T, shared_pre_low, preferred_element_type=jnp.float32)
    shared_up_grad = jnp.dot(normed_two.T, shared_lin_low, preferred_element_type=jnp.float32)
    normed_grad = (
        normed_grad
        + jnp.dot(shared_pre_low, shared_gate.T, preferred_element_type=jnp.float32)
        + jnp.dot(shared_lin_low, shared_up.T, preferred_element_type=jnp.float32)
    )
    normed_grad, gate_grads, switch_raw = (
        lax.psum(normed_grad.astype(jnp.bfloat16), "tp").astype(jnp.float32),
        lax.psum(gate_grads.astype(jnp.bfloat16), "tp").astype(jnp.float32),
        lax.psum(switch_part.astype(jnp.bfloat16), "tp").astype(jnp.float32),
    )
    prob_grads = jnp.sum(expert_marks * gate_grads[:, :, None], axis=1)
    logit_grads = router_probs * (
        prob_grads - jnp.sum(router_probs * prob_grads, axis=-1, keepdims=True)
    )
    normed_two_float = normed_two.astype(jnp.float32)
    router_grad = jnp.dot(normed_two_float.T, logit_grads, precision=highest)
    switch_pre_grad = switch_raw * switch * (1.0 - switch)
    switch_grad = jnp.dot(switch_pre_grad, normed_two_float, precision=highest)
    normed_grad = (
        normed_grad
        + jnp.dot(logit_grads, router_weight.astype(jnp.float32).T, precision=highest)
        + switch_pre_grad[:, None] * shared_switch.astype(jnp.float32)[None, :]
    )
    hidden_norm_grad, ffn_gain_grad = second_pull(normed_grad)
    hidden_grad = upstream + hidden_norm_grad
    branch_low = hidden_grad.astype(jnp.bfloat16)
    out_weight_grad = jnp.dot(head_rows.T, branch_low, preferred_element_type=jnp.float32)
    head_grad = (
        jnp.dot(branch_low, out_weight.T, preferred_element_type=jnp.float32)
        .astype(jnp.bfloat16)
        .reshape(token_count, local_heads, head_dim)
    )
    head_grad_seq = lax.all_to_all(head_grad, "ctx", split_axis=1, concat_axis=0, tiled=True)
    scores = attend_scores(query_rows, key_rows, allowed, score_scale)
    probs_again = jnp.exp(scores - log_total)
    probs_back = probs_again.astype(jnp.bfloat16)
    prob_grad = jnp.einsum(
        "qhd,khd->hqk", head_grad_seq, value_rows, preferred_element_type=jnp.float32
    )
    value_grad = jnp.einsum(
        "hqk,qhd->khd", probs_back, head_grad_seq, preferred_element_type=jnp.float32
    )
    score_grad = probs_again * (
        prob_grad - jnp.sum(probs_again * prob_grad, axis=-1, keepdims=True)
    )
    score_low = score_grad.astype(jnp.bfloat16)
    query_grad = (
        jnp.einsum("hqk,khd->qhd", score_low, key_rows, preferred_element_type=jnp.float32)
        * score_scale
    )
    key_grad = (
        jnp.einsum("hqk,qhd->khd", score_low, query_rows, preferred_element_type=jnp.float32)
        * score_scale
    )
    query_grad = rotate(query_grad, cosine, -sine_table)
    key_grad = rotate(key_grad, cosine, -sine_table)
    stacked = jnp.stack([query_grad, key_grad, value_grad]).astype(jnp.bfloat16)
    proj_grad = lax.all_to_all(stacked, "ctx", split_axis=1, concat_axis=2, tiled=True).reshape(
        3, token_count, local_heads * head_dim
    )
    bias_grad = jnp.sum(proj_grad.astype(jnp.float32), axis=1).reshape(3, local_heads, head_dim)
    qkv_grad = jnp.einsum("sd,kse->kde", normed_one, proj_grad, preferred_element_type=jnp.float32)
    normed_one_grad = jnp.einsum(
        "kse,kde->sd", proj_grad, qkv_weight, preferred_element_type=jnp.float32
    )
    normed_one_grad = lax.psum(normed_one_grad.astype(jnp.bfloat16), "tp").astype(jnp.float32)
    input_norm_grad, attn_gain_grad = first_pull(normed_one_grad)
    tokens_grad = hidden_grad + input_norm_grad
    grads = (
        attn_gain_grad,
        qkv_grad,
        bias_grad,
        out_weight_grad,
        ffn_gain_grad,
        router_grad,
        expert_gate_grad,
        expert_up_grad,
        expert_down_grad,
        shared_gate_grad,
        shared_up_grad,
        shared_down_grad,
        switch_grad,
    )
    return (layer_out, tokens_grad, grads)


def body(
    tokens_in,
    cotangent,
    expert_ids,
    prefix_len,
    attn_gain,
    qkv_weight,
    qkv_bias,
    out_weight,
    ffn_gain,
    router_weight,
    expert_gate,
    expert_up,
    expert_down,
    shared_gate,
    shared_up,
    shared_down,
    shared_switch,
):
    shards = (
        attn_gain,
        qkv_weight,
        out_weight,
        ffn_gain,
        router_weight,
        expert_gate,
        expert_up,
        expert_down,
        shared_gate,
        shared_up,
        shared_down,
        shared_switch,
    )
    outputs = []
    input_grads = []
    summed = None
    for batch_index in range(tokens_in.shape[0]):
        full_weights = collect(shards)
        layer_out, tokens_grad, grads = micro_step(
            full_weights,
            qkv_bias,
            tokens_in[batch_index, 0],
            cotangent[batch_index, 0],
            expert_ids[batch_index, 0],
            prefix_len[batch_index, 0],
        )
        outputs.append(layer_out)
        input_grads.append(tokens_grad)
        grads = reduce_grads(grads)
        if summed is None:
            summed = grads
        else:
            summed = tuple((earlier + later for earlier, later in zip(summed, grads)))
    return (jnp.stack(outputs)[:, None], jnp.stack(input_grads)[:, None]) + tuple(summed)


def solution(mesh):
    in_specs = (
        P(None, "shard", "ctx", None),
        P(None, "shard", "ctx", None),
        P(None, "shard", "ctx", None),
        P(None, "shard"),
        P("shard"),
        P(None, "shard", "tp"),
        P(None, "tp", None),
        P("tp", "shard"),
        P("shard"),
        P("shard", None),
        P(None, "shard", "tp"),
        P(None, "shard", "tp"),
        P(None, "tp", "shard"),
        P("shard", "tp"),
        P("shard", "tp"),
        P("tp", "shard"),
        P("shard"),
    )
    out_specs = (
        P(None, "shard", "ctx", None),
        P(None, "shard", "ctx", None),
        P(("shard", "ctx")),
        P(None, ("shard", "ctx"), "tp"),
        P(None, "tp", ("shard", "ctx")),
        P("tp", ("shard", "ctx")),
        P(("shard", "ctx")),
        P(("shard", "ctx"), None),
        P(None, ("shard", "ctx"), "tp"),
        P(None, ("shard", "ctx"), "tp"),
        P(None, "tp", ("shard", "ctx")),
        P(("shard", "ctx"), "tp"),
        P(("shard", "ctx"), "tp"),
        P("tp", ("shard", "ctx")),
        P(("shard", "ctx")),
    )
    return jax.shard_map(body, mesh=mesh, in_specs=in_specs, out_specs=out_specs, check_vma=False)
```

profile of v0, /device:TPU:0, one launch (start us, length us, event | category | flops | bytes accessed | tf_op | source)
XLA Modules:
  0.0 5728.6 jit_solution(9796219697283529521)
XLA Ops:
  21.4 61.4 %all-gather.12.cloned.1.call-done = bf16[3,2048,512]{2,1,0:T(8,128)(2,1)} async-done(((bf16[3,512,512]{2,1,0:T(8,128)(2,1)}), bf16[3,2048,512]{2,1,0:T(8,128)(2,1)}) %all-gather.12.cloned.1.call-update) | async-done | bytes 6291472 | tf_op jit(solution)/shard_map/all_gather | solution.py:72
  291.8 63.5 %all-gather.24.cloned.1.call-done = bf16[2048,1408]{1,0:T(8,128)(2,1)} async-done(((bf16[512,1408]{1,0:T(8,128)(2,1)}), bf16[2048,1408]{1,0:T(8,128)(2,1)}) %all-gather.24.cloned.1.call-update) | async-done | bytes 5767184 | tf_op jit(solution)/shard_map/all_gather | solution.py:80
  360.3 62.3 %all-gather.26.cloned.1.call-done = bf16[1408,2048]{1,0:T(8,128)(2,1)} async-done(((bf16[1408,512]{1,0:T(8,128)(2,1)}), bf16[1408,2048]{1,0:T(8,128)(2,1)}) %all-gather.26.cloned.1.call-update) | async-done | bytes 5767184 | tf_op jit(solution)/shard_map/all_gather | solution.py:81
  435.4 102.7 %all-gather.18.cloned.1.call-done = bf16[8,2048,352]{1,2,0:T(8,128)(2,1)} async-done(((bf16[8,512,352]{1,2,0:T(8,128)(2,1)}), bf16[8,2048,352]{1,2,0:T(8,128)(2,1)}) %all-gather.18.cloned.1.call-update) | async-done | bytes 11534352 | tf_op jit(solution)/shard_map/all_gather | solution.py:77
  545.6 108.1 %all-gather.20.cloned.1.call-done = bf16[8,352,2048]{2,1,0:T(8,128)(2,1)} async-done(((bf16[8,352,512]{2,1,0:T(8,128)(2,1)}), bf16[8,352,2048]{2,1,0:T(8,128)(2,1)}) %all-gather.20.cloned.1.call-update) | async-done | bytes 11534352 | tf_op jit(solution)/shard_map/all_gather | solution.py:78
  663.7 105.5 %all-gather.16.cloned.1.call-done = bf16[8,2048,352]{1,2,0:T(8,128)(2,1)} async-done(((bf16[8,512,352]{1,2,0:T(8,128)(2,1)}), bf16[8,2048,352]{1,2,0:T(8,128)(2,1)}) %all-gather.16.cloned.1.call-update) | async-done | bytes 11534352 | tf_op jit(solution)/shard_map/all_gather | solution.py:76
  974.7 40.8 all-reduce.23.cloned.1.call-done
  1233.1 47.1 all-reduce.21.cloned.1.call-done
  1283.1 43.9 all-reduce.11
  1375.0 90.3 %reduce-scatter.29.cloned.1.call-done = bf16[512,256]{1,0:T(8,128)(2,1)} async-done(((bf16[512,2048]{1,0:T(8,128)(2,1)}), bf16[512,256]{1,0:T(8,128)(2,1)}) %reduce-scatter.29.cloned.1.call-update) | async-done | bytes 262160 | tf_op jit(solution)/shard_map/reduce_scatter | solution.py:97
  1467.1 224.5 %reduce-scatter.57.cloned.1.call-done = bf16[1408,256]{1,0:T(8,128)(2,1)} async-done(((bf16[1408,2048]{1,0:T(8,128)(2,1)}), bf16[1408,256]{1,0:T(8,128)(2,1)}) %reduce-scatter.57.cloned.1.call-update) | async-done | bytes 720912 | tf_op jit(solution)/shard_map/reduce_scatter | solution.py:121
  1691.6 227.7 %reduce-scatter.59.cloned.1.call-done = bf16[1408,256]{1,0:T(8,128)(2,1)} async-done(((bf16[1408,2048]{1,0:T(8,128)(2,1)}), bf16[1408,256]{1,0:T(8,128)(2,1)}) %reduce-scatter.59.cloned.1.call-update) | async-done | bytes 720912 | tf_op jit(solution)/shard_map/reduce_scatter | solution.py:121
  1921.9 225.0 %reduce-scatter.53.cloned.1.call-done = bf16[256,1408]{1,0:T(8,128)(2,1)} async-done(((bf16[2048,1408]{1,0:T(8,128)(2,1)}), bf16[256,1408]{1,0:T(8,128)(2,1)}) %reduce-scatter.53.cloned.1.call-update) | async-done | bytes 720912 | tf_op jit(solution)/shard_map/reduce_scatter | solution.py:118
  2146.9 227.7 %reduce-scatter.55.cloned.1.call-done = bf16[256,1408]{1,0:T(8,128)(2,1)} async-done(((bf16[2048,1408]{1,0:T(8,128)(2,1)}), bf16[256,1408]{1,0:T(8,128)(2,1)}) %reduce-scatter.55.cloned.1.call-update) | async-done | bytes 720912 | tf_op jit(solution)/shard_map/reduce_scatter | solution.py:118
  2377.2 225.1 %reduce-scatter.49.cloned.1.call-done = bf16[256,1408]{1,0:T(8,128)(2,1)} async-done(((bf16[2048,1408]{1,0:T(8,128)(2,1)}), bf16[256,1408]{1,0:T(8,128)(2,1)}) %reduce-scatter.49.cloned.1.call-update) | async-done | bytes 720912 | tf_op jit(solution)/shard_map/reduce_scatter | solution.py:115
  2602.3 227.7 %reduce-scatter.51.cloned.1.call-done = bf16[256,1408]{1,0:T(8,128)(2,1)} async-done(((bf16[2048,1408]{1,0:T(8,128)(2,1)}), bf16[256,1408]{1,0:T(8,128)(2,1)}) %reduce-scatter.51.cloned.1.call-update) | async-done | bytes 720912 | tf_op jit(solution)/shard_map/reduce_scatter | solution.py:115
  2832.6 107.9 %reduce-scatter.27.cloned.1.call-done = bf16[3,256,512]{1,2,0:T(8,128)(2,1)} async-done(((bf16[3,2048,512]{1,2,0:T(8,128)(2,1)}), bf16[3,256,512]{1,2,0:T(8,128)(2,1)}) %reduce-scatter.27.cloned.1.call-update) | async-done | bytes 786448 | tf_op jit(solution)/shard_map/reduce_scatter | solution.py:91
  2940.5 111.3 %reduce-scatter.25.cloned.1.call-done = bf16[3,256,512]{1,2,0:T(8,128)(2,1)} async-done(((bf16[3,2048,512]{1,2,0:T(8,128)(2,1)}), bf16[3,256,512]{1,2,0:T(8,128)(2,1)}) %reduce-scatter.25.cloned.1.call-update) | async-done | bytes 786448 | tf_op jit(solution)/shard_map/reduce_scatter | solution.py:91
  3054.9 441.1 %reduce-scatter.45.cloned.1.call-done = bf16[8,352,256]{2,1,0:T(8,128)(2,1)} async-done(((bf16[8,352,2048]{2,1,0:T(8,128)(2,1)}), bf16[8,352,256]{2,1,0:T(8,128)(2,1)}) %reduce-scatter.45.cloned.1.call-update) | async-done | bytes 1441808 | tf_op jit(solution)/shard_map/reduce_scatter | solution.py:112
  3496.0 444.2 %reduce-scatter.47.cloned.1.call-done = bf16[8,352,256]{2,1,0:T(8,128)(2,1)} async-done(((bf16[8,352,2048]{2,1,0:T(8,128)(2,1)}), bf16[8,352,256]{2,1,0:T(8,128)(2,1)}) %reduce-scatter.47.cloned.1.call-update) | async-done | bytes 1441808 | tf_op jit(solution)/shard_map/reduce_scatter | solution.py:112
  3943.9 440.7 %reduce-scatter.43.cloned.1.call-done = bf16[8,256,352]{1,2,0:T(8,128)(2,1)} async-done(((bf16[8,2048,352]{1,2,0:T(8,128)(2,1)}), bf16[8,256,352]{1,2,0:T(8,128)(2,1)}) %reduce-scatter.43.cloned.1.call-update) | async-done | bytes 1441808 | tf_op jit(solution)/shard_map/reduce_scatter | solution.py:109
  4384.6 444.4 %reduce-scatter.41.cloned.1.call-done = bf16[8,256,352]{1,2,0:T(8,128)(2,1)} async-done(((bf16[8,2048,352]{1,2,0:T(8,128)(2,1)}), bf16[8,256,352]{1,2,0:T(8,128)(2,1)}) %reduce-scatter.41.cloned.1.call-update) | async-done | bytes 1441808 | tf_op jit(solution)/shard_map/reduce_scatter | solution.py:109
  4832.6 440.6 %reduce-scatter.39.cloned.1.call-done = bf16[8,256,352]{1,2,0:T(8,128)(2,1)} async-done(((bf16[8,2048,352]{1,2,0:T(8,128)(2,1)}), bf16[8,256,352]{1,2,0:T(8,128)(2,1)}) %reduce-scatter.39.cloned.1.call-update) | async-done | bytes 1441808 | tf_op jit(solution)/shard_map/reduce_scatter | solution.py:106
  5273.2 444.4 %reduce-scatter.37.cloned.1.call-done = bf16[8,256,352]{1,2,0:T(8,128)(2,1)} async-done(((bf16[8,2048,352]{1,2,0:T(8,128)(2,1)}), bf16[8,256,352]{1,2,0:T(8,128)(2,1)}) %reduce-scatter.37.cloned.1.call-update) | async-done | bytes 1441808 | tf_op jit(solution)/shard_map/reduce_scatter | solution.py:106
  (740 shorter events, 752.3 us)
Async XLA Ops:
  154.6 200.7 %all-gather.24.cloned.1.call-start = ((), (), s32[]{:S(2)}) async-start(), calls=%async_computation.34 | async-start | bytes 7208960 | tf_op jit(solution)/shard_map/all_gather | solution.py:80
  155.2 267.4 %all-gather.26.cloned.1.call-start = ((), (), s32[]{:S(2)}) async-start(), calls=%async_computation.35 | async-start | bytes 7208960 | tf_op jit(solution)/shard_map/all_gather | solution.py:81
  155.7 382.4 %all-gather.18.cloned.1.call-start = ((), (), s32[]{:S(2)}) async-start(), calls=%async_computation.31 | async-start | bytes 14417920 | tf_op jit(solution)/shard_map/all_gather | solution.py:77
  156.5 497.2 %all-gather.20.cloned.1.call-start = ((), (), s32[]{:S(2)}) async-start(), calls=%async_computation.32 | async-start | bytes 14417920 | tf_op jit(solution)/shard_map/all_gather | solution.py:78
  157.3 611.9 %all-gather.16.cloned.1.call-start = ((), (), s32[]{:S(2)}) async-start(), calls=%async_computation.30 | async-start | bytes 14417920 | tf_op jit(solution)/shard_map/all_gather | solution.py:76
  158.0 857.4 %all-reduce.23.cloned.1.call-start = ((), (), s32[]{:S(2)}) async-start(), calls=%async_computation.58 | async-start | bytes 3145728 | tf_op jit(solution)/shard_map/psum | solution.py:269
  1056.6 172.9 %reduce-scatter.33.cloned.1.call-start = ((), (), s32[]{:S(2)}) async-start(), calls=%async_computation.40 | async-start | bytes 36864 | tf_op jit(solution)/shard_map/reduce_scatter | solution.py:103
  1096.1 184.2 %all-reduce.21.cloned.1.call-start = ((), (), s32[]{:S(2)}) async-start(), calls=%async_computation.57 | async-start | bytes 6291456 | tf_op jit(solution)/shard_map/psum | solution.py:214
  1108.3 266.7 %reduce-scatter.31.cloned.1.call-start = ((), (), s32[]{:S(2)}) async-start(), calls=%async_computation.39 | async-start | bytes 2359296 | tf_op jit(solution)/shard_map/reduce_scatter | solution.py:97
  1111.8 353.5 %reduce-scatter.29.cloned.1.call-start = ((), (), s32[]{:S(2)}) async-start(), calls=%async_computation.38 | async-start | bytes 2359296 | tf_op jit(solution)/shard_map/reduce_scatter | solution.py:97
  1115.2 576.4 %reduce-scatter.57.cloned.1.call-start = ((), (), s32[]{:S(2)}) async-start(), calls=%async_computation.52 | async-start | bytes 6488064 | tf_op jit(solution)/shard_map/reduce_scatter | solution.py:121
  1122.0 797.4 %reduce-scatter.59.cloned.1.call-start = ((), (), s32[]{:S(2)}) async-start(), calls=%async_computation.53 | async-start | bytes 6488064 | tf_op jit(solution)/shard_map/reduce_scatter | solution.py:121
  1127.3 1019.6 %reduce-scatter.53.cloned.1.call-start = ((), (), s32[]{:S(2)}) async-start(), calls=%async_computation.50 | async-start | bytes 6488064 | tf_op jit(solution)/shard_map/reduce_scatter | solution.py:118
  1132.7 1241.9 %reduce-scatter.55.cloned.1.call-start = ((), (), s32[]{:S(2)}) async-start(), calls=%async_computation.51 | async-start | bytes 6488064 | tf_op jit(solution)/shard_map/reduce_scatter | solution.py:118
  1138.1 1464.3 %reduce-scatter.49.cloned.1.call-start = ((), (), s32[]{:S(2)}) async-start(), calls=%async_computation.48 | async-start | bytes 6488064 | tf_op jit(solution)/shard_map/reduce_scatter | solution.py:115
  1143.4 1686.7 %reduce-scatter.51.cloned.1.call-start = ((), (), s32[]{:S(2)}) async-start(), calls=%async_computation.49 | async-start | bytes 6488064 | tf_op jit(solution)/shard_map/reduce_scatter | solution.py:115
  1148.7 1791.8 %reduce-scatter.27.cloned.1.call-start = ((), (), s32[]{:S(2)}) async-start(), calls=%async_computation.37 | async-start | bytes 7077888 | tf_op jit(solution)/shard_map/reduce_scatter | solution.py:91
  1155.7 1896.0 %reduce-scatter.25.cloned.1.call-start = ((), (), s32[]{:S(2)}) async-start(), calls=%async_computation.36 | async-start | bytes 7077888 | tf_op jit(solution)/shard_map/reduce_scatter | solution.py:91
  1162.1 2333.9 %reduce-scatter.45.cloned.1.call-start = ((), (), s32[]{:S(2)}) async-start(), calls=%async_computation.46 | async-start | bytes 12976128 | tf_op jit(solution)/shard_map/reduce_scatter | solution.py:112
  1173.9 2766.3 %reduce-scatter.47.cloned.1.call-start = ((), (), s32[]{:S(2)}) async-start(), calls=%async_computation.47 | async-start | bytes 12976128 | tf_op jit(solution)/shard_map/reduce_scatter | solution.py:112
  1185.5 3199.0 %reduce-scatter.43.cloned.1.call-start = ((), (), s32[]{:S(2)}) async-start(), calls=%async_computation.45 | async-start | bytes 12976128 | tf_op jit(solution)/shard_map/reduce_scatter | solution.py:109
  1195.9 3633.1 %reduce-scatter.41.cloned.1.call-start = ((), (), s32[]{:S(2)}) async-start(), calls=%async_computation.44 | async-start | bytes 12976128 | tf_op jit(solution)/shard_map/reduce_scatter | solution.py:109
  1206.2 4066.9 %reduce-scatter.39.cloned.1.call-start = ((), (), s32[]{:S(2)}) async-start(), calls=%async_computation.43 | async-start | bytes 12976128 | tf_op jit(solution)/shard_map/reduce_scatter | solution.py:106
  1216.4 4501.1 %reduce-scatter.37.cloned.1.call-start = ((), (), s32[]{:S(2)}) async-start(), calls=%async_computation.42 | async-start | bytes 12976128 | tf_op jit(solution)/shard_map/reduce_scatter | solution.py:106
  (211 other events, 4899.1 us)
Sparse Core Ops, SparseCore 0:
  9.9 72.8 all-gather.11
  154.1 66.0 all-reduce.18
  221.9 65.7 all-gather.21
  289.4 65.7 all-gather.23
  424.4 113.6 all-gather.17
  539.9 113.6 all-gather.19
  655.5 113.6 all-gather.15
  1214.0 66.2 all-reduce.20
  1283.0 91.9 reduce-scatter.30
  1377.7 87.5 reduce-scatter.28
  1467.4 224.1 reduce-scatter.56
  1693.9 225.3 reduce-scatter.58
  1921.5 225.3 reduce-scatter.52
  2149.2 225.3 reduce-scatter.54
  2376.9 225.3 reduce-scatter.48
  2604.6 225.3 reduce-scatter.50
  2833.9 106.5 reduce-scatter.26
  2945.0 106.7 reduce-scatter.24
  3053.9 442.0 reduce-scatter.44
  3498.1 442.0 reduce-scatter.46
  3942.5 442.0 reduce-scatter.42
  4386.9 442.0 reduce-scatter.40
  4831.1 442.0 reduce-scatter.38
  5275.5 442.0 reduce-scatter.36
  (7 shorter events, 285.8 us)
where the time goes:
time: 5740 us; the launch traced here: 5730 us
  waiting for transfers between devices  5060 us (88%)
  matrix products  297 us (5%)
  local copies, waits for them, and re-layouts  124 us (2%)
  other arithmetic  110 us (2%)
  blocking collectives  83.9 us (1%)
    reduce_scatter x2, waiting for transfers between devices, reduce_grads(): lax.psum_scatter(grad_list[8].astype(jnp.bfloat16), ('shard', 'ctx'), sca...  885 us
    reduce_scatter x2, waiting for transfers between devices, reduce_grads(): lax.psum_scatter(grad_list[7].astype(jnp.bfloat16), ('shard', 'ctx'), sca...  885 us
    reduce_scatter x2, waiting for transfers between devices, reduce_grads(): lax.psum_scatter(grad_list[6].astype(jnp.bfloat16), ('shard', 'ctx'), sca...  885 us
    reduce_scatter x2, waiting for transfers between devices, reduce_grads(): lax.psum_scatter(grad_list[9].astype(jnp.bfloat16), ('shard', 'ctx'), sca...  453 us
    reduce_scatter x2, waiting for transfers between devices, reduce_grads(): lax.psum_scatter(grad_list[10].astype(jnp.bfloat16), ('shard', 'ctx'), sc...  453 us
    reduce_scatter x2, waiting for transfers between devices, reduce_grads(): lax.psum_scatter(grad_list[11].astype(jnp.bfloat16), ('shard', 'ctx'), sc...  452 us
    reduce_scatter x2, waiting for transfers between devices, reduce_grads(): lax.psum_scatter(grad_list[1].astype(jnp.bfloat16), ('shard', 'ctx'), sca...  219 us
    reduce_scatter x2, waiting for transfers between devices, reduce_grads(): lax.psum_scatter(grad_list[3].astype(jnp.bfloat16), ('shard', 'ctx'), sca...  129 us
  transfers between devices with their start and end apart: 39, of which 34 were waited for; matrix products, arithmetic and copies ran while one was open for 5% of the time, Pallas kernels for 0%

commit v1 on v0

v1 whole, which is shorter than its diff:
```python
import jax
import jax.numpy as jnp
import numpy as np
from jax import lax
from jax.sharding import PartitionSpec as P

epsilon = 1e-06
rope_base = 1000000.0
highest = lax.Precision.HIGHEST
f32 = jnp.float32
bf16 = jnp.bfloat16


def rms_scale(values, gain_vec):
    factor = lax.rsqrt(jnp.mean(values * values, axis=-1, keepdims=True) + epsilon)
    return values * factor * gain_vec


def rope_tables(length, head_dim):
    half_dim = head_dim // 2
    frequency = rope_base ** (-(np.arange(half_dim) * 2.0) / head_dim)
    places = np.arange(length)[:, None] * frequency[None, :]
    return jnp.asarray(np.cos(places), f32), jnp.asarray(np.sin(places), f32)


def rotate(values, cosine, sine_table):
    half_dim = values.shape[-1] // 2
    first_half = values[..., :half_dim]
    second_half = values[..., half_dim:]
    return jnp.concatenate(
        [
            first_half * cosine - second_half * sine_table,
            second_half * cosine + first_half * sine_table,
        ],
        axis=-1,
    )


def dot(left, right):
    return jnp.dot(left, right, preferred_element_type=f32)


def dot_rows(left, right):
    return lax.dot_general(left, right, (((0,), (0,)), ((), ())), preferred_element_type=f32)


def dot_cols(left, right):
    return lax.dot_general(left, right, (((1,), (1,)), ((), ())), preferred_element_type=f32)


def swap(values, axis, bit):
    count = lax.axis_size(axis)
    return lax.ppermute(values, axis, [(i, i ^ bit) for i in range(count)])


def pick(values, place, axis):
    return lax.dynamic_index_in_dim(values, place, axis, keepdims=False)


def sum_tp(terms):
    count = lax.axis_size("tp")
    place = lax.axis_index("tp")
    bit = 1
    while bit < count:
        pairs = terms.reshape((terms.shape[0] // 2, 2) + terms.shape[1:])
        low = (place // bit) % 2
        sent = pick(pairs, 1 - low, 1).astype(bf16)
        terms = pick(pairs, low, 1).astype(f32) + swap(sent, "tp", bit).astype(f32)
        bit *= 2
    return terms[0]


def gather_tp(block):
    count = lax.axis_size("tp")
    place = lax.axis_index("tp")
    held = block[None]
    bit = count // 2
    while bit >= 1:
        other = swap(held, "tp", bit)
        high = (place // bit) % 2
        held = jnp.where(
            high == 0, jnp.stack([held, other], 1), jnp.stack([other, held], 1)
        ).reshape((held.shape[0] * 2,) + block.shape)
        bit //= 2
    return held.reshape((count * block.shape[0],) + block.shape[1:])


def pad_to(values, axis, size):
    room = [(0, 0)] * values.ndim
    room[axis] = (0, size - values.shape[axis])
    return jnp.pad(values, room)


def round_up(size):
    return -(-size // 128) * 128


def body(
    tokens_in,
    cotangent,
    expert_ids,
    prefix_len,
    attn_gain,
    qkv_weight,
    qkv_bias,
    out_weight,
    ffn_gain,
    router_weight,
    expert_gate,
    expert_up,
    expert_down,
    shared_gate,
    shared_up,
    shared_down,
    shared_switch,
):
    n_sh, n_ctx, n_tp = lax.axis_size("shard"), lax.axis_size("ctx"), lax.axis_size("tp")
    my_sh, my_ctx, my_tp = lax.axis_index("shard"), lax.axis_index("ctx"), lax.axis_index("tp")
    micro, _, rows, width = tokens_in.shape
    picks = expert_ids.shape[-1]
    tok = micro * rows
    part = tok // n_tp
    total = n_sh * tok
    length = rows * n_ctx
    depth = qkv_weight.shape[1]
    own = width // (n_sh * n_ctx)
    local_heads, head_dim = qkv_bias.shape[1:]
    group_heads = local_heads // n_ctx
    group = group_heads * head_dim
    experts, _, hidden = expert_gate.shape
    shared_hidden = shared_gate.shape[1]
    score_scale = head_dim ** (-0.5)
    per, cut = (experts // n_sh, 1) if n_sh <= experts else (1, n_sh // experts)
    unit, share = hidden // cut, shared_hidden // n_sh
    unit_pad, share_pad = round_up(unit), round_up(share)
    block = per * unit_pad + share_pad

    inputs = tokens_in.reshape(tok, width)
    upstream = cotangent.reshape(tok, width)
    ids = expert_ids.reshape(tok, picks)

    def mine(values):
        return lax.dynamic_slice_in_dim(values, my_tp * part, part, 0)

    small = jnp.concatenate(
        [
            attn_gain,
            ffn_gain,
            shared_switch,
            router_weight.T.reshape(-1),
            ids.astype(bf16).reshape(-1),
        ]
    )
    small = lax.all_gather(small, "shard", axis=0, tiled=False)
    first_gain = small[:, :depth].reshape(width).astype(f32)
    second_gain = small[:, depth : 2 * depth].reshape(width).astype(f32)
    switch_vec = small[:, 2 * depth : 3 * depth].reshape(width)
    router_full = (
        small[:, 3 * depth : (3 + experts) * depth]
        .reshape(n_sh, experts, depth)
        .transpose(0, 2, 1)
        .reshape(width, experts)
    )
    ids_all = small[:, (3 + experts) * depth :].reshape(total, picks).astype(jnp.int32)

    qkv_local = (
        qkv_weight.reshape(3, depth, n_ctx, group).transpose(1, 2, 0, 3).reshape(depth, -1)
    )
    qkv_full = lax.all_gather(qkv_local, "shard", axis=0, tiled=True)
    bias_row = qkv_bias.reshape(3, n_ctx, group).transpose(1, 0, 2).reshape(1, -1).astype(f32)
    out_full = lax.all_gather(out_weight, "shard", axis=1, tiled=True)

    def spread_in(expert_part, shared_part):
        one = (
            expert_part.reshape(experts, depth, cut, unit)
            .transpose(0, 2, 1, 3)
            .reshape(n_sh, per, depth, unit)
        )
        one = pad_to(one, 3, unit_pad).transpose(0, 2, 1, 3).reshape(n_sh, depth, per * unit_pad)
        two = pad_to(shared_part.reshape(depth, n_sh, share).transpose(1, 0, 2), 2, share_pad)
        return [one, two]

    gate_up = jnp.concatenate(
        spread_in(expert_gate, shared_gate) + spread_in(expert_up, shared_up), axis=2
    )
    gate_up = lax.all_to_all(gate_up, "shard", 0, 0, tiled=True).reshape(width, 2 * block)
    down = jnp.concatenate(
        [
            pad_to(expert_down.reshape(n_sh, per, unit, depth), 2, unit_pad).reshape(
                n_sh, per * unit_pad, depth
            ),
            pad_to(shared_down.reshape(n_sh, share, depth), 1, share_pad),
        ],
        axis=1,
    )
    down = lax.all_to_all(down, "shard", 0, 0, tiled=True).transpose(1, 0, 2).reshape(block, width)
    up_all = lax.all_gather(mine(upstream), ("shard", "tp"), axis=0, tiled=True)

    normed_one = rms_scale(inputs.astype(f32), first_gain).astype(bf16)
    projected = (dot(normed_one, qkv_full) + bias_row).astype(bf16)
    by_heads = lax.all_to_all(
        projected.reshape(tok, n_ctx, 3 * group).transpose(1, 0, 2), "ctx", 0, 0, tiled=True
    )
    by_heads = (
        by_heads.reshape(n_ctx, micro, rows, 3, group_heads, head_dim)
        .transpose(3, 1, 4, 0, 2, 5)
        .reshape(3, micro, group_heads, length, head_dim)
    )
    cosine, sine_table = rope_tables(length, head_dim)
    query_rows = rotate(by_heads[0].astype(f32), cosine, sine_table).astype(bf16)
    key_rows = rotate(by_heads[1].astype(f32), cosine, sine_table).astype(bf16)
    value_rows = by_heads[2]
    places = jnp.arange(length, dtype=jnp.int32)
    allowed = (places[None, :] <= places[:, None])[None] | (
        places[None, None, :] < prefix_len.reshape(micro, 1, 1)
    )
    scores = (
        jnp.einsum("mhqd,mhkd->mhqk", query_rows, key_rows, preferred_element_type=f32)
        * score_scale
    )
    scores = jnp.where(allowed[:, None], scores, -1000000000.0)
    raised = jnp.exp(scores - jnp.max(scores, axis=-1, keepdims=True))
    probs = raised / jnp.sum(raised, axis=-1, keepdims=True)
    probs_low = probs.astype(bf16)
    attended = jnp.einsum(
        "mhqk,mhkd->mhqd", probs_low, value_rows, preferred_element_type=f32
    ).astype(bf16)
    attended = (
        attended.reshape(micro, group_heads, n_ctx, rows, head_dim)
        .transpose(2, 0, 3, 1, 4)
        .reshape(n_ctx, tok, group)
    )
    head_rows = (
        lax.all_to_all(attended, "ctx", 0, 0, tiled=True)
        .transpose(1, 0, 2)
        .reshape(tok, n_ctx * group)
    )
    attn_total = sum_tp(dot(head_rows, out_full).reshape(n_tp, part, width))

    my_inputs = mine(inputs).astype(f32)
    my_up = mine(upstream).astype(f32)
    hidden_res = my_inputs + attn_total
    second_float, second_pull = jax.vjp(rms_scale, hidden_res, second_gain)
    my_normed = second_float.astype(bf16)
    normed_two = lax.all_gather(my_normed, ("shard", "tp"), axis=0, tiled=True)

    routing = jnp.concatenate([router_full, switch_vec[:, None]], axis=1)

    def route(values):
        logits = dot(values, routing)
        return jax.nn.softmax(logits[:, :experts], axis=-1), jax.nn.sigmoid(logits[:, experts])

    probs_all, switch_all = route(normed_two)
    first_expert = my_sh * per // cut
    gates, names = [], []
    for k in range(per):
        named = jnp.any(ids_all == first_expert + k, axis=1)
        chosen = lax.dynamic_index_in_dim(probs_all, first_expert + k, 1, keepdims=False)
        names.append(named)
        gates.append(jnp.where(named, chosen, 0.0))
    gates.append(switch_all)
    column = lax.broadcasted_iota(jnp.int32, (total, block), 1)
    gate_wide = jnp.broadcast_to(gates[-1][:, None], (total, block))
    for k in reversed(range(per)):
        gate_wide = jnp.where(column < (k + 1) * unit_pad, gates[k][:, None], gate_wide)

    pre = dot(normed_two, gate_up)
    pre_gate, pre_up = pre[:, :block], pre[:, block:]
    sigma = jax.nn.sigmoid(pre_gate)
    silu = pre_gate * sigma
    act = silu * pre_up
    act_low = (gate_wide * act).astype(bf16)
    back = dot_cols(up_all, down)
    act_grad = gate_wide * back
    pre_grad = jnp.concatenate(
        [
            (act_grad * pre_up * (sigma + silu * (1.0 - sigma))).astype(bf16),
            (act_grad * silu).astype(bf16),
        ],
        axis=1,
    )
    mixed = dot(act_low, down).astype(bf16)
    product = act * back
    lane = lax.broadcasted_iota(jnp.int32, (1, 128), 1)
    gate_terms = jnp.zeros((total, 128), f32)
    for k in range(per):
        term = jnp.sum(product[:, k * unit_pad : (k + 1) * unit_pad], axis=1)
        term = jnp.where(names[k], term, 0.0)
        gate_terms = gate_terms + jnp.where(lane == first_expert + k, term[:, None], 0.0)
    term = jnp.sum(product[:, per * unit_pad :], axis=1)
    gate_terms = gate_terms + jnp.where(lane == experts, term[:, None], 0.0)
    gate_terms = lax.psum_scatter(
        gate_terms.astype(bf16), ("shard", "tp"), scatter_dimension=0, tiled=True
    ).astype(f32)
    normed_grad = lax.psum_scatter(
        dot_cols(pre_grad, gate_up).astype(bf16),
        ("shard", "tp"),
        scatter_dimension=0,
        tiled=True,
    ).astype(f32)
    ffn_total = lax.psum_scatter(
        mixed, ("shard", "tp"), scatter_dimension=0, tiled=True
    ).astype(f32)
    layer_out = gather_tp((hidden_res + ffn_total).astype(bf16))

    def halves(values):
        split = values.reshape(total, n_sh, n_ctx, own)
        return (
            pick(split, 1 - my_ctx, 2).reshape(total, n_sh * own),
            pick(split, my_ctx, 2).reshape(total, n_sh * own),
        )

    up_other, up_mine = halves(up_all)
    two_other, two_mine = halves(normed_two)
    down_other = swap(dot_rows(act_low, up_other).astype(bf16), "ctx", 1)
    gate_up_other = swap(dot_rows(two_other, pre_grad).astype(bf16), "ctx", 1)
    down_grad = (dot_rows(act_low, up_mine) + down_other.astype(f32)).astype(bf16)
    gate_up_grad = (dot_rows(two_mine, pre_grad) + gate_up_other.astype(f32)).astype(bf16)
    down_grad = lax.all_to_all(
        down_grad.reshape(block, n_sh, own).transpose(1, 0, 2), "shard", 0, 0, tiled=True
    ).astype(f32)
    gate_up_grad = lax.all_to_all(
        gate_up_grad.reshape(n_sh, own, 2 * block), "shard", 0, 0, tiled=True
    ).astype(f32)

    def spread_out(grads):
        one = grads[:, :, : per * unit_pad].reshape(n_sh, own, per, unit_pad)[..., :unit]
        one = (
            one.transpose(0, 2, 1, 3)
            .reshape(experts, cut, own, unit)
            .transpose(0, 2, 1, 3)
            .reshape(experts, own, hidden)
        )
        two = grads[:, :, per * unit_pad : per * unit_pad + share]
        return one, two.transpose(1, 0, 2).reshape(own, shared_hidden)

    expert_gate_grad, shared_gate_grad = spread_out(gate_up_grad[:, :, :block])
    expert_up_grad, shared_up_grad = spread_out(gate_up_grad[:, :, block:])
    expert_down_grad = (
        down_grad[:, : per * unit_pad]
        .reshape(n_sh, per, unit_pad, own)[:, :, :unit]
        .reshape(experts, hidden, own)
    )
    shared_down_grad = down_grad[:, per * unit_pad :][:, :share].reshape(shared_hidden, own)

    my_probs, my_switch = route(my_normed)
    prob_grads = gate_terms[:, :experts]
    logit_grads = my_probs * (
        prob_grads - jnp.sum(my_probs * prob_grads, axis=-1, keepdims=True)
    )
    switch_pre_grad = gate_terms[:, experts] * my_switch * (1.0 - my_switch)
    route_grads = jnp.concatenate([logit_grads, switch_pre_grad[:, None]], axis=1)
    normed_float = my_normed.astype(f32)
    routing_grad = lax.dot_general(
        route_grads, normed_float, (((0,), (0,)), ((), ())), precision=highest
    )
    normed_grad = normed_grad + lax.dot_general(
        route_grads, routing.astype(f32), (((1,), (1,)), ((), ())), precision=highest
    )
    hidden_norm_grad, ffn_gain_grad = second_pull(normed_grad)
    hidden_grad = my_up + hidden_norm_grad
    early = lax.psum(
        jnp.concatenate([routing_grad, ffn_gain_grad[None]], axis=0), ("shard", "ctx", "tp")
    )

    branch_low = gather_tp(hidden_grad.astype(bf16))
    out_weight_grad = dot_rows(head_rows, branch_low).astype(bf16)
    out_weight_grad = lax.psum_scatter(out_weight_grad, "shard", scatter_dimension=1, tiled=True)
    out_weight_grad = lax.psum_scatter(
        out_weight_grad, "ctx", scatter_dimension=1, tiled=True
    ).astype(f32)
    head_grad = dot_cols(branch_low, out_full).astype(bf16)
    head_grad = lax.all_to_all(
        head_grad.reshape(tok, n_ctx, group).transpose(1, 0, 2), "ctx", 0, 0, tiled=True
    )
    head_grad = (
        head_grad.reshape(n_ctx, micro, rows, group_heads, head_dim)
        .transpose(1, 3, 0, 2, 4)
        .reshape(micro, group_heads, length, head_dim)
    )
    prob_grad = jnp.einsum("mhqd,mhkd->mhqk", head_grad, value_rows, preferred_element_type=f32)
    value_grad = jnp.einsum("mhqk,mhqd->mhkd", probs_low, head_grad, preferred_element_type=f32)
    score_low = (
        probs * (prob_grad - jnp.sum(probs * prob_grad, axis=-1, keepdims=True))
    ).astype(bf16)
    query_grad = (
        jnp.einsum("mhqk,mhkd->mhqd", score_low, key_rows, preferred_element_type=f32)
        * score_scale
    )
    key_grad = (
        jnp.einsum("mhqk,mhqd->mhkd", score_low, query_rows, preferred_element_type=f32)
        * score_scale
    )
    stacked = jnp.stack(
        [
            rotate(query_grad, cosine, -sine_table),
            rotate(key_grad, cosine, -sine_table),
            value_grad,
        ]
    ).astype(bf16)
    stacked = (
        stacked.reshape(3, micro, group_heads, n_ctx, rows, head_dim)
        .transpose(3, 1, 4, 0, 2, 5)
        .reshape(n_ctx, tok, 3 * group)
    )
    proj_grad = (
        lax.all_to_all(stacked, "ctx", 0, 0, tiled=True)
        .transpose(1, 0, 2)
        .reshape(tok, n_ctx * 3 * group)
    )
    qkv_grad = dot_rows(normed_one, proj_grad).astype(bf16)
    qkv_grad = lax.psum_scatter(qkv_grad, "shard", scatter_dimension=0, tiled=True)
    qkv_grad = lax.psum_scatter(qkv_grad, "ctx", scatter_dimension=0, tiled=True).astype(f32)
    qkv_grad = (
        qkv_grad.reshape(own, n_ctx, 3, group).transpose(2, 0, 1, 3).reshape(3, own, n_ctx * group)
    )
    bias_grad = jnp.sum(proj_grad.astype(f32), axis=0)
    normed_one_grad = sum_tp(dot_cols(proj_grad, qkv_full).reshape(n_tp, part, width))
    _, first_pull = jax.vjp(rms_scale, my_inputs, first_gain)
    input_norm_grad, attn_gain_grad = first_pull(normed_one_grad)
    tokens_grad = gather_tp((hidden_grad + input_norm_grad).astype(bf16)).astype(f32)

    bias_spread = jnp.where(
        jnp.arange(n_tp)[:, None] == my_tp, bias_grad[None], 0.0
    ).reshape(-1)
    late = lax.psum(jnp.concatenate([attn_gain_grad, bias_spread]), ("shard", "ctx", "tp"))
    late_bias = lax.dynamic_slice_in_dim(late[width:], my_tp * bias_grad.size, bias_grad.size)
    late_bias = (
        late_bias.reshape(n_ctx, 3, group_heads, head_dim)
        .transpose(1, 0, 2, 3)
        .reshape(3, local_heads, head_dim)
    )
    place = my_sh * n_ctx + my_ctx
    early = lax.dynamic_slice_in_dim(early, place * own, own, 1)
    bias_own = head_dim // (n_sh * n_ctx)
    shape = (micro, 1, rows, width)
    return (
        layer_out.reshape(shape),
        tokens_grad.reshape(shape),
        lax.dynamic_slice_in_dim(late[:width], place * own, own),
        qkv_grad,
        lax.dynamic_slice_in_dim(late_bias, place * bias_own, bias_own, 2),
        out_weight_grad,
        early[experts + 1],
        early[:experts].T,
        expert_gate_grad,
        expert_up_grad,
        expert_down_grad,
        shared_gate_grad,
        shared_up_grad,
        shared_down_grad,
        early[experts],
    )


def solution(mesh):
    in_specs = (
        P(None, "shard", "ctx", None),
        P(None, "shard", "ctx", None),
        P(None, "shard", "ctx", None),
        P(None, "shard"),
        P("shard"),
        P(None, "shard", "tp"),
        P(None, "tp", None),
        P("tp", "shard"),
        P("shard"),
        P("shard", None),
        P(None, "shard", "tp"),
        P(None, "shard", "tp"),
        P(None, "tp", "shard"),
        P("shard", "tp"),
        P("shard", "tp"),
        P("tp", "shard"),
        P("shard"),
    )
    out_specs = (
        P(None, "shard", "ctx", None),
        P(None, "shard", "ctx", None),
        P(("shard", "ctx")),
        P(None, ("shard", "ctx"), "tp"),
        P(None, "tp", ("shard", "ctx")),
        P("tp", ("shard", "ctx")),
        P(("shard", "ctx")),
        P(("shard", "ctx"), None),
        P(None, ("shard", "ctx"), "tp"),
        P(None, ("shard", "ctx"), "tp"),
        P(None, "tp", ("shard", "ctx")),
        P(("shard", "ctx"), "tp"),
        P(("shard", "ctx"), "tp"),
        P("tp", ("shard", "ctx")),
        P(("shard", "ctx")),
    )
    return jax.shard_map(body, mesh=mesh, in_specs=in_specs, out_specs=out_specs, check_vma=False)
```

time: 5740 us -> 1350 us (0.24)
  waiting for transfers between devices: 5060 us -> 750 us
  local copies, waits for them, and re-layouts: 124 us -> 266 us
  matrix products: 297 us -> 160 us
  other arithmetic: 110 us -> 44.9 us
    reduce_scatter x18 -> x6, waiting for transfers between devices: 4360 us -> 206 us  [the longest x1 73.5 us: body(): lax.psum_scatter(dot_cols(pre_grad, gate_up).astype(bf16), ('shard', 'tp'...]
    all_gather x8 -> x4, waiting for transfers between devices: 543 us -> 59.3 us  [the longest x1 59.3 us: body(): qkv_full = lax.all_gather(qkv_local, 'shard', axis=0, tiled=True)]
    ppermute x0 -> x12, waiting for transfers between devices: none -> 274 us  [swap(): return lax.ppermute(values, axis, [(i, i ^ bit) for i in range(count)])]
    dot_general x70 -> x23, matrix products: 297 us -> 156 us  [the longest x6 53.6 us: dot_rows(): lax.dot_general(left, right, (((0,), (0,)), ((), ())), preferred_element_...]
    all_to_all x8, waiting for transfers between devices: 56.1 us -> 189 us  [the longest x1 82.2 us: body(): lax.all_to_all(gate_up, 'shard', 0, 0, tiled=True).reshape(width, 2 * block)]
    psum x3 -> x1, waiting for transfers between devices: 96.9 us -> 0.01 us  [body(): lax.psum(jnp.concatenate([routing_grad, ffn_gain_grad[None]], axis=0), ('...]
    unnamed x407 -> x154, local copies, waits for them, and re-layouts: 31.2 us -> 94.3 us
  transfers between devices with their start and end apart: 39 -> 32, of which waited for: 34 -> 17; matrix products, arithmetic and copies ran while one was open for 5% -> 31% of each run, Pallas kernels for 0% -> 0%
where the time goes in v1:
time: 1350 us; the launch traced here: 1340 us
  waiting for transfers between devices  750 us (56%)
  local copies, waits for them, and re-layouts  266 us (20%)
  matrix products  160 us (12%)
  blocking collectives  57.7 us (4%)
  other arithmetic  44.9 us (3%)
  starting transfers between devices  43.7 us (3%)
  between operations  16.1 us (1%)
    ppermute x12, waiting for transfers between devices, swap(): return lax.ppermute(values, axis, [(i, i ^ bit) for i in range(count)])  274 us
    unnamed x154, local copies, waits for them, and re-layouts  94.3 us
    all_to_all x1, waiting for transfers between devices, body(): lax.all_to_all(gate_up, 'shard', 0, 0, tiled=True).reshape(width, 2 * block)  82.2 us
    reduce_scatter x1, waiting for transfers between devices, body(): lax.psum_scatter(dot_cols(pre_grad, gate_up).astype(bf16), ('shard', 'tp'...  73.5 us
    reduce_scatter x1, waiting for transfers between devices, body(): lax.psum_scatter(mixed, ('shard', 'tp'), scatter_dimension=0, tiled=True)  73.3 us
    reduce_scatter x1, waiting for transfers between devices, body(): lax.psum_scatter(qkv_grad, 'shard', scatter_dimension=0, tiled=True)  59.6 us
    all_gather x1, waiting for transfers between devices, body(): qkv_full = lax.all_gather(qkv_local, 'shard', axis=0, tiled=True)  59.3 us
    dot_general x6, matrix products, dot_rows(): lax.dot_general(left, right, (((0,), (0,)), ((), ())), preferred_element_...  53.6 us
  transfers between devices with their start and end apart: 32, of which 17 were waited for; matrix products, arithmetic and copies ran while one was open for 31% of the time, Pallas kernels for 0%

profile of v1, /device:TPU:0, one launch (start us, length us, event | category | flops | bytes accessed | tf_op | source)
XLA Modules:
  0.0 1338.1 jit_solution(14997470237720870086)
XLA Ops:
  24.5 59.3 %all-gather.6.cloned.1.call-done = bf16[2048,1536]{1,0:T(8,128)(2,1)} async-done(((bf16[512,1536]{1,0:T(8,128)(2,1)}), bf16[2048,1536]{1,0:T(8,128)(2,1)}) %all-gather.6.cloned.1.call-update) | async-done | bytes 6291472 | tf_op jit(solution)/shard_map/all_gather | solution.py:169
  95.1 27.7 %all-to-all-done = bf16[2,384,768]{2,1,0:T(8,128)(2,1)S(1)} async-done(((bf16[2,384,768]{2,1,0:T(8,128)(2,1)}), bf16[2,384,768]{2,1,0:T(8,128)(2,1)S(1)}, u32[]{:S(2)}, u32[]{:S(2)}) %all-to-all-start) | async-done | bytes 1179680 | tf_op jit(solution)/shard_map/all_to_all | solution.py:201
  268.9 82.2 %all-to-all-done.2 = bf16[4,512,2304]{2,1,0:T(8,128)(2,1)} async-done(((bf16[4,512,2304]{2,1,0:T(8,128)(2,1)}), bf16[4,512,2304]{2,1,0:T(8,128)(2,1)}, u32[]{:S(2)}, u32[]{:S(2)}) %all-to-all-start.2) | async-done | bytes 9437216 | tf_op jit(solution)/shard_map/all_to_all | solution.py:186
  356.4 21.2 %fusion.76 = f32[1536,2304]{1,0:T(8,128)} fusion(bf16[1536,2048]{1,0:T(8,128)(2,1)} %all-gather.10.cloned.1.call-done, bf16[2048,2304]{1,0:T(8,128)(2,1)} %bitcast.32), kind=kOutput, calls=%fused_computation.212 | convolution fusion | flops 14495514624 | bytes 29884416 | tf_op jit(solution)/shard_map/dot_general | solution.py:40
  377.6 31.4 %all-to-all-done.3 = bf16[4,1152,512]{1,2,0:T(8,128)(2,1)} async-done(((bf16[4,1152,512]{1,2,0:T(8,128)(2,1)}), bf16[4,1152,512]{1,2,0:T(8,128)(2,1)}, u32[]{:S(2)}, u32[]{:S(2)}) %all-to-all-start.3) | async-done | bytes 4718624 | tf_op jit(solution)/shard_map/all_to_all | solution.py:196
  409.0 20.0 %multiply_convert_fusion.1 = (bf16[1536,1152]{1,0:T(8,128)(2,1)}, bf16[1536,1152]{1,0:T(8,128)(2,1)}, f32[1536,1152]{1,0:T(8,128)S(1)}, bf16[1536,1152]{1,0:T(8,128)(2,1)}) fusion(f32[1536,2304]{1,0:T(8,128)} %fusion.76, f32[1536]{0:T(1024)S(1)} %get-tuple-element.119, f32[1536]{0:T(1024)S(1)} %get-tuple-element.68, f32[1536]{0:T(1024)S(1)} %get-tuple-element.67, ...), kind=kOutput, calls=%fused_computation.18 | convolution fusion | flops 7281377280 | bytes 42881280 | tf_op jit(solution)/shard_map/dot_general | solution.py:48
  431.1 21.0 %convolution_convert_fusion.1 = bf16[1536,2048]{1,0:T(8,128)(2,1)} fusion(bf16[2048,2304]{1,0:T(8,128)(2,1)} %bitcast.32, bf16[1536,1152]{1,0:T(8,128)(2,1)} %get-tuple-element.74, bf16[1536,1152]{1,0:T(8,128)(2,1)} %get-tuple-element.73), kind=kOutput, calls=%fused_computation.14 | convolution fusion | flops 14512816128 | bytes 22806528 | tf_op jit(solution)/shard_map/dot_general | solution.py:48
  452.2 13.1 convolution_convert_fusion.2
  466.5 19.9 %reduce-scatter.22.cloned.1.call-done = bf16[96,128]{1,0:T(8,128)(2,1)} async-done(((bf16[1536,128]{1,0:T(8,128)(2,1)}), bf16[96,128]{1,0:T(8,128)(2,1)}) %reduce-scatter.22.cloned.1.call-update) | async-done | bytes 24592
  487.4 73.5 %reduce-scatter.12.cloned.1.call-done = bf16[96,2048]{1,0:T(8,128)(2,1)} async-done(((bf16[1536,2048]{1,0:T(8,128)(2,1)}), bf16[96,2048]{1,0:T(8,128)(2,1)}) %reduce-scatter.12.cloned.1.call-update) | async-done | bytes 393232 | tf_op jit(solution)/shard_map/reduce_scatter | solution.py:295
  563.2 73.3 %reduce-scatter.10.cloned.1.call-done = bf16[96,2048]{1,0:T(8,128)(2,1)} async-done(((bf16[1536,2048]{1,0:T(8,128)(2,1)}), bf16[96,2048]{1,0:T(8,128)(2,1)}) %reduce-scatter.10.cloned.1.call-update) | async-done | bytes 393232 | tf_op jit(solution)/shard_map/reduce_scatter | solution.py:301
  703.9 15.8 %constant_dynamic-slice_fusion.3 = (bf16[1536,4,1,256]{3,2,1,0:T(2,128)(2,1)}, bf16[1536,4,1,256]{3,2,1,0:T(2,128)(2,1)}) fusion(bf16[1536,4,2,256]{3,2,1,0:T(2,128)(2,1)} %reshape.749, s32[]{:T(128)S(6)} %select_n.281, s32[]{:T(128)S(6)} %select_n.282), kind=kLoop, calls=%fused_computation.165 | loop fusion | bytes 12582920 | tf_op jit(solution)/shard_map/jit(dynamic_index_in_dim)/dynamic_slice | solution.py:57
  719.7 15.2 %copy.232 = bf16[1536,4,1,256]{0,3,1,2:T(8,128)(2,1)} copy(bf16[1536,4,1,256]{3,2,1,0:T(2,128)(2,1)} %get-tuple-element.80) | data formatting | bytes 6291456
  744.2 12.8 convolution_convert_fusion.3
  759.9 14.3 %constant_dynamic-slice_fusion = (bf16[1536,4,1,256]{3,2,1,0:T(2,128)(2,1)}, bf16[1536,4,1,256]{3,2,1,0:T(2,128)(2,1)}) fusion(bf16[1536,4,2,256]{3,2,1,0:T(2,128)(2,1)S(1)} %bitcast.227, s32[]{:T(128)S(6)} %select_n.282, s32[]{:T(128)S(6)} %select_n.281), kind=kLoop, calls=%fused_computation.162 | loop fusion | bytes 12582920 | tf_op jit(solution)/shard_map/jit(dynamic_index_in_dim)/dynamic_slice | solution.py:57
  774.2 15.2 %copy.234 = bf16[1536,4,1,256]{0,3,1,2:T(8,128)(2,1)} copy(bf16[1536,4,1,256]{3,2,1,0:T(2,128)(2,1)} %get-tuple-element.77) | data formatting | bytes 6291456
  798.0 15.3 %copy.233 = bf16[1536,4,1,256]{0,3,1,2:T(8,128)(2,1)} copy(bf16[1536,4,1,256]{3,2,1,0:T(2,128)(2,1)} %get-tuple-element.78) | data formatting | bytes 6291456
  813.3 15.2 %copy.231 = bf16[1536,4,1,256]{0,3,1,2:T(8,128)(2,1)} copy(bf16[1536,4,1,256]{3,2,1,0:T(2,128)(2,1)} %get-tuple-element.79) | data formatting | bytes 6291456
  828.4 235.8 %collective-permute-done.11 = bf16[1152,1024]{0,1:T(8,128)(2,1)S(1)} collective-permute-done((bf16[1152,1024]{0,1:T(8,128)(2,1)}, bf16[1152,1024]{0,1:T(8,128)(2,1)S(1)}, u32[]{:S(2)}, u32[]{:S(2)}) %collective-permute-start.11) | collective-permute-done | bytes 2359328 | tf_op jit(solution)/shard_map/ppermute | solution.py:53
  1076.7 13.3 add_convert_fusion
  1132.3 29.6 %all-to-all-done.6 = bf16[4,256,2304]{1,2,0:T(8,128)(2,1)} async-done(((bf16[4,256,2304]{1,2,0:T(8,128)(2,1)}), bf16[4,256,2304]{1,2,0:T(8,128)(2,1)}, u32[]{:S(2)}, u32[]{:S(2)}) %all-to-all-start.6) | async-done | bytes 4718624 | tf_op jit(solution)/shard_map/all_to_all | solution.py:322
  1187.8 59.6 %reduce-scatter.14.cloned.1.call-done = bf16[512,1536]{1,0:T(8,128)(2,1)} async-done(((bf16[2048,1536]{1,0:T(8,128)(2,1)}), bf16[512,1536]{1,0:T(8,128)(2,1)}) %reduce-scatter.14.cloned.1.call-update) | async-done | bytes 1572880 | tf_op jit(solution)/shard_map/reduce_scatter | solution.py:412
  1257.5 14.1 %collective-permute-done.8 = bf16[1,96,2048]{2,1,0:T(8,128)(2,1)S(1)} collective-permute-done((bf16[1,96,2048]{2,1,0:T(8,128)(2,1)}, bf16[1,96,2048]{2,1,0:T(8,128)(2,1)S(1)}, u32[]{:S(2)}, u32[]{:S(2)}) %collective-permute-start.8) | collective-permute-done | bytes 393248 | tf_op jit(solution)/shard_map/ppermute | solution.py:53
  1273.1 48.0 %psum.14 = f32[8192]{0:T(1024)S(1)} all-reduce(f32[8192]{0:T(1024)S(1)} %pad_maximum_fusion.15), channel_id=1, replica_groups=mesh['shard'=4,'ctx'=2,'tp'=4] {'shard','ctx','tp'}, use_global_device_ids=true, to_apply=%region_23.24 | all-reduce | flops 8192 | bytes 65536 | tf_op jit(solution)/shard_map/psum | solution.py:426
  (376 shorter events, 375.3 us)
Async XLA Ops:
  7.2 76.6 %all-gather.6.cloned.1.call-start = ((), (), s32[]{:S(2)}) async-start(), calls=%async_computation.15 | async-start | bytes 7864320 | tf_op jit(solution)/shard_map/all_gather | solution.py:169
  10.8 138.2 %all-gather.8.cloned.1.call-start = ((), (), s32[]{:S(2)}) async-start(), calls=%async_computation.16 | async-start | bytes 2621440 | tf_op jit(solution)/shard_map/all_gather | solution.py:171
  90.4 32.4 %all-to-all-start = ((bf16[2,384,768]{2,1,0:T(8,128)(2,1)}), bf16[2,384,768]{2,1,0:T(8,128)(2,1)S(1)}, u32[]{:S(2)}, u32[]{:S(2)}) async-start(bf16[2,384,768]{2,1,0:T(8,128)(2,1)} %bitcast.246), calls=%async_computation | async-start | bytes 2359296 | tf_op jit(solution)/shard_map/all_to_all | solution.py:201
  137.4 126.9 %all-gather.10.cloned.1.call-start = ((), (), s32[]{:S(2)}) async-start(), calls=%async_computation.17 | async-start | bytes 6684672 | tf_op jit(solution)/shard_map/all_gather | solution.py:245
  172.7 236.3 %all-gather.12.cloned.1.call-start = ((), (), s32[]{:S(2)}) async-start(), calls=%async_computation.19 | async-start | bytes 6684672 | tf_op jit(solution)/shard_map/all_gather | solution.py:197
  235.6 115.5 %all-to-all-start.2 = ((bf16[4,512,2304]{2,1,0:T(8,128)(2,1)}), bf16[4,512,2304]{2,1,0:T(8,128)(2,1)}, u32[]{:S(2)}, u32[]{:S(2)}) async-start(bf16[4,512,2304]{2,1,0:T(8,128)(2,1)} %fusion.6), calls=%async_computation.2 | async-start | bytes 18874368 | tf_op jit(solution)/shard_map/all_to_all | solution.py:186
  351.1 57.9 %all-to-all-start.3 = ((bf16[4,1152,512]{1,2,0:T(8,128)(2,1)}), bf16[4,1152,512]{1,2,0:T(8,128)(2,1)}, u32[]{:S(2)}, u32[]{:S(2)}) async-start(bf16[4,1152,512]{1,2,0:T(8,128)(2,1)} %fusion.11), calls=%async_computation.3 | async-start | bytes 9437184 | tf_op jit(solution)/shard_map/all_to_all | solution.py:196
  356.0 130.4 %reduce-scatter.22.cloned.1.call-start = ((), (), s32[]{:S(2)}) async-start(), calls=%async_computation.26 | async-start | bytes 417792
  430.9 130.1 %reduce-scatter.12.cloned.1.call-start = ((), (), s32[]{:S(2)}) async-start(), calls=%async_computation.20 | async-start | bytes 6684672 | tf_op jit(solution)/shard_map/reduce_scatter | solution.py:295
  452.2 184.4 %reduce-scatter.10.cloned.1.call-start = ((), (), s32[]{:S(2)}) async-start(), calls=%async_computation.18 | async-start | bytes 6684672 | tf_op jit(solution)/shard_map/reduce_scatter | solution.py:301
  655.2 32.5 %all-to-all-start.4 = ((bf16[2,384,256]{2,1,0:T(8,128)(2,1)}), bf16[2,384,256]{2,1,0:T(8,128)(2,1)}, u32[]{:S(2)}, u32[]{:S(2)}) async-start(bf16[2,384,256]{2,1,0:T(8,128)(2,1)} %bitcast.222), calls=%async_computation.6 | async-start | bytes 786432 | tf_op jit(solution)/shard_map/all_to_all | solution.py:373
  659.4 507.7 %reduce-scatter.18.cloned.1.call-start = ((), (), s32[]{:S(2)}) async-start(), calls=%async_computation.23 | async-start | bytes 2621440 | tf_op jit(solution)/shard_map/reduce_scatter | solution.py:368
  699.7 36.4 %all-to-all-start.5 = ((bf16[2,384,768]{2,1,0:T(8,128)(2,1)}), bf16[2,384,768]{2,1,0:T(8,128)(2,1)S(1)}, u32[]{:S(2)}, u32[]{:S(2)}) async-start(bf16[2,384,768]{2,1,0:T(8,128)(2,1)} %reshape.740), calls=%async_computation.7 | async-start | bytes 2359296 | tf_op jit(solution)/shard_map/all_to_all | solution.py:407
  703.9 476.2 %all-reduce.8.cloned.1.call-start = ((), (), s32[]{:S(2)}) async-start(), calls=%async_computation.25 | async-start | bytes 262144 | tf_op jit(solution)/shard_map/psum | solution.py:362
  735.8 511.6 %reduce-scatter.14.cloned.1.call-start = ((), (), s32[]{:S(2)}) async-start(), calls=%async_computation.21 | async-start | bytes 7864320 | tf_op jit(solution)/shard_map/reduce_scatter | solution.py:412
  756.9 319.8 %collective-permute-start.10 = (bf16[1024,2304]{1,0:T(8,128)(2,1)}, bf16[1024,2304]{1,0:T(8,128)(2,1)}, u32[]{:S(2)}, u32[]{:S(2)}) collective-permute-start(bf16[1024,2304]{1,0:T(8,128)(2,1)} %convolution_convert_fusion.3), channel_id=1, source_target_pairs={{0,4},{4,0},{1,5},{5,1},{2,6},{6,2},{3,7},{7,3},{8,12},{12,8},{9,1... | collective-permute-start | bytes 14155784 | tf_op jit(solution)/shard_map/ppermute | solution.py:53
  797.9 266.3 %collective-permute-start.11 = (bf16[1152,1024]{0,1:T(8,128)(2,1)}, bf16[1152,1024]{0,1:T(8,128)(2,1)S(1)}, u32[]{:S(2)}, u32[]{:S(2)}) collective-permute-start(bf16[1152,1024]{0,1:T(8,128)(2,1)} %convolution_convert_fusion.4), channel_id=1, source_target_pairs={{0,4},{4,0},{1,5},{5,1},{2,6},{6,2},{3,7},{7,3},{8,12},{12,8},{9,1... | collective-permute-start | bytes 7077896 | tf_op jit(solution)/shard_map/ppermute | solution.py:53
  1104.3 57.6 %all-to-all-start.6 = ((bf16[4,256,2304]{1,2,0:T(8,128)(2,1)}), bf16[4,256,2304]{1,2,0:T(8,128)(2,1)}, u32[]{:S(2)}, u32[]{:S(2)}) async-start(bf16[4,256,2304]{1,2,0:T(8,128)(2,1)} %copy.205), calls=%async_computation.12 | async-start | bytes 9437184 | tf_op jit(solution)/shard_map/all_to_all | solution.py:322
  1109.3 216.6 %reduce-scatter.20.cloned.1.call-start = ((), (), s32[]{:S(2)}) async-start(), calls=%async_computation.24 | async-start | bytes 786432 | tf_op jit(solution)/shard_map/reduce_scatter | solution.py:369
  1132.2 50.6 %collective-permute-start.6 = (bf16[2,96,2048]{2,1,0:T(8,128)(2,1)S(1)}, bf16[2,96,2048]{2,1,0:T(8,128)(2,1)}, u32[]{:S(2)}, u32[]{:S(2)}) collective-permute-start(bf16[2,96,2048]{2,1,0:T(8,128)(2,1)S(1)} %fusion.35), channel_id=1, source_target_pairs={{0,1},{1,0},{2,3},{3,2},{4,5},{5,4},{6,7},{7,6},{8,9},{9,8},{10,11... | collective-permute-start | bytes 2359304 | tf_op jit(solution)/shard_map/ppermute | solution.py:53
  1167.0 160.7 %reduce-scatter.16.cloned.1.call-start = ((), (), s32[]{:S(2)}) async-start(), calls=%async_computation.22 | async-start | bytes 2359296 | tf_op jit(solution)/shard_map/reduce_scatter | solution.py:413
  1179.2 68.2 %collective-permute-start.2 = (bf16[1,96,2048]{2,1,0:T(8,128)(2,1)}, bf16[1,96,2048]{2,1,0:T(8,128)(2,1)}, u32[]{:S(2)}, u32[]{:S(2)}) collective-permute-start(bf16[1,96,2048]{2,1,0:T(8,128)(2,1)} %get-tuple-element.99), channel_id=1, source_target_pairs={{0,2},{1,3},{2,0},{3,1},{4,6},{5,7},{6,4},{7,5},{8,10},{9,11},{10,... | collective-permute-start | bytes 1179656 | tf_op jit(solution)/shard_map/ppermute | solution.py:53
  1187.3 63.4 %collective-permute-start.7 = (bf16[1,96,2048]{2,1,0:T(8,128)(2,1)}, bf16[1,96,2048]{2,1,0:T(8,128)(2,1)}, u32[]{:S(2)}, u32[]{:S(2)}) collective-permute-start(bf16[1,96,2048]{2,1,0:T(8,128)(2,1)} %dynamic-slice_convert_fusion.1), channel_id=1, source_target_pairs={{0,2},{1,3},{2,0},{3,1},{4,6},{5,7},{6,4},{7,5},{8,10},{9,11},{10,... | collective-permute-start | bytes 1179656 | tf_op jit(solution)/shard_map/ppermute | solution.py:53
  1272.9 50.9 %collective-permute-start.9 = (bf16[2,96,2048]{2,1,0:T(8,128)(2,1)S(1)}, bf16[2,96,2048]{2,1,0:T(8,128)(2,1)S(1)}, u32[]{:S(2)}, u32[]{:S(2)}) collective-permute-start(bf16[2,96,2048]{2,1,0:T(8,128)(2,1)S(1)} %maximum_select_fusion.7), channel_id=1, source_target_pairs={{0,1},{1,0},{2,3},{3,2},{4,5},{5,4},{6,7},{7,6},{8,9},{9,8},{10,11... | collective-permute-start | bytes 2359304 | tf_op jit(solution)/shard_map/ppermute | solution.py:53
  (74 other events, 1168.9 us)
Sparse Core Ops, SparseCore 0:
  10.9 72.8 all-gather.5
  85.6 35.1 all-gather.7
  172.8 37.0 all-gather.9
  211.9 45.2 all-gather.11
  431.0 55.4 reduce-scatter.21
  488.7 72.1 reduce-scatter.11
  563.3 73.2 reduce-scatter.9
  664.0 35.8 reduce-scatter.17
  736.0 433.1 all-reduce.7
  1172.0 75.4 reduce-scatter.13
  1249.7 20.1 reduce-scatter.19
  1272.1 44.9 reduce-scatter.15

commit v2 on v1

v2 whole, which is shorter than its diff:
```python
import functools

import jax
import jax.numpy as jnp
import numpy as np
from jax import lax
from jax.experimental import pallas as pl
from jax.experimental.pallas import tpu as pltpu
from jax.sharding import PartitionSpec as P

epsilon = 1e-06
rope_base = 1000000.0
highest = lax.Precision.HIGHEST
f32 = jnp.float32
bf16 = jnp.bfloat16


def rms_scale(values, gain_vec):
    factor = lax.rsqrt(jnp.mean(values * values, axis=-1, keepdims=True) + epsilon)
    return values * factor * gain_vec


def rope_tables(length, head_dim):
    half_dim = head_dim // 2
    frequency = rope_base ** (-(np.arange(half_dim) * 2.0) / head_dim)
    places = np.arange(length)[:, None] * frequency[None, :]
    return jnp.asarray(np.cos(places), f32), jnp.asarray(np.sin(places), f32)


def rotate(values, cosine, sine_table):
    half_dim = values.shape[-1] // 2
    first_half = values[..., :half_dim]
    second_half = values[..., half_dim:]
    return jnp.concatenate(
        [
            first_half * cosine - second_half * sine_table,
            second_half * cosine + first_half * sine_table,
        ],
        axis=-1,
    )


def dot(left, right):
    return jnp.dot(left, right, preferred_element_type=f32)


def dot_rows(left, right):
    return lax.dot_general(left, right, (((0,), (0,)), ((), ())), preferred_element_type=f32)


def dot_cols(left, right):
    return lax.dot_general(left, right, (((1,), (1,)), ((), ())), preferred_element_type=f32)


def swap(values, axis, bit):
    count = lax.axis_size(axis)
    return lax.ppermute(values, axis, [(i, i ^ bit) for i in range(count)])


def pick(values, place, axis):
    return lax.dynamic_index_in_dim(values, place, axis, keepdims=False)


def sum_tp(terms):
    count = lax.axis_size("tp")
    place = lax.axis_index("tp")
    bit = 1
    while bit < count:
        pairs = terms.reshape((terms.shape[0] // 2, 2) + terms.shape[1:])
        low = (place // bit) % 2
        sent = pick(pairs, 1 - low, 1).astype(bf16)
        terms = pick(pairs, low, 1).astype(f32) + swap(sent, "tp", bit).astype(f32)
        bit *= 2
    return terms[0]


def gather_tp(block):
    count = lax.axis_size("tp")
    place = lax.axis_index("tp")
    held = block[None]
    bit = count // 2
    while bit >= 1:
        other = swap(held, "tp", bit)
        high = (place // bit) % 2
        held = jnp.where(
            high == 0, jnp.stack([held, other], 1), jnp.stack([other, held], 1)
        ).reshape((held.shape[0] * 2,) + block.shape)
        bit //= 2
    return held.reshape((count * block.shape[0],) + block.shape[1:])


def round_up(size):
    return -(-size // 128) * 128


def pad_to(values, axis, size):
    room = [(0, 0)] * values.ndim
    room[axis] = (0, size - values.shape[axis])
    return jnp.pad(values, room)


def tie(values, *after):
    return lax.optimization_barrier((values,) + after)[0]


def core_groups():
    n_sh, half = lax.axis_size("shard"), lax.axis_size("tp") // 2
    return [
        [s * 2 * half + z * 2 + core for s in range(n_sh) for z in range(half)]
        for core in range(2)
    ]


def exchange(values):
    return lax.all_to_all(
        values, ("shard", "tp"), 0, 0, tiled=True, axis_index_groups=core_groups()
    )


def gather_core(block):
    peers = lax.axis_size("shard") * lax.axis_size("tp") // 2
    return exchange(jnp.broadcast_to(block[None], (peers,) + block.shape))


def both_cores(own):
    return jnp.concatenate([own, swap(own, "tp", 1)]).reshape(-1, own.shape[-1])


def sum_core(other, make_own):
    arrived = swap(other, "tp", 1)
    return (make_own().astype(f32) + arrived.astype(f32)).astype(bf16)


def sum_shard_z(own):
    half = lax.axis_size("tp") // 2
    z = lax.axis_index("tp") // 2
    own = lax.all_to_all(own, "shard", 0, 0, tiled=True)
    own = jnp.sum(own.reshape((-1, half) + own.shape[1:]).astype(f32), axis=0)
    return pick(own, z, 0) + swap(pick(own, 1 - z, 0).astype(bf16), "tp", 2).astype(f32)


def sum_rows_small(terms):
    n_sh, half = lax.axis_size("shard"), lax.axis_size("tp") // 2
    terms = terms[0] + swap(terms[1], "tp", 1)
    terms = terms.reshape((n_sh, half) + terms.shape[1:]).swapaxes(0, 1)
    for axis, place, scale in (
        ("tp", lax.axis_index("tp") // 2, 2),
        ("shard", lax.axis_index("shard"), 1),
    ):
        bit = 1
        while terms.shape[0] > 1:
            pairs = terms.reshape((terms.shape[0] // 2, 2) + terms.shape[1:])
            low = (place // bit) % 2
            terms = pick(pairs, low, 1) + swap(pick(pairs, 1 - low, 1), axis, bit * scale)
            bit *= 2
        terms = terms[0]
    return terms


def sum_tp_small(terms):
    bit = 1
    while bit < lax.axis_size("tp"):
        terms = terms + swap(terms, "tp", bit)
        bit *= 2
    return terms


def others(values, axis):
    count = lax.axis_size(axis)
    return [values[0]] + [swap(values[k], axis, k) for k in range(1, count)]


def in_order(pieces, axis):
    place = lax.axis_index(axis) ^ jnp.arange(len(pieces), dtype=jnp.int32)
    return jnp.take(jnp.stack(pieces), place, axis=0)


def place_kernel(count, place, rows, *refs):
    out = refs[-1]
    size = rows.shape[0] // count
    room = round_up(size)
    for k in range(count):
        part = rows[k * size : (k + 1) * size]
        if room > size:
            part = jnp.concatenate(
                [part, jnp.zeros((room - size, part.shape[1]), part.dtype)], axis=0
            )
        out[k * room : (k + 1) * room, :] = part


def place_columns(values, count, held, place, parts):
    rows, depth = values.shape
    n_sh = lax.axis_size("shard")
    chunk = depth // parts
    height = count * round_up(rows // count)
    operands = [values]
    specs = [pl.BlockSpec((rows, chunk), lambda c, at: (0, c))]
    aliases = {}
    if held is not None:
        aliases = {2: 0}
        operands.append(held)
        specs.append(pl.BlockSpec(memory_space=pl.ANY))
    return pl.pallas_call(
        functools.partial(place_kernel, count),
        grid_spec=pltpu.PrefetchScalarGridSpec(
            num_scalar_prefetch=1,
            grid=(parts,),
            in_specs=specs,
            out_specs=pl.BlockSpec((height, chunk), lambda c, at: (0, c * n_sh + at[0])),
        ),
        out_shape=jax.ShapeDtypeStruct((height, n_sh * depth), bf16),
        input_output_aliases=aliases,
        compiler_params=pltpu.CompilerParams(vmem_limit_bytes=32 * 2**20),
        cost_estimate=pl.CostEstimate(
            flops=0, bytes_accessed=4 * height * depth, transcendentals=0
        ),
    )(jnp.reshape(place, (1,)), *operands)


def unpack_kernel(place, *refs):
    count = len(refs) - 2
    one, two = refs[count:]
    first = one.shape[1]
    for step in range(count):

        @pl.when(pl.program_id(0) == step)
        def _(grads=refs[step]):
            one[0] = grads[:first].astype(f32)
            two[0] = grads[first:].astype(f32)


def unpack(pieces, place, first):
    count = len(pieces)
    units, own = pieces[0].shape

    def where(step, at):
        return (at[0] ^ step, 0, 0)

    return pl.pallas_call(
        unpack_kernel,
        grid_spec=pltpu.PrefetchScalarGridSpec(
            num_scalar_prefetch=1,
            grid=(count,),
            in_specs=[pl.BlockSpec((units, own), lambda step, at: (0, 0))] * count,
            out_specs=[
                pl.BlockSpec((1, first, own), where),
                pl.BlockSpec((1, units - first, own), where),
            ],
        ),
        out_shape=[
            jax.ShapeDtypeStruct((count, first, own), f32),
            jax.ShapeDtypeStruct((count, units - first, own), f32),
        ],
        compiler_params=pltpu.CompilerParams(vmem_limit_bytes=32 * 2**20),
        cost_estimate=pl.CostEstimate(
            flops=0, bytes_accessed=6 * count * own * units, transcendentals=0
        ),
    )(jnp.reshape(place, (1,)), *pieces)


def body(
    tokens_in,
    cotangent,
    expert_ids,
    prefix_len,
    attn_gain,
    qkv_weight,
    qkv_bias,
    out_weight,
    ffn_gain,
    router_weight,
    expert_gate,
    expert_up,
    expert_down,
    shared_gate,
    shared_up,
    shared_down,
    shared_switch,
):
    n_sh, n_ctx, n_tp = lax.axis_size("shard"), lax.axis_size("ctx"), lax.axis_size("tp")
    my_sh, my_ctx, my_tp = lax.axis_index("shard"), lax.axis_index("ctx"), lax.axis_index("tp")
    micro, _, rows, width = tokens_in.shape
    picks = expert_ids.shape[-1]
    tok = micro * rows
    part = tok // n_tp
    total = n_sh * tok
    length = rows * n_ctx
    depth = qkv_weight.shape[1]
    own = width // (n_sh * n_ctx)
    local_heads, head_dim = qkv_bias.shape[1:]
    heads_width = local_heads * head_dim
    experts, _, hidden = expert_gate.shape
    shared_hidden = shared_gate.shape[1]
    score_scale = head_dim ** (-0.5)
    per = max(experts // n_sh, 1)
    mine_first = experts * hidden // n_sh
    unit = mine_first // per
    used = mine_first + shared_hidden // n_sh
    block = round_up(used)

    inputs = tokens_in.reshape(tok, width)
    upstream = cotangent.reshape(tok, width)
    ids = expert_ids.reshape(tok, picks)

    def mine(values):
        return lax.dynamic_slice_in_dim(values, my_tp * part, part, 0)

    small = jnp.concatenate(
        [
            attn_gain,
            ffn_gain,
            shared_switch,
            router_weight.T.reshape(-1),
            ids.astype(bf16).reshape(-1),
        ]
    )
    small = in_order(others([small] * n_sh, "shard"), "shard")
    first_gain = small[:, :depth].reshape(width).astype(f32)
    second_gain = small[:, depth : 2 * depth].reshape(width).astype(f32)
    switch_vec = small[:, 2 * depth : 3 * depth].reshape(width)
    router_full = (
        small[:, 3 * depth : (3 + experts) * depth]
        .reshape(n_sh, experts, depth)
        .transpose(0, 2, 1)
        .reshape(width, experts)
    )
    ids_all = small[:, (3 + experts) * depth :].reshape(n_sh * n_tp // 2, 2, part, picks)
    core = my_tp % 2
    ids_all = jnp.stack([pick(ids_all, core, 1), pick(ids_all, 1 - core, 1)])
    ids_all = ids_all.reshape(total, picks).astype(jnp.int32)

    qkv_local = qkv_weight.transpose(1, 0, 2).reshape(depth, 3 * heads_width)
    qkv_full = lax.all_gather(qkv_local, "shard", axis=0, tiled=True)
    bias_row = qkv_bias.reshape(1, 3 * heads_width).astype(f32)
    out_full = lax.all_gather(out_weight, "shard", axis=1, tiled=True)

    parts = n_ctx if own % 128 == 0 else 1
    chunk = depth // parts

    def to_parts(values):
        shape = values.shape[:-1]
        values = values.reshape(shape + (n_sh, parts, chunk))
        return values.swapaxes(-3, -2).reshape(shape + (width,))

    def from_parts(values):
        shape = values.shape[:-1]
        values = values.reshape(shape + (parts, n_sh, chunk))
        return values.swapaxes(-3, -2).reshape(shape + (width,))

    gate_up_local = (
        expert_gate.transpose(0, 2, 1).reshape(n_sh, mine_first, depth),
        shared_gate.T.reshape(n_sh, used - mine_first, depth),
        expert_up.transpose(0, 2, 1).reshape(n_sh, mine_first, depth),
        shared_up.T.reshape(n_sh, used - mine_first, depth),
    )
    down_local = (
        expert_down.reshape(n_sh, mine_first, depth),
        shared_down.reshape(n_sh, used - mine_first, depth),
    )

    def fetch(values, k, after):
        values = jnp.concatenate([pick(v, my_sh ^ k, 0) for v in values])
        return swap(tie(values, after), "shard", k) if k else values

    def fetch_gate_up(which, after, held):
        for k in which:
            values = fetch(gate_up_local, k, after)
            held = place_columns(values, 2, held, my_sh ^ k, parts)
        return held

    near, far = range(n_sh // 2 + 1), range(n_sh // 2 + 1, n_sh)

    normed_one = rms_scale(inputs.astype(f32), first_gain).astype(bf16)
    projected = (dot(normed_one, qkv_full) + bias_row).astype(bf16)

    def heads(values):
        return values.reshape(micro, rows, local_heads, head_dim).transpose(0, 2, 1, 3)

    def flat(values):
        return values.transpose(0, 2, 1, 3).reshape(tok, heads_width)

    cosine, sine_table = rope_tables(length, head_dim)
    cosine = lax.dynamic_slice_in_dim(cosine, my_ctx * rows, rows, 0)
    sine_table = lax.dynamic_slice_in_dim(sine_table, my_ctx * rows, rows, 0)
    query_rows, key_rows = (
        rotate(
            heads(projected[:, k * heads_width : (k + 1) * heads_width]).astype(f32),
            cosine,
            sine_table,
        ).astype(bf16)
        for k in range(2)
    )
    value_rows = heads(projected[:, 2 * heads_width :])
    own_rows = jnp.stack([key_rows, value_rows])
    other_rows = swap(own_rows, "ctx", 1)
    gate_up = fetch_gate_up(near, qkv_full, None)
    key_all, value_all = jnp.concatenate([own_rows, other_rows], axis=3)
    steps = jnp.arange(rows, dtype=jnp.int32)
    query_at = my_ctx * rows + steps
    key_at = jnp.concatenate([query_at, (1 - my_ctx) * rows + steps])
    allowed = (key_at[None, :] <= query_at[:, None])[None] | (
        key_at[None, None, :] < prefix_len.reshape(micro, 1, 1)
    )
    scores = (
        jnp.einsum("mhqd,mhkd->mhqk", query_rows, key_all, preferred_element_type=f32)
        * score_scale
    )
    scores = jnp.where(allowed[:, None], scores, -1000000000.0)
    raised = jnp.exp(scores - jnp.max(scores, axis=-1, keepdims=True))
    probs = raised / jnp.sum(raised, axis=-1, keepdims=True)
    probs_low = probs.astype(bf16)
    head_rows = flat(
        jnp.einsum("mhqk,mhkd->mhqd", probs_low, value_all, preferred_element_type=f32).astype(
            bf16
        )
    )
    head_rows = tie(head_rows, gate_up)
    gate_up = fetch_gate_up(far, other_rows, gate_up)
    down_pieces = [fetch(down_local, k, head_rows) for k in range(n_sh)]
    attn_total = sum_tp(dot(head_rows, out_full).reshape(n_tp, part, width))

    my_inputs = mine(inputs).astype(f32)
    my_up = mine(upstream).astype(f32)
    hidden_res = my_inputs + tie(attn_total, gate_up, *down_pieces)
    second_float, second_pull = jax.vjp(rms_scale, hidden_res, second_gain)
    my_normed = second_float.astype(bf16)
    normed_two = both_cores(gather_core(to_parts(my_normed)))
    up_core = gather_core(tie(to_parts(mine(upstream)), my_normed))
    routing = jnp.concatenate([router_full, switch_vec[:, None]], axis=1)

    def route(values, weights):
        logits = dot(values, weights)
        return jax.nn.softmax(logits[:, :experts], axis=-1), jax.nn.sigmoid(logits[:, experts])

    probs_all, switch_all = route(normed_two, to_parts(routing.T).T)
    first_expert = my_sh * experts // n_sh
    gates, names = [], []
    for k in range(per):
        named = jnp.any(ids_all == first_expert + k, axis=1)
        chosen = lax.dynamic_index_in_dim(probs_all, first_expert + k, 1, keepdims=False)
        names.append(named)
        gates.append(jnp.where(named, chosen, 0.0))
    gates.append(switch_all)
    column = lax.broadcasted_iota(jnp.int32, (total, block), 1)
    gate_wide = jnp.broadcast_to(gates[-1][:, None], (total, block))
    for k in reversed(range(per)):
        gate_wide = jnp.where(column < (k + 1) * unit, gates[k][:, None], gate_wide)

    pre = dot_cols(normed_two, gate_up)
    pre_gate, pre_up = pre[:, :block], pre[:, block:]
    sigma = jax.nn.sigmoid(pre_gate)
    silu = pre_gate * sigma
    act = silu * pre_up
    act_low = (gate_wide * act).astype(bf16)
    up_all = both_cores(tie(up_core, pre))
    down = None
    for k in range(n_sh):
        down = place_columns(tie(down_pieces[k], pre), 1, down, my_sh ^ k, parts)
    back = dot_cols(up_all, down)
    act_grad = gate_wide * back
    pre_grad = jnp.concatenate(
        [
            (act_grad * pre_up * (sigma + silu * (1.0 - sigma))).astype(bf16),
            (act_grad * silu).astype(bf16),
        ],
        axis=1,
    )
    product = act * back
    lane = lax.broadcasted_iota(jnp.int32, (1, 128), 1)
    gate_terms = jnp.zeros((total, 128), f32)
    for k in range(per + 1):
        inside = (column >= k * unit) & (column < ((k + 1) * unit if k < per else block))
        term = jnp.sum(jnp.where(inside, product, 0.0), axis=1)
        if k < per:
            term = jnp.where(names[k], term, 0.0)
        at = first_expert + k if k < per else experts
        gate_terms = gate_terms + jnp.where(lane == at, term[:, None], 0.0)
    half = total // 2
    peers = n_sh * n_tp // 2

    def grad_whole(units, values):
        if parts == n_ctx:
            span = width // n_ctx
            return jnp.stack(
                [
                    dot_rows(units, values[:, c * span : (c + 1) * span]).astype(bf16)
                    for c in range(n_ctx)
                ]
            )
        whole = dot_rows(units, values).astype(bf16)
        return whole.reshape(used, n_sh, n_ctx, own).transpose(2, 0, 1, 3).reshape(n_ctx, used, -1)

    def sum_ctx_parts(whole):
        return lax.psum_scatter(whole, "ctx", scatter_dimension=0, tiled=True)[0]

    down_whole = grad_whole(act_low[:, :used], up_all)
    down_piece = sum_ctx_parts(down_whole)
    pre_grad = tie(pre_grad, down_whole)

    def spread(values):
        return values.astype(bf16).reshape(peers, part, values.shape[-1])

    gate_terms = sum_rows_small(gate_terms.reshape(2, peers, part, gate_terms.shape[-1]))
    own_grad = sum_core(
        spread(dot(pre_grad[half:], gate_up)),
        lambda: dot(pre_grad[:half], gate_up).reshape(peers, part, width),
    )
    pre_grad = tie(pre_grad, own_grad)
    gate_whole = grad_whole(pre_grad[:, :used], normed_two)
    up_whole = grad_whole(pre_grad[:, block : block + used], normed_two)
    cut_at = used // 2
    gate_first = sum_ctx_parts(gate_whole[:, :cut_at])
    act_low = tie(act_low, up_whole)
    own_mixed = sum_core(
        spread(dot(act_low[half:], down)),
        lambda: dot(act_low[:half], down).reshape(peers, part, width),
    )
    normed_grad = sum_shard_z(tie(own_grad, gate_terms))
    own_mixed = tie(own_mixed, normed_grad)
    normed_grad = from_parts(tie(normed_grad, gate_whole, up_whole, own_mixed))
    ffn_total = from_parts(sum_shard_z(own_mixed))

    def settle(piece):
        pieces = [
            lax.dynamic_slice_in_dim(piece, (my_sh ^ k) * own, own, 1) for k in range(n_sh)
        ]
        one, two = unpack(others(pieces, "shard"), my_sh, mine_first)
        return one.reshape(experts, hidden, own), two.reshape(shared_hidden, own)

    my_probs, my_switch = route(my_normed, routing)
    prob_grads = gate_terms[:, :experts]
    logit_grads = my_probs * (
        prob_grads - jnp.sum(my_probs * prob_grads, axis=-1, keepdims=True)
    )
    switch_pre_grad = gate_terms[:, experts] * my_switch * (1.0 - my_switch)
    route_grads = jnp.concatenate([logit_grads, switch_pre_grad[:, None]], axis=1)
    normed_float = my_normed.astype(f32)
    routing_grad = lax.dot_general(
        route_grads, normed_float, (((0,), (0,)), ((), ())), precision=highest
    )
    normed_grad = normed_grad + lax.dot_general(
        route_grads, routing.astype(f32), (((1,), (1,)), ((), ())), precision=highest
    )
    hidden_norm_grad, ffn_gain_grad = second_pull(normed_grad)
    hidden_grad = my_up + hidden_norm_grad

    def sum_shard(terms):
        pieces = others([pick(terms, my_sh ^ k, 0) for k in range(n_sh)], "shard")
        return sum(piece.astype(f32) for piece in pieces)

    def sum_ctx(terms):
        arrived = swap(pick(terms, 1 - my_ctx, 0).astype(bf16), "ctx", 1)
        return pick(terms, my_ctx, 0) + arrived.astype(f32)

    branch_low = gather_tp(hidden_grad.astype(bf16))
    out_weight_grad = dot_rows(head_rows, branch_low).astype(bf16)
    out_weight_grad = sum_shard(
        out_weight_grad.reshape(-1, n_sh, n_ctx * own).transpose(1, 0, 2)
    ).reshape(-1, n_ctx, own)
    out_weight_grad = sum_ctx(out_weight_grad.transpose(1, 0, 2))
    head_grad = dot_cols(branch_low, out_full).astype(bf16)
    expert_down_grad, shared_down_grad = settle(down_piece)
    my_out = (hidden_res + ffn_total).astype(bf16)
    head_grad = heads(head_grad)
    prob_grad = jnp.einsum("mhqd,mhkd->mhqk", head_grad, value_all, preferred_element_type=f32)
    value_grad = jnp.einsum("mhqk,mhqd->mhkd", probs_low, head_grad, preferred_element_type=f32)
    score_low = (
        probs * (prob_grad - jnp.sum(probs * prob_grad, axis=-1, keepdims=True))
    ).astype(bf16)
    query_grad = jnp.einsum("mhqk,mhkd->mhqd", score_low, key_all, preferred_element_type=f32)
    key_grad = jnp.einsum("mhqk,mhqd->mhkd", score_low, query_rows, preferred_element_type=f32)
    pair_grad = jnp.stack([key_grad, value_grad])
    arrived = swap(pair_grad[..., rows:, :].astype(bf16), "ctx", 1)
    arrived = tie(arrived, expert_down_grad, shared_down_grad, my_out)
    gate_last = sum_ctx_parts(tie(gate_whole[:, cut_at:], arrived))
    up_piece = sum_ctx_parts(tie(up_whole, arrived))
    key_grad, value_grad = pair_grad[..., :rows, :] + arrived.astype(f32)
    proj_grad = jnp.concatenate(
        [
            flat(rotate(query_grad * score_scale, cosine, -sine_table).astype(bf16)),
            flat(rotate(key_grad * score_scale, cosine, -sine_table).astype(bf16)),
            flat(value_grad.astype(bf16)),
        ],
        axis=1,
    )
    one_terms = dot_cols(proj_grad, qkv_full)
    qkv_grad = dot_rows(normed_one, proj_grad).astype(bf16)
    qkv_summed = sum_shard(qkv_grad.reshape(n_sh, n_ctx * own, -1))
    qkv_grad = sum_ctx(qkv_summed.reshape(n_ctx, own, -1))
    turned_gate, shared_gate_grad = settle(
        tie(jnp.concatenate([gate_first, gate_last]), qkv_summed)
    )
    expert_gate_grad, shared_gate_grad = turned_gate.transpose(0, 2, 1), shared_gate_grad.T
    qkv_grad = qkv_grad.reshape(own, 3, heads_width).transpose(1, 0, 2)
    count = n_sh * n_ctx
    bias_own = head_dim // count
    bias_grad = jnp.sum(proj_grad.astype(f32), axis=0)
    bias_grad = bias_grad.reshape(3 * local_heads, head_dim)
    wide = inputs.astype(f32)
    factor = lax.rsqrt(jnp.mean(wide * wide, axis=-1, keepdims=True) + epsilon)
    attn_gain_grad = jnp.sum(one_terms * (wide * factor), axis=0, keepdims=True)
    late = jnp.concatenate([routing_grad, ffn_gain_grad[None], attn_gain_grad], axis=0)
    late = jnp.concatenate(
        [
            late.reshape(-1, count, own).transpose(1, 0, 2).reshape(count, -1),
            bias_grad.reshape(-1, count, bias_own).transpose(1, 0, 2).reshape(count, -1),
        ],
        axis=1,
    )
    late = jnp.sum(lax.all_to_all(late, ("shard", "ctx"), 0, 0, tiled=True), axis=0)
    bias_grad = late[(experts + 3) * own :].reshape(3, local_heads, bias_own)
    late = sum_tp_small(late[: (experts + 3) * own]).reshape(experts + 3, own)
    turned_up, shared_up_grad = settle(tie(up_piece, turned_gate))
    expert_up_grad, shared_up_grad = turned_up.transpose(0, 2, 1), shared_up_grad.T
    normed_one_grad = sum_tp(one_terms.reshape(n_tp, part, width))
    _, first_pull = jax.vjp(lambda v: rms_scale(v, first_gain), my_inputs)
    (input_norm_grad,) = first_pull(normed_one_grad)
    my_tokens_grad = (hidden_grad + input_norm_grad).astype(bf16)
    my_tokens_grad = tie(my_tokens_grad, turned_gate)
    tokens_grad = gather_tp(my_tokens_grad).astype(f32)

    layer_out = gather_tp(my_out)
    shape = (micro, 1, rows, width)
    return (
        layer_out.reshape(shape),
        tokens_grad.reshape(shape),
        late[experts + 2],
        qkv_grad,
        bias_grad,
        out_weight_grad,
        late[experts + 1],
        late[:experts].T,
        expert_gate_grad,
        expert_up_grad,
        expert_down_grad,
        shared_gate_grad,
        shared_up_grad,
        shared_down_grad,
        late[experts],
    )


def solution(mesh):
    in_specs = (
        P(None, "shard", "ctx", None),
        P(None, "shard", "ctx", None),
        P(None, "shard", "ctx", None),
        P(None, "shard"),
        P("shard"),
        P(None, "shard", "tp"),
        P(None, "tp", None),
        P("tp", "shard"),
        P("shard"),
        P("shard", None),
        P(None, "shard", "tp"),
        P(None, "shard", "tp"),
        P(None, "tp", "shard"),
        P("shard", "tp"),
        P("shard", "tp"),
        P("tp", "shard"),
        P("shard"),
    )
    out_specs = (
        P(None, "shard", "ctx", None),
        P(None, "shard", "ctx", None),
        P(("shard", "ctx")),
        P(None, ("shard", "ctx"), "tp"),
        P(None, "tp", ("shard", "ctx")),
        P("tp", ("shard", "ctx")),
        P(("shard", "ctx")),
        P(("shard", "ctx"), None),
        P(None, ("shard", "ctx"), "tp"),
        P(None, ("shard", "ctx"), "tp"),
        P(None, "tp", ("shard", "ctx")),
        P(("shard", "ctx"), "tp"),
        P(("shard", "ctx"), "tp"),
        P("tp", ("shard", "ctx")),
        P(("shard", "ctx")),
    )
    return jax.shard_map(body, mesh=mesh, in_specs=in_specs, out_specs=out_specs, check_vma=False)
```

time: 1350 us -> 993 us (0.74)
  waiting for transfers between devices: 750 us -> 450 us
  local copies, waits for them, and re-layouts: 266 us -> 138 us
  other arithmetic: 44.9 us -> 101 us
  starting transfers between devices: 43.7 us -> 67.2 us
  blocking collectives: 57.7 us -> 41 us
  Pallas kernels: 0 us -> 14.7 us
    reduce_scatter x6 -> x4, waiting for transfers between devices: 206 us -> 0.04 us  [sum_ctx_parts(): return lax.psum_scatter(whole, 'ctx', scatter_dimension=0, tiled=True)[0]]
    all_to_all x8 -> x4, waiting for transfers between devices: 189 us -> 71.8 us  [the longest x2 35.8 us: sum_shard_z(): own = lax.all_to_all(own, 'shard', 0, 0, tiled=True)]
    ppermute x12 -> x50, waiting for transfers between devices: 274 us -> 339 us  [swap(): return lax.ppermute(values, axis, [(i, i ^ bit) for i in range(count)])]
    psum x1 -> x0, blocking collectives: 48 us -> none  [body(): lax.psum(jnp.concatenate([attn_gain_grad, bias_spread]), ('shard', 'ctx',...]
    reshape x21 -> x20, local copies, waits for them, and re-layouts: 68.1 us -> 22.4 us  [the longest x5 5.99 us: to_parts(): values = values.reshape(shape + (n_sh, parts, chunk))]
    ppermute x12 -> x50, starting transfers between devices: 6.39 us -> 48.8 us  [swap(): return lax.ppermute(values, axis, [(i, i ^ bit) for i in range(count)])]
    unnamed x154 -> x251, local copies, waits for them, and re-layouts: 94.3 us -> 52.8 us
    all_to_all x0 -> x1, blocking collectives: none -> 41 us  [exchange(): lax.all_to_all(values, ('shard', 'tp'), 0, 0, tiled=True, axis_index_grou...]
  transfers between devices with their start and end apart: 32 -> 60, of which waited for: 17 -> 26; matrix products, arithmetic and copies ran while one was open for 31% -> 27% of each run, Pallas kernels for 0% -> 1%
where the time goes in v2:
time: 993 us; the launch traced here: 981 us
  waiting for transfers between devices  450 us (45%)
  matrix products  153 us (15%)
  local copies, waits for them, and re-layouts  138 us (14%)
  other arithmetic  101 us (10%)
  starting transfers between devices  67.2 us (7%)
  blocking collectives  41 us (4%)
  between operations  16.5 us (2%)
  Pallas kernels  14.7 us (1%)
    ppermute x50, waiting for transfers between devices, swap(): return lax.ppermute(values, axis, [(i, i ^ bit) for i in range(count)])  339 us
    unnamed x251, local copies, waits for them, and re-layouts  52.8 us
    dot_general x8, matrix products, dot(): return jnp.dot(left, right, preferred_element_type=f32)  49.2 us
    ppermute x50, starting transfers between devices, swap(): return lax.ppermute(values, axis, [(i, i ^ bit) for i in range(count)])  48.8 us
    dot_general x4, matrix products, dot_cols(): lax.dot_general(left, right, (((1,), (1,)), ((), ())), preferred_element_...  46.7 us
    dot_general x8, matrix products, dot_rows(): lax.dot_general(left, right, (((0,), (0,)), ((), ())), preferred_element_...  44.9 us
    all_to_all x1, blocking collectives, exchange(): lax.all_to_all(values, ('shard', 'tp'), 0, 0, tiled=True, axis_index_grou...  41 us
    all_gather x1, waiting for transfers between devices, body(): qkv_full = lax.all_gather(qkv_local, 'shard', axis=0, tiled=True)  39 us
  transfers between devices with their start and end apart: 60, of which 26 were waited for; matrix products, arithmetic and copies ran while one was open for 27% of the time, Pallas kernels for 1%

profile of v2, /device:TPU:0, one launch (start us, length us, event | category | flops | bytes accessed | tf_op | source)
XLA Modules:
  0.0 981.0 jit_solution(12566357817841203723)
XLA Ops:
  44.2 39.0 %all-gather.3.cloned.1.call-done = bf16[2048,1536]{0,1:T(8,128)(2,1)} async-done(((bf16[512,1536]{0,1:T(8,128)(2,1)}), bf16[2048,1536]{0,1:T(8,128)(2,1)}) %all-gather.3.cloned.1.call-update) | async-done | bytes 6291472 | tf_op jit(solution)/shard_map/all_gather | solution.py:333
  104.5 32.4 %collective-permute-done.3 = bf16[2,2,4,192,128]{4,3,2,1,0:T(8,128)(2,1)S(1)} collective-permute-done((bf16[2,2,4,192,128]{4,3,2,1,0:T(8,128)(2,1)S(1)}, bf16[2,2,4,192,128]{4,3,2,1,0:T(8,128)(2,1)S(1)}, u32[]{:S(2)}, u32[]{:S(2)}) %collective-permute-start.3) | collective-permute-done | bytes 786464 | tf_op jit(solution)/shard_map/ppermute | solution.py:57
  156.3 40.3 %collective-permute-done.4.rows = bf16[2112,512]{1,0:T(8,128)(2,1)S(1)} collective-permute-done((bf16[2112,512]{1,0:T(8,128)(2,1)}, bf16[2112,512]{1,0:T(8,128)(2,1)S(1)}, u32[]{:S(2)}, u32[]{:S(2)}) %collective-permute-start.4) | collective-permute-done | bytes 2162720 | tf_op jit(solution)/shard_map/ppermute | solution.py:57
  225.9 30.8 %collective-permute-done.10.rows = bf16[1056,512]{1,0:T(8,128)(2,1)S(1)} collective-permute-done((bf16[1056,512]{1,0:T(8,128)(2,1)}, bf16[1056,512]{1,0:T(8,128)(2,1)S(1)}, u32[]{:S(2)}, u32[]{:S(2)}) %collective-permute-start.10) | collective-permute-done | bytes 1081376 | tf_op jit(solution)/shard_map/ppermute | solution.py:57
  268.4 41.0 %all_to_all.29 = bf16[8,96,2048]{2,1,0:T(8,128)(2,1)} all-to-all(bf16[8,96,2048]{2,1,0:T(8,128)(2,1)S(1)} %broadcast_in_dim.181), channel_id=1, replica_groups={{0,2,8,10,16,18,24,26},{1,3,9,11,17,19,25,27},{4,6,12,14,20,22,28,30},{..., dimensions={0} | all-to-all | bytes 6291456 | tf_op jit(solution)/shard_map/all_to_all | solution.py:115
  330.6 19.5 %fusion.107 = f32[1536,2304]{1,0:T(8,128)} fusion(bf16[1536,2048]{1,0:T(8,128)(2,1)S(1)} %bitcast.381, bf16[2304,2048]{1,0:T(8,128)(2,1)} %copy-done.4), kind=kOutput, calls=%fused_computation.348 | convolution fusion | flops 14495514624 | bytes 29884416 | tf_op jit(solution)/shard_map/dot_general | solution.py:52
  350.0 16.3 %all-to-all-done.1 = bf16[8,96,2048]{2,1,0:T(8,128)(2,1)} async-done(((bf16[8,96,2048]{2,1,0:T(8,128)(2,1)}), bf16[8,96,2048]{2,1,0:T(8,128)(2,1)}, u32[]{:S(2)}, u32[]{:S(2)}) %all-to-all-start.1) | async-done | bytes 3145760 | tf_op jit(solution)/shard_map/all_to_all | solution.py:115
  386.1 21.5 %multiply_convert_fusion.1 = (bf16[1536,1152]{1,0:T(8,128)(2,1)}, bf16[1536,1152]{1,0:T(8,128)(2,1)}, f32[1536,1152]{1,0:T(8,128)}, bf16[1536,1152]{1,0:T(8,128)(2,1)}) fusion(f32[1536,2304]{1,0:T(8,128)} %fusion.107, f32[1536]{0:T(1024)S(1)} %divide_reduce_fusion, f32[1536]{0:T(1024)S(1)} %get-tuple-element.147, f32[1536]{0:T(1024)S(1)} %get-tuple-element.146, ...), kind=kOutput, calls=%fused_computation.8 | convolution fusion | flops 7281377280 | bytes 42881280 | tf_op jit(solution)/shard_map/dot_general | solution.py:52
  432.6 10.8 %fusion.6 = bf16[768,2048]{1,0:T(8,128)(2,1)} fusion(bf16[2304,2048]{1,0:T(8,128)(2,1)S(1)} %bitcast.378, bf16[1536,2304]{1,0:T(8,128)(2,1)} %pad_maximum_fusion), kind=kOutput, calls=%fused_computation.38 | convolution fusion | flops 7249330176 | bytes 16121856 | tf_op jit(solution)/shard_map/dot_general | solution.py:44
  458.9 12.3 %fusion.4 = f32[768,2048]{1,0:T(8,128)S(1)} fusion(bf16[2304,2048]{1,0:T(8,128)(2,1)} %copy-done.4, bf16[1536,2304]{1,0:T(8,128)(2,1)} %pad_maximum_fusion), kind=kOutput, calls=%fused_computation.36 | convolution fusion | flops 7247757312 | bytes 19267584 | tf_op jit(solution)/shard_map/dot_general | solution.py:44
  508.1 19.7 %all-to-all-done.2 = bf16[8,96,2048]{2,1,0:T(8,128)(2,1)S(1)} async-done(((bf16[8,96,2048]{2,1,0:T(8,128)(2,1)}), bf16[8,96,2048]{2,1,0:T(8,128)(2,1)S(1)}, u32[]{:S(2)}, u32[]{:S(2)}) %all-to-all-start.2) | async-done | bytes 3145760 | tf_op jit(solution)/shard_map/all_to_all | solution.py:137
  535.9 11.1 %collective-permute-done.20 = bf16[96,2048]{1,0:T(8,128)(2,1)S(1)} collective-permute-done((bf16[96,2048]{1,0:T(8,128)(2,1)S(1)}, bf16[96,2048]{1,0:T(8,128)(2,1)S(1)}, u32[]{:S(2)}, u32[]{:S(2)}) %collective-permute-start.20) | collective-permute-done | bytes 393248 | tf_op jit(solution)/shard_map/ppermute | solution.py:57
  575.5 16.1 %all-to-all-done.3 = bf16[8,96,2048]{2,1,0:T(8,128)(2,1)} async-done(((bf16[8,96,2048]{2,1,0:T(8,128)(2,1)}), bf16[8,96,2048]{2,1,0:T(8,128)(2,1)}, u32[]{:S(2)}, u32[]{:S(2)}) %all-to-all-start.3) | async-done | bytes 3145760 | tf_op jit(solution)/shard_map/all_to_all | solution.py:137
  597.8 20.0 %collective-permute-done.21 = bf16[96,2048]{1,0:T(8,128)(2,1)S(1)} collective-permute-done((bf16[96,2048]{1,0:T(8,128)(2,1)S(1)}, bf16[96,2048]{1,0:T(8,128)(2,1)S(1)}, u32[]{:S(2)}, u32[]{:S(2)}) %collective-permute-start.21) | collective-permute-done | bytes 393248 | tf_op jit(solution)/shard_map/ppermute | solution.py:57
  626.7 9.5 collective-permute-done.24
  655.0 11.6 %collective-permute-done.27.refs_1_ = bf16[1056,256]{1,0:T(8,128)(2,1)S(1)} collective-permute-done((bf16[1056,256]{1,0:T(8,128)(2,1)S(1)}, bf16[1056,256]{1,0:T(8,128)(2,1)S(1)}, u32[]{:S(2)}, u32[]{:S(2)}) %collective-permute-start.27) | collective-permute-done | bytes 540704 | tf_op jit(solution)/shard_map/ppermute | solution.py:57
  666.6 12.0 %collective-permute-done.28.refs_2_ = bf16[1056,256]{1,0:T(8,128)(2,1)S(1)} collective-permute-done((bf16[1056,256]{1,0:T(8,128)(2,1)S(1)}, bf16[1056,256]{1,0:T(8,128)(2,1)S(1)}, u32[]{:S(2)}, u32[]{:S(2)}) %collective-permute-start.28) | collective-permute-done | bytes 540704 | tf_op jit(solution)/shard_map/ppermute | solution.py:57
  681.0 28.7 %collective-permute-done.26 = bf16[2,2,4,192,128]{4,3,2,1,0:T(8,128)(2,1)S(1)} collective-permute-done((bf16[2,2,4,192,128]{4,3,2,1,0:T(8,128)(2,1)}, bf16[2,2,4,192,128]{4,3,2,1,0:T(8,128)(2,1)S(1)}, u32[]{:S(2)}, u32[]{:S(2)}) %collective-permute-start.26) | collective-permute-done | bytes 786464 | tf_op jit(solution)/shard_map/ppermute | solution.py:57
  711.1 12.4 %collective-permute-done.22 = bf16[1,96,2048]{2,1,0:T(8,128)(2,1)S(1)} collective-permute-done((bf16[1,96,2048]{2,1,0:T(8,128)(2,1)S(1)}, bf16[1,96,2048]{2,1,0:T(8,128)(2,1)S(1)}, u32[]{:S(2)}, u32[]{:S(2)}) %collective-permute-start.22) | collective-permute-done | bytes 393248 | tf_op jit(solution)/shard_map/ppermute | solution.py:57
  789.4 19.7 %all-to-all-done.4 = f32[8,1,3008]{2,1,0:T(1,128)} async-done(((f32[8,1,3008]{2,1,0:T(1,128)}), f32[8,1,3008]{2,1,0:T(1,128)}, u32[]{:S(2)}, u32[]{:S(2)}) %all-to-all-start.4) | async-done | bytes 96288 | tf_op jit(solution)/shard_map/all_to_all | solution.py:610
  814.1 33.8 %collective-permute-done.33 = bf16[512,1536]{1,0:T(8,128)(2,1)} collective-permute-done((bf16[512,1536]{1,0:T(8,128)(2,1)}, bf16[512,1536]{1,0:T(8,128)(2,1)}, u32[]{:S(2)}, u32[]{:S(2)}) %collective-permute-start.33) | collective-permute-done | bytes 1572896 | tf_op jit(solution)/shard_map/ppermute | solution.py:57
  870.5 10.9 %collective-permute-done.36.refs_2_ = bf16[1056,256]{1,0:T(8,128)(2,1)S(1)} collective-permute-done((bf16[1056,256]{1,0:T(8,128)(2,1)S(1)}, bf16[1056,256]{1,0:T(8,128)(2,1)S(1)}, u32[]{:S(2)}, u32[]{:S(2)}) %collective-permute-start.36) | collective-permute-done | bytes 540704 | tf_op jit(solution)/shard_map/ppermute | solution.py:57
  888.1 42.9 %collective-permute-done.38 = bf16[1,96,2048]{2,1,0:T(8,128)(2,1)} collective-permute-done((bf16[1,96,2048]{2,1,0:T(8,128)(2,1)S(1)}, bf16[1,96,2048]{2,1,0:T(8,128)(2,1)}, u32[]{:S(2)}, u32[]{:S(2)}) %collective-permute-start.38) | collective-permute-done | bytes 393248 | tf_op jit(solution)/shard_map/ppermute | solution.py:57
  958.0 12.3 %collective-permute-done.48.refs_2_ = bf16[1056,256]{1,0:T(8,128)(2,1)S(1)} collective-permute-done((bf16[1056,256]{1,0:T(8,128)(2,1)S(1)}, bf16[1056,256]{1,0:T(8,128)(2,1)S(1)}, u32[]{:S(2)}, u32[]{:S(2)}) %collective-permute-start.48) | collective-permute-done | bytes 540704 | tf_op jit(solution)/shard_map/ppermute | solution.py:57
  (596 shorter events, 439.9 us)
Async XLA Ops:
  7.2 76.0 %all-gather.3.cloned.1.call-start = ((), (), s32[]{:S(2)}) async-start(), calls=%async_computation.9 | async-start | bytes 7864320 | tf_op jit(solution)/shard_map/all_gather | solution.py:333
  10.0 190.9 %all-gather.5.cloned.1.call-start = ((), (), s32[]{:S(2)}) async-start(), calls=%async_computation.10 | async-start | bytes 2621440 | tf_op jit(solution)/shard_map/all_gather | solution.py:335
  83.2 67.1 %collective-permute-start.5 = (bf16[2112,512]{1,0:T(8,128)(2,1)}, bf16[2112,512]{1,0:T(8,128)(2,1)}, u32[]{:S(2)}, u32[]{:S(2)}) collective-permute-start(bf16[2112,512]{1,0:T(8,128)(2,1)} %pad_maximum_fusion.7), channel_id=1, source_target_pairs={{0,8},{8,0},{16,24},{24,16},{1,9},{9,1},{17,25},{25,17},{2,10},{10... | collective-permute-start | bytes 6488072 | tf_op jit(solution)/shard_map/ppermute | solution.py:57
  84.7 111.9 %collective-permute-start.4 = (bf16[2112,512]{1,0:T(8,128)(2,1)}, bf16[2112,512]{1,0:T(8,128)(2,1)S(1)}, u32[]{:S(2)}, u32[]{:S(2)}) collective-permute-start(bf16[2112,512]{1,0:T(8,128)(2,1)} %pad_maximum_fusion.6), channel_id=1, source_target_pairs={{0,16},{8,24},{16,0},{24,8},{1,17},{9,25},{17,1},{25,9},{2,18},{10... | collective-permute-start | bytes 6488072 | tf_op jit(solution)/shard_map/ppermute | solution.py:57
  144.9 70.6 %collective-permute-start.8 = (bf16[2112,512]{1,0:T(8,128)(2,1)}, bf16[2112,512]{1,0:T(8,128)(2,1)}, u32[]{:S(2)}, u32[]{:S(2)}) collective-permute-start(bf16[2112,512]{1,0:T(8,128)(2,1)} %pad_maximum_fusion.9), channel_id=1, source_target_pairs={{0,24},{8,16},{16,8},{24,0},{1,25},{9,17},{17,9},{25,1},{2,26},{10... | collective-permute-start | bytes 6488072 | tf_op jit(solution)/shard_map/ppermute | solution.py:57
  207.0 49.6 %collective-permute-start.10 = (bf16[1056,512]{1,0:T(8,128)(2,1)}, bf16[1056,512]{1,0:T(8,128)(2,1)S(1)}, u32[]{:S(2)}, u32[]{:S(2)}) collective-permute-start(bf16[1056,512]{1,0:T(8,128)(2,1)} %pad_maximum_fusion.15), channel_id=1, source_target_pairs={{0,16},{8,24},{16,0},{24,8},{1,17},{9,25},{17,1},{25,9},{2,18},{10... | collective-permute-start | bytes 3244040 | tf_op jit(solution)/shard_map/ppermute | solution.py:57
  207.6 49.0 %collective-permute-start.11 = (bf16[1056,512]{1,0:T(8,128)(2,1)}, bf16[1056,512]{1,0:T(8,128)(2,1)S(1)}, u32[]{:S(2)}, u32[]{:S(2)}) collective-permute-start(bf16[1056,512]{1,0:T(8,128)(2,1)} %pad_maximum_fusion.16), channel_id=1, source_target_pairs={{0,24},{8,16},{16,8},{24,0},{1,25},{9,17},{17,9},{25,1},{2,26},{10... | collective-permute-start | bytes 3244040 | tf_op jit(solution)/shard_map/ppermute | solution.py:57
  209.1 48.9 %collective-permute-start.9 = (bf16[1056,512]{1,0:T(8,128)(2,1)}, bf16[1056,512]{1,0:T(8,128)(2,1)}, u32[]{:S(2)}, u32[]{:S(2)}) collective-permute-start(bf16[1056,512]{1,0:T(8,128)(2,1)} %pad_maximum_fusion.14), channel_id=1, source_target_pairs={{0,8},{8,0},{16,24},{24,16},{1,9},{9,1},{17,25},{25,17},{2,10},{10... | collective-permute-start | bytes 3244040 | tf_op jit(solution)/shard_map/ppermute | solution.py:57
  320.1 46.2 %all-to-all-start.1 = ((bf16[8,96,2048]{2,1,0:T(8,128)(2,1)}), bf16[8,96,2048]{2,1,0:T(8,128)(2,1)}, u32[]{:S(2)}, u32[]{:S(2)}) async-start(bf16[8,96,2048]{2,1,0:T(8,128)(2,1)} %broadcast_in_dim.189), calls=%async_computation.1 | async-start | bytes 6291456 | tf_op jit(solution)/shard_map/all_to_all | solution.py:115
  492.3 157.4 %reduce-scatter.5.cloned.1.call-start = ((), (), s32[]{:S(2)}) async-start(), calls=%async_computation.11 | async-start | bytes 6488064 | tf_op jit(solution)/shard_map/reduce_scatter | solution.py:494
  506.1 41.0 %collective-permute-start.15 = (bf16[8,96,2048]{2,1,0:T(8,128)(2,1)}, bf16[8,96,2048]{2,1,0:T(8,128)(2,1)}, u32[]{:S(2)}, u32[]{:S(2)}) collective-permute-start(bf16[8,96,2048]{2,1,0:T(8,128)(2,1)} %bitcast.79), channel_id=1, source_target_pairs={{0,1},{1,0},{2,3},{3,2},{4,5},{5,4},{6,7},{7,6},{8,9},{9,8},{10,11... | collective-permute-start | bytes 9437192 | tf_op jit(solution)/shard_map/ppermute | solution.py:57
  551.9 39.7 %all-to-all-start.3 = ((bf16[8,96,2048]{2,1,0:T(8,128)(2,1)}), bf16[8,96,2048]{2,1,0:T(8,128)(2,1)}, u32[]{:S(2)}, u32[]{:S(2)}) async-start(bf16[8,96,2048]{2,1,0:T(8,128)(2,1)} %add_convert_fusion), calls=%async_computation.3 | async-start | bytes 6291456 | tf_op jit(solution)/shard_map/all_to_all | solution.py:137
  556.7 295.1 %reduce-scatter.7.cloned.1.call-start = ((), (), s32[]{:S(2)}) async-start(), calls=%async_computation.12 | async-start | bytes 3244032 | tf_op jit(solution)/shard_map/reduce_scatter | solution.py:494
  626.4 225.4 %reduce-scatter.9.cloned.1.call-start = ((), (), s32[]{:S(2)}) async-start(), calls=%async_computation.13 | async-start | bytes 3244032 | tf_op jit(solution)/shard_map/reduce_scatter | solution.py:494
  649.7 60.0 %collective-permute-start.26 = (bf16[2,2,4,192,128]{4,3,2,1,0:T(8,128)(2,1)}, bf16[2,2,4,192,128]{4,3,2,1,0:T(8,128)(2,1)S(1)}, u32[]{:S(2)}, u32[]{:S(2)}) collective-permute-start(bf16[2,2,4,192,128]{4,3,2,1,0:T(8,128)(2,1)} %fusion.39), channel_id=1, source_target_pairs={{0,4},{4,0},{1,5},{5,1},{2,6},{6,2},{3,7},{7,3},{8,12},{12,8},{9,1... | collective-permute-start | bytes 2359304 | tf_op jit(solution)/shard_map/ppermute | solution.py:57
  710.6 230.5 %reduce-scatter.11.cloned.1.call-start = ((), (), s32[]{:S(2)}) async-start(), calls=%async_computation.14 | async-start | bytes 6488064 | tf_op jit(solution)/shard_map/reduce_scatter | solution.py:494
  741.6 42.1 %collective-permute-start.44 = (bf16[512,512]{1,0:T(8,128)(2,1)}, bf16[512,512]{1,0:T(8,128)(2,1)}, u32[]{:S(2)}, u32[]{:S(2)}) collective-permute-start(bf16[512,512]{1,0:T(8,128)(2,1)} %bitcast.369), channel_id=1, source_target_pairs={{0,16},{8,24},{16,0},{24,8},{1,17},{9,25},{17,1},{25,9},{2,18},{10... | collective-permute-start | bytes 1572872 | tf_op jit(solution)/shard_map/ppermute | solution.py:57
  744.0 40.2 %collective-permute-start.45 = (bf16[512,512]{1,0:T(8,128)(2,1)}, bf16[512,512]{1,0:T(8,128)(2,1)}, u32[]{:S(2)}, u32[]{:S(2)}) collective-permute-start(bf16[512,512]{1,0:T(8,128)(2,1)} %bitcast.368), channel_id=1, source_target_pairs={{0,24},{8,16},{16,8},{24,0},{1,25},{9,17},{17,9},{25,1},{2,26},{10... | collective-permute-start | bytes 1572872 | tf_op jit(solution)/shard_map/ppermute | solution.py:57
  769.4 44.6 %collective-permute-start.32 = (bf16[512,1536]{1,0:T(8,128)(2,1)}, bf16[512,1536]{1,0:T(8,128)(2,1)}, u32[]{:S(2)}, u32[]{:S(2)}) collective-permute-start(bf16[512,1536]{1,0:T(8,128)(2,1)} %get-tuple-element.158), channel_id=1, source_target_pairs={{0,8},{8,0},{16,24},{24,16},{1,9},{9,1},{17,25},{25,17},{2,10},{10... | collective-permute-start | bytes 4718600 | tf_op jit(solution)/shard_map/ppermute | solution.py:57
  776.4 71.5 %collective-permute-start.33 = (bf16[512,1536]{1,0:T(8,128)(2,1)}, bf16[512,1536]{1,0:T(8,128)(2,1)}, u32[]{:S(2)}, u32[]{:S(2)}) collective-permute-start(bf16[512,1536]{1,0:T(8,128)(2,1)} %get-tuple-element.160), channel_id=1, source_target_pairs={{0,16},{8,24},{16,0},{24,8},{1,17},{9,25},{17,1},{25,9},{2,18},{10... | collective-permute-start | bytes 4718600 | tf_op jit(solution)/shard_map/ppermute | solution.py:57
  779.3 68.6 %collective-permute-start.34 = (bf16[512,1536]{1,0:T(8,128)(2,1)}, bf16[512,1536]{1,0:T(8,128)(2,1)}, u32[]{:S(2)}, u32[]{:S(2)}) collective-permute-start(bf16[512,1536]{1,0:T(8,128)(2,1)} %get-tuple-element.159), channel_id=1, source_target_pairs={{0,24},{8,16},{16,8},{24,0},{1,25},{9,17},{17,9},{25,1},{2,26},{10... | collective-permute-start | bytes 4718600 | tf_op jit(solution)/shard_map/ppermute | solution.py:57
  812.4 71.1 %collective-permute-start.46 = (bf16[512,256]{0,1:T(8,128)(2,1)}, bf16[512,256]{0,1:T(8,128)(2,1)}, u32[]{:S(2)}, u32[]{:S(2)}) collective-permute-start(bf16[512,256]{0,1:T(8,128)(2,1)} %fusion.70), channel_id=1, source_target_pairs={{0,4},{4,0},{1,5},{5,1},{2,6},{6,2},{3,7},{7,3},{8,12},{12,8},{9,1... | collective-permute-start | bytes 786440 | tf_op jit(solution)/shard_map/ppermute | solution.py:57
  859.5 73.6 %collective-permute-start.42 = (bf16[256,1536]{1,0:T(8,128)(2,1)}, bf16[256,1536]{1,0:T(8,128)(2,1)}, u32[]{:S(2)}, u32[]{:S(2)}) collective-permute-start(bf16[256,1536]{1,0:T(8,128)(2,1)} %fusion.52), channel_id=1, source_target_pairs={{0,4},{4,0},{1,5},{5,1},{2,6},{6,2},{3,7},{7,3},{8,12},{12,8},{9,1... | collective-permute-start | bytes 2359304 | tf_op jit(solution)/shard_map/ppermute | solution.py:57
  883.5 47.5 %collective-permute-start.38 = (bf16[1,96,2048]{2,1,0:T(8,128)(2,1)S(1)}, bf16[1,96,2048]{2,1,0:T(8,128)(2,1)}, u32[]{:S(2)}, u32[]{:S(2)}) collective-permute-start(bf16[1,96,2048]{2,1,0:T(8,128)(2,1)S(1)} %bitcast.419), channel_id=1, source_target_pairs={{0,2},{1,3},{2,0},{3,1},{4,6},{5,7},{6,4},{7,5},{8,10},{9,11},{10,... | collective-permute-start | bytes 1179656 | tf_op jit(solution)/shard_map/ppermute | solution.py:57
  (153 other events, 1759.3 us)
Sparse Core Ops, SparseCore 0:
  10.5 72.7 all-gather.2
  85.0 52.2 all-gather.4
  506.2 104.6 reduce-scatter.4
  626.5 89.9 reduce-scatter.6
  719.2 55.6 reduce-scatter.8
  777.2 147.0 reduce-scatter.10

commit v3 on v2

--- a/solution.py
+++ b/solution.py
@@ -13,6 +13,7 @@
 highest = lax.Precision.HIGHEST
 f32 = jnp.float32
 bf16 = jnp.bfloat16
+small_cost = pl.CostEstimate(flops=1000, bytes_accessed=1000, transcendentals=0)
 
 
 def rms_scale(values, gain_vec):
@@ -123,38 +124,18 @@
 
 
 def both_cores(own):
-    return jnp.concatenate([own, swap(own, "tp", 1)]).reshape(-1, own.shape[-1])
-
-
-def sum_core(other, make_own):
-    arrived = swap(other, "tp", 1)
-    return (make_own().astype(f32) + arrived.astype(f32)).astype(bf16)
-
-
-def sum_shard_z(own):
-    half = lax.axis_size("tp") // 2
+    flat = (own.shape[0] * own.shape[1], own.shape[2])
+    return own.reshape(flat), swap(own, "tp", 1).reshape(flat)
+
+
+def sum_shard(pieces):
     z = lax.axis_index("tp") // 2
-    own = lax.all_to_all(own, "shard", 0, 0, tiled=True)
-    own = jnp.sum(own.reshape((-1, half) + own.shape[1:]).astype(f32), axis=0)
-    return pick(own, z, 0) + swap(pick(own, 1 - z, 0).astype(bf16), "tp", 2).astype(f32)
-
-
-def sum_rows_small(terms):
-    n_sh, half = lax.axis_size("shard"), lax.axis_size("tp") // 2
-    terms = terms[0] + swap(terms[1], "tp", 1)
-    terms = terms.reshape((n_sh, half) + terms.shape[1:]).swapaxes(0, 1)
-    for axis, place, scale in (
-        ("tp", lax.axis_index("tp") // 2, 2),
-        ("shard", lax.axis_index("shard"), 1),
-    ):
-        bit = 1
-        while terms.shape[0] > 1:
-            pairs = terms.reshape((terms.shape[0] // 2, 2) + terms.shape[1:])
-            low = (place // bit) % 2
-            terms = pick(pairs, low, 1) + swap(pick(pairs, 1 - low, 1), axis, bit * scale)
-            bit *= 2
-        terms = terms[0]
-    return terms
+    own = sum(piece.astype(f32) for piece in pieces)
+    return pick(own, z, 0), pick(own, 1 - z, 0).astype(bf16)
+
+
+def swap_z(sent):
+    return swap(sent, "tp", 2).astype(f32)
 
 
 def sum_tp_small(terms):
@@ -215,6 +196,151 @@
             flops=0, bytes_accessed=4 * height * depth, transcendentals=0
         ),
     )(jnp.reshape(place, (1,)), *operands)
+
+
+def hidden_kernel(
+    bounds, step, values_a, values_b, up_a, up_b, gate_up, down, gates, act_out, grad_out, terms_out
+):
+    block = down.shape[0]
+    pairs = pl.num_programs(0) // 2
+    first = pl.program_id(0) < pairs
+    values = jnp.where(first, values_a[...], values_b[...])
+    up = jnp.where(first, up_a[...], up_b[...])
+    tile = values.shape[0]
+    count = len(bounds)
+    gate_columns = [gates[:, k : k + 1] for k in range(count)]
+    named_columns = [gates[:, count + k : count + k + 1] for k in range(count)]
+    lane = lax.broadcasted_iota(jnp.int32, (1, 128), 1)
+    terms = jnp.zeros((tile, 128), f32)
+    for j in range(block // step):
+        at = j * step
+        pre_gate = dot_cols(values, gate_up[at : at + step, :])
+        pre_up = dot_cols(values, gate_up[block + at : block + at + step, :])
+        back = dot_cols(up, down[at : at + step, :])
+        column = at + lax.broadcasted_iota(jnp.int32, (1, step), 1)
+        sigma = jax.nn.sigmoid(pre_gate)
+        silu = pre_gate * sigma
+        act = silu * pre_up
+        product = act * back
+        wide = jnp.zeros((tile, step), f32)
+        low = 0
+        for k in range(count):
+            if low < at + step and bounds[k] > at:
+                inside = (column >= low) & (column < bounds[k])
+                wide = jnp.where(inside, gate_columns[k], wide)
+                term = jnp.sum(jnp.where(inside, product, 0.0), axis=1, keepdims=True)
+                terms = terms + jnp.where(lane == k, term * named_columns[k], 0.0)
+            low = bounds[k]
+        act_grad = wide * back
+        act_out[:, at : at + step] = (wide * act).astype(bf16)
+        grad_out[:, at : at + step] = (act_grad * pre_up * (sigma + silu * (1.0 - sigma))).astype(
+            bf16
+        )
+        grad_out[:, block + at : block + at + step] = (act_grad * silu).astype(bf16)
+    terms_out[...] = terms
+
+
+def hidden_units(values, up, gate_up, down, gates, bounds):
+    half, width = values[0].shape
+    block = down.shape[0]
+    tile = half // 2 if half % 32 == 0 and half <= 1024 else 384
+    pairs = half // tile
+    own_rows = pl.BlockSpec((tile, width), lambda i: (jnp.minimum(i, pairs - 1), 0))
+    other_rows = pl.BlockSpec((tile, width), lambda i: (jnp.maximum(i - pairs, 0), 0))
+    return pl.pallas_call(
+        functools.partial(hidden_kernel, bounds, 128 if block % 384 else 384),
+        grid=(2 * pairs,),
+        in_specs=[
+            own_rows,
+            other_rows,
+            own_rows,
+            other_rows,
+            pl.BlockSpec((2 * block, width), lambda i: (0, 0), pipeline_mode=pl.Buffered(1)),
+            pl.BlockSpec((block, width), lambda i: (0, 0), pipeline_mode=pl.Buffered(1)),
+            pl.BlockSpec((tile, 128), lambda i: (i, 0)),
+        ],
+        out_specs=[
+            pl.BlockSpec((tile, block), lambda i: (i, 0)),
+            pl.BlockSpec((tile, 2 * block), lambda i: (i, 0)),
+            pl.BlockSpec((tile, 128), lambda i: (i, 0)),
+        ],
+        out_shape=[
+            jax.ShapeDtypeStruct((2 * half, block), bf16),
+            jax.ShapeDtypeStruct((2 * half, 2 * block), bf16),
+            jax.ShapeDtypeStruct((2 * half, 128), f32),
+        ],
+        compiler_params=pltpu.CompilerParams(vmem_limit_bytes=60 * 2**20),
+        cost_estimate=small_cost,
+    )(values[0], values[1], up[0], up[1], gate_up, down, gates)
+
+
+def rows_kernel(left, right, *refs):
+    out = refs[-1]
+    value = dot(left[...], right[...])
+    if len(refs) > 1:
+        value = value + refs[0][...].astype(f32)
+    out[...] = value.astype(bf16)
+
+
+def cost(flops, nbytes):
+    return pl.CostEstimate(flops=flops, bytes_accessed=nbytes, transcendentals=0)
+
+
+def rows_dot(left, which, right, add=None, urgent=True):
+    half, depth = left.shape[0] // 2, left.shape[1]
+    width = right.shape[1]
+    step = 512
+    specs = [
+        pl.BlockSpec((half, depth), lambda j: (which, 0), pipeline_mode=pl.Buffered(1)),
+        pl.BlockSpec((depth, step), lambda j: (0, j)),
+    ]
+    out_spec = pl.BlockSpec((half, step), lambda j: (0, j))
+    operands = [left, right]
+    if add is not None:
+        operands.append(add)
+        specs.append(out_spec)
+    return pl.pallas_call(
+        rows_kernel,
+        grid=(width // step,),
+        in_specs=specs,
+        out_specs=out_spec,
+        out_shape=jax.ShapeDtypeStruct((half, width), bf16),
+        compiler_params=pltpu.CompilerParams(vmem_limit_bytes=56 * 2**20),
+        cost_estimate=small_cost if urgent else cost(2 * half * depth * width, 8 * half * width),
+    )(*operands)
+
+
+def units_kernel(used, units, values_a, values_b, out, turned):
+    half = values_a.shape[0]
+
+    @pl.when(pl.program_id(0) == 0)
+    def _():
+        for j in range(units.shape[0] // 128):
+            turned[:, j * 128 : (j + 1) * 128] = units[j * 128 : (j + 1) * 128, :].T
+
+    value = dot(turned[:, :half], values_a[...]) + dot(turned[:, half:], values_b[...])
+    out[0] = value[:used].astype(bf16)
+
+
+def units_dot(units, which, used, values, parts):
+    half, width = values[0].shape
+    block = round_up(used)
+    step = 256
+    each = width // parts // step
+    return pl.pallas_call(
+        functools.partial(units_kernel, used),
+        grid=(width // step,),
+        in_specs=[
+            pl.BlockSpec((2 * half, block), lambda j: (0, which), pipeline_mode=pl.Buffered(1)),
+            pl.BlockSpec((half, step), lambda j: (0, j)),
+            pl.BlockSpec((half, step), lambda j: (0, j)),
+        ],
+        out_specs=pl.BlockSpec((1, used, step), lambda j: (j // each, 0, j % each)),
+        out_shape=jax.ShapeDtypeStruct((parts, used, width // parts), bf16),
+        scratch_shapes=[pltpu.VMEM((block, 2 * half), bf16)],
+        compiler_params=pltpu.CompilerParams(vmem_limit_bytes=56 * 2**20),
+        cost_estimate=small_cost,
+    )(units, values[0], values[1])
 
 
 def unpack_kernel(place, *refs):
@@ -417,115 +543,102 @@
     head_rows = tie(head_rows, gate_up)
     gate_up = fetch_gate_up(far, other_rows, gate_up)
     down_pieces = [fetch(down_local, k, head_rows) for k in range(n_sh)]
+    up_spread = to_parts(mine(upstream))
+    up_spread = jnp.broadcast_to(up_spread[None], (n_sh * n_tp // 2, part, width))
     attn_total = sum_tp(dot(head_rows, out_full).reshape(n_tp, part, width))
 
     my_inputs = mine(inputs).astype(f32)
     my_up = mine(upstream).astype(f32)
-    hidden_res = my_inputs + tie(attn_total, gate_up, *down_pieces)
+    hidden_res = my_inputs + tie(attn_total, gate_up, up_spread, *down_pieces)
     second_float, second_pull = jax.vjp(rms_scale, hidden_res, second_gain)
     my_normed = second_float.astype(bf16)
-    normed_two = both_cores(gather_core(to_parts(my_normed)))
-    up_core = gather_core(tie(to_parts(mine(upstream)), my_normed))
+    normed_core = gather_core(to_parts(my_normed))
+    normed_two = both_cores(normed_core)
+    up_core = exchange(tie(up_spread, normed_core))
     routing = jnp.concatenate([router_full, switch_vec[:, None]], axis=1)
 
     def route(values, weights):
         logits = dot(values, weights)
         return jax.nn.softmax(logits[:, :experts], axis=-1), jax.nn.sigmoid(logits[:, experts])
 
-    probs_all, switch_all = route(normed_two, to_parts(routing.T).T)
+    routing_parts = to_parts(routing.T).T
+    probs_all, switch_all = (
+        jnp.concatenate(both) for both in zip(*(route(v, routing_parts) for v in normed_two))
+    )
     first_expert = my_sh * experts // n_sh
-    gates, names = [], []
+    gates, names, bounds = [], [], []
     for k in range(per):
         named = jnp.any(ids_all == first_expert + k, axis=1)
         chosen = lax.dynamic_index_in_dim(probs_all, first_expert + k, 1, keepdims=False)
-        names.append(named)
+        names.append(named.astype(f32))
         gates.append(jnp.where(named, chosen, 0.0))
+        bounds.append((k + 1) * unit)
     gates.append(switch_all)
-    column = lax.broadcasted_iota(jnp.int32, (total, block), 1)
-    gate_wide = jnp.broadcast_to(gates[-1][:, None], (total, block))
-    for k in reversed(range(per)):
-        gate_wide = jnp.where(column < (k + 1) * unit, gates[k][:, None], gate_wide)
-
-    pre = dot_cols(normed_two, gate_up)
-    pre_gate, pre_up = pre[:, :block], pre[:, block:]
-    sigma = jax.nn.sigmoid(pre_gate)
-    silu = pre_gate * sigma
-    act = silu * pre_up
-    act_low = (gate_wide * act).astype(bf16)
-    up_all = both_cores(tie(up_core, pre))
+    names.append(jnp.ones_like(switch_all))
+    bounds.append(used)
+    gates = pad_to(jnp.stack(gates + names, axis=1), 1, 128)
+
+    up_all = both_cores(up_core)
     down = None
     for k in range(n_sh):
-        down = place_columns(tie(down_pieces[k], pre), 1, down, my_sh ^ k, parts)
-    back = dot_cols(up_all, down)
-    act_grad = gate_wide * back
-    pre_grad = jnp.concatenate(
-        [
-            (act_grad * pre_up * (sigma + silu * (1.0 - sigma))).astype(bf16),
-            (act_grad * silu).astype(bf16),
-        ],
-        axis=1,
-    )
-    product = act * back
+        down = place_columns(down_pieces[k], 1, down, my_sh ^ k, parts)
+    act_low, pre_grad, gate_terms = hidden_units(
+        normed_two, up_all, gate_up, down, gates, tuple(bounds)
+    )
     lane = lax.broadcasted_iota(jnp.int32, (1, 128), 1)
-    gate_terms = jnp.zeros((total, 128), f32)
-    for k in range(per + 1):
-        inside = (column >= k * unit) & (column < ((k + 1) * unit if k < per else block))
-        term = jnp.sum(jnp.where(inside, product, 0.0), axis=1)
-        if k < per:
-            term = jnp.where(names[k], term, 0.0)
-        at = first_expert + k if k < per else experts
-        gate_terms = gate_terms + jnp.where(lane == at, term[:, None], 0.0)
+    gate_terms = sum(
+        jnp.where(lane == (first_expert + k if k < per else experts), gate_terms[:, k : k + 1], 0.0)
+        for k in range(per + 1)
+    )
     half = total // 2
     peers = n_sh * n_tp // 2
 
-    def grad_whole(units, values):
+    def grad_whole(units, which, values):
+        whole = units_dot(units, which, used, values, parts)
         if parts == n_ctx:
-            span = width // n_ctx
-            return jnp.stack(
-                [
-                    dot_rows(units, values[:, c * span : (c + 1) * span]).astype(bf16)
-                    for c in range(n_ctx)
-                ]
-            )
-        whole = dot_rows(units, values).astype(bf16)
-        return whole.reshape(used, n_sh, n_ctx, own).transpose(2, 0, 1, 3).reshape(n_ctx, used, -1)
+            return whole
+        whole = whole.reshape(used, n_sh, n_ctx, own)
+        return whole.transpose(2, 0, 1, 3).reshape(n_ctx, used, -1)
 
     def sum_ctx_parts(whole):
-        return lax.psum_scatter(whole, "ctx", scatter_dimension=0, tiled=True)[0]
-
-    down_whole = grad_whole(act_low[:, :used], up_all)
+        return lax.psum_scatter(whole, "ctx", scatter_dimension=0, tiled=True)
+
+    def sum_core(left, right, urgent):
+        arrived = swap(rows_dot(left, 1, right, None, urgent), "tp", 1)
+        return rows_dot(left, 0, right, arrived, urgent)
+
+    def by_shard(own):
+        own = own.reshape(n_sh, n_tp // 2, part, own.shape[-1])
+        return [pick(own, my_sh ^ k, 0) for k in range(n_sh)]
+
+    gate_terms = gate_terms.reshape(2, half, gate_terms.shape[-1])
+    gate_terms = (gate_terms[0] + swap(gate_terms[1], "tp", 1)).astype(bf16)
+    down_whole = grad_whole(act_low, 0, up_all)
     down_piece = sum_ctx_parts(down_whole)
-    pre_grad = tie(pre_grad, down_whole)
-
-    def spread(values):
-        return values.astype(bf16).reshape(peers, part, values.shape[-1])
-
-    gate_terms = sum_rows_small(gate_terms.reshape(2, peers, part, gate_terms.shape[-1]))
-    own_grad = sum_core(
-        spread(dot(pre_grad[half:], gate_up)),
-        lambda: dot(pre_grad[:half], gate_up).reshape(peers, part, width),
-    )
-    pre_grad = tie(pre_grad, own_grad)
-    gate_whole = grad_whole(pre_grad[:, :used], normed_two)
-    up_whole = grad_whole(pre_grad[:, block : block + used], normed_two)
-    cut_at = used // 2
-    gate_first = sum_ctx_parts(gate_whole[:, :cut_at])
-    act_low = tie(act_low, up_whole)
-    own_mixed = sum_core(
-        spread(dot(act_low[half:], down)),
-        lambda: dot(act_low[:half], down).reshape(peers, part, width),
-    )
-    normed_grad = sum_shard_z(tie(own_grad, gate_terms))
-    own_mixed = tie(own_mixed, normed_grad)
-    normed_grad = from_parts(tie(normed_grad, gate_whole, up_whole, own_mixed))
-    ffn_total = from_parts(sum_shard_z(own_mixed))
-
-    def settle(piece):
-        pieces = [
-            lax.dynamic_slice_in_dim(piece, (my_sh ^ k) * own, own, 1) for k in range(n_sh)
+    own_grad = sum_core(tie(pre_grad, down_whole), gate_up, True)
+    own_grad = by_shard(jnp.concatenate([own_grad, gate_terms], axis=1))
+    own_mixed = sum_core(tie(act_low, *own_grad), down, False)
+    own_grad = [tie(v, own_mixed) for v in others(own_grad, "shard")]
+    mixed = [tie(v, *own_grad) for v in by_shard(own_mixed)]
+    mixed = others(mixed, "shard")
+    grad_kept, grad_sent = sum_shard(own_grad)
+    gate_whole = grad_whole(tie(pre_grad, grad_sent), 0, normed_two)
+    gate_piece = sum_ctx_parts(gate_whole)
+    normed_grad = grad_kept + tie(swap_z(grad_sent), gate_whole)
+    gate_terms = normed_grad[:, width:]
+    normed_grad = from_parts(normed_grad[:, :width])
+
+    def owned(piece):
+        return [
+            lax.dynamic_slice_in_dim(piece[0], (my_sh ^ k) * own, own, 1) for k in range(n_sh)
         ]
-        one, two = unpack(others(pieces, "shard"), my_sh, mine_first)
-        return one.reshape(experts, hidden, own), two.reshape(shared_hidden, own)
+
+    def settle(pieces, *after):
+        return unpack([tie(p, *after) for p in pieces], my_sh, mine_first)
+
+    def turned(one, two):
+        one = one.reshape(experts, hidden, own).transpose(0, 2, 1)
+        return one, two.reshape(shared_hidden, own).T
 
     my_probs, my_switch = route(my_normed, routing)
     prob_grads = gate_terms[:, :experts]
@@ -544,23 +657,28 @@
     hidden_norm_grad, ffn_gain_grad = second_pull(normed_grad)
     hidden_grad = my_up + hidden_norm_grad
 
-    def sum_shard(terms):
-        pieces = others([pick(terms, my_sh ^ k, 0) for k in range(n_sh)], "shard")
-        return sum(piece.astype(f32) for piece in pieces)
-
-    def sum_ctx(terms):
-        arrived = swap(pick(terms, 1 - my_ctx, 0).astype(bf16), "ctx", 1)
-        return pick(terms, my_ctx, 0) + arrived.astype(f32)
-
-    branch_low = gather_tp(hidden_grad.astype(bf16))
+    def pieces_of(terms):
+        return [pick(terms, my_sh ^ k, 0) for k in range(n_sh)]
+
+    def sum_pieces(pieces, *after):
+        return sum(tie(piece, *after).astype(f32) for piece in others(pieces, "shard"))
+
+    def for_other(terms):
+        return pick(terms, 1 - my_ctx, 0).astype(bf16)
+
+
+    my_branch = hidden_grad.astype(bf16)
+    up_whole = grad_whole(tie(pre_grad, my_branch), 1, normed_two)
+    up_piece = sum_ctx_parts(up_whole)
+    down_terms = others(owned(down_piece), "shard")
+    mixed_kept, mixed_sent = sum_shard([tie(v, my_branch) for v in mixed])
+    branch_low = tie(gather_tp(my_branch), up_whole, mixed_sent, *down_terms)
     out_weight_grad = dot_rows(head_rows, branch_low).astype(bf16)
-    out_weight_grad = sum_shard(
-        out_weight_grad.reshape(-1, n_sh, n_ctx * own).transpose(1, 0, 2)
-    ).reshape(-1, n_ctx, own)
-    out_weight_grad = sum_ctx(out_weight_grad.transpose(1, 0, 2))
+    out_terms = [
+        lax.dynamic_slice_in_dim(out_weight_grad, (my_sh ^ k) * n_ctx * own, n_ctx * own, 1)
+        for k in range(n_sh)
+    ]
     head_grad = dot_cols(branch_low, out_full).astype(bf16)
-    expert_down_grad, shared_down_grad = settle(down_piece)
-    my_out = (hidden_res + ffn_total).astype(bf16)
     head_grad = heads(head_grad)
     prob_grad = jnp.einsum("mhqd,mhkd->mhqk", head_grad, value_all, preferred_element_type=f32)
     value_grad = jnp.einsum("mhqk,mhqd->mhkd", probs_low, head_grad, preferred_element_type=f32)
@@ -570,10 +688,17 @@
     query_grad = jnp.einsum("mhqk,mhkd->mhqd", score_low, key_all, preferred_element_type=f32)
     key_grad = jnp.einsum("mhqk,mhqd->mhkd", score_low, query_rows, preferred_element_type=f32)
     pair_grad = jnp.stack([key_grad, value_grad])
-    arrived = swap(pair_grad[..., rows:, :].astype(bf16), "ctx", 1)
-    arrived = tie(arrived, expert_down_grad, shared_down_grad, my_out)
-    gate_last = sum_ctx_parts(tie(gate_whole[:, cut_at:], arrived))
-    up_piece = sum_ctx_parts(tie(up_whole, arrived))
+    pair_sent = pair_grad[..., rows:, :].astype(bf16)
+    arrived = swap(pair_sent, "ctx", 1)
+    down_parts = settle(down_terms, pair_sent)
+    expert_down_grad = down_parts[0].reshape(experts, hidden, own)
+    shared_down_grad = down_parts[1].reshape(shared_hidden, own)
+    out_summed = sum_pieces(out_terms, pair_sent)
+    gate_parts = settle(others(owned(gate_piece), "shard"), pair_sent)
+    mixed_sum = mixed_kept + swap_z(tie(mixed_sent, pair_sent))
+    my_out = (hidden_res + from_parts(mixed_sum)).astype(bf16)
+    layer_out = gather_tp(my_out)
+    arrived = tie(arrived, my_out, *down_parts, out_summed, *gate_parts)
     key_grad, value_grad = pair_grad[..., :rows, :] + arrived.astype(f32)
     proj_grad = jnp.concatenate(
         [
@@ -583,15 +708,19 @@
         ],
         axis=1,
     )
-    one_terms = dot_cols(proj_grad, qkv_full)
     qkv_grad = dot_rows(normed_one, proj_grad).astype(bf16)
-    qkv_summed = sum_shard(qkv_grad.reshape(n_sh, n_ctx * own, -1))
-    qkv_grad = sum_ctx(qkv_summed.reshape(n_ctx, own, -1))
-    turned_gate, shared_gate_grad = settle(
-        tie(jnp.concatenate([gate_first, gate_last]), qkv_summed)
-    )
-    expert_gate_grad, shared_gate_grad = turned_gate.transpose(0, 2, 1), shared_gate_grad.T
-    qkv_grad = qkv_grad.reshape(own, 3, heads_width).transpose(1, 0, 2)
+    qkv_terms = qkv_grad.reshape(n_sh, n_ctx * own, -1)
+    in_square = n_sh == 4
+    if in_square:
+        my_x, my_y = my_sh % 2, my_sh // 2
+        middle = qkv_terms.shape[2] // 2
+        qkv_terms = qkv_terms.reshape(2, 2, n_ctx * own, -1)
+        one_half, two_half = qkv_terms[..., :middle], qkv_terms[..., middle:]
+        kept_terms = pick(one_half, my_x, 1), pick(two_half, my_y, 0)
+        qkv_terms = [pick(one_half, 1 - my_x, 1), pick(two_half, 1 - my_y, 0)]
+    else:
+        qkv_terms = pieces_of(qkv_terms)
+    one_terms = dot_cols(tie(proj_grad, *qkv_terms), qkv_full)
     count = n_sh * n_ctx
     bias_own = head_dim // count
     bias_grad = jnp.sum(proj_grad.astype(f32), axis=0)
@@ -607,19 +736,48 @@
         ],
         axis=1,
     )
-    late = jnp.sum(lax.all_to_all(late, ("shard", "ctx"), 0, 0, tiled=True), axis=0)
+    expert_gate_grad, shared_gate_grad = turned(*gate_parts)
+    out_summed = tie(out_summed, one_terms).reshape(-1, n_ctx, own).transpose(1, 0, 2)
+    out_got = swap(for_other(out_summed), "ctx", 1)
+    out_weight_grad = pick(out_summed, my_ctx, 0) + out_got.astype(f32)
+    normed_one_grad = sum_tp(one_terms.reshape(n_tp, part, width))
+    if in_square:
+        one_half = kept_terms[0].astype(f32) + swap(qkv_terms[0], "shard", 1).astype(f32)
+        two_half = kept_terms[1].astype(f32) + swap(qkv_terms[1], "shard", 2).astype(f32)
+        kept_terms = pick(one_half, my_y, 0), pick(two_half, my_x, 0)
+        qkv_terms = [
+            pick(one_half, 1 - my_y, 0).astype(bf16),
+            pick(two_half, 1 - my_x, 0).astype(bf16),
+        ]
+        normed_one_grad = tie(normed_one_grad, *qkv_terms)
+    _, first_pull = jax.vjp(lambda v: rms_scale(v, first_gain), my_inputs)
+    (input_norm_grad,) = first_pull(normed_one_grad)
+    my_tokens_grad = tie((hidden_grad + input_norm_grad).astype(bf16), out_got)
+    tokens_grad = gather_tp(my_tokens_grad).astype(f32)
+    late_rows = lax.all_to_all(tie(late, my_tokens_grad), ("shard", "ctx"), 0, 0, tiled=True)
+    late = jnp.sum(late_rows, axis=0)
     bias_grad = late[(experts + 3) * own :].reshape(3, local_heads, bias_own)
     late = sum_tp_small(late[: (experts + 3) * own]).reshape(experts + 3, own)
-    turned_up, shared_up_grad = settle(tie(up_piece, turned_gate))
-    expert_up_grad, shared_up_grad = turned_up.transpose(0, 2, 1), shared_up_grad.T
-    normed_one_grad = sum_tp(one_terms.reshape(n_tp, part, width))
-    _, first_pull = jax.vjp(lambda v: rms_scale(v, first_gain), my_inputs)
-    (input_norm_grad,) = first_pull(normed_one_grad)
-    my_tokens_grad = (hidden_grad + input_norm_grad).astype(bf16)
-    my_tokens_grad = tie(my_tokens_grad, turned_gate)
-    tokens_grad = gather_tp(my_tokens_grad).astype(f32)
-
-    layer_out = gather_tp(my_out)
+    up_terms = owned(tie(up_piece, my_tokens_grad, late_rows))
+    if in_square:
+        qkv_got = [swap(qkv_terms[0], "shard", 2), swap(qkv_terms[1], "shard", 1)]
+        qkv_summed = jnp.concatenate(
+            [
+                kept + tie(got, my_tokens_grad, *up_terms).astype(f32)
+                for kept, got in zip(kept_terms, qkv_got)
+            ],
+            axis=1,
+        )
+    else:
+        qkv_summed = sum_pieces(qkv_terms, my_tokens_grad, *up_terms)
+    up_terms = others(up_terms, "shard")
+    qkv_summed = qkv_summed.reshape(n_ctx, own, -1)
+    qkv_sent = for_other(qkv_summed)
+    qkv_got = swap(qkv_sent, "ctx", 1)
+    qkv_grad = pick(qkv_summed, my_ctx, 0) + qkv_got.astype(f32)
+    qkv_grad = qkv_grad.reshape(own, 3, heads_width).transpose(1, 0, 2)
+
+    expert_up_grad, shared_up_grad = turned(*settle(up_terms, qkv_got))
     shape = (micro, 1, rows, width)
     return (
         layer_out.reshape(shape),

time: 993 us -> 867 us (0.87)
  Pallas kernels: 14.7 us -> 140 us
  matrix products: 153 us -> 35.9 us
  waiting for transfers between devices: 450 us -> 353 us
  other arithmetic: 101 us -> 68.3 us
    pallas_call x0 -> x8, Pallas kernels: none -> 123 us  [the longest x1 41.7 us: hidden_units(): pl.pallas_call(functools.partial(hidden_kernel, bounds, 128 if block % 38...]
    ppermute x50 -> x54, waiting for transfers between devices: 339 us -> 256 us  [swap(): return lax.ppermute(values, axis, [(i, i ^ bit) for i in range(count)])]
    all_to_all x3 -> x1, waiting for transfers between devices: 55.5 us -> 0.01 us  [body(): lax.all_to_all(tie(late, my_tokens_grad), ('shard', 'ctx'), 0, 0, tiled=T...]
    dot_general x4 -> x2, matrix products: 46.7 us -> 5 us  [dot_cols(): lax.dot_general(left, right, (((1,), (1,)), ((), ())), preferred_element_...]
    dot_general x8 -> x2, matrix products: 44.9 us -> 5.61 us  [dot_rows(): lax.dot_general(left, right, (((0,), (0,)), ((), ())), preferred_element_...]
    dot_general x8 -> x5, matrix products: 49.2 us -> 13.3 us  [dot(): return jnp.dot(left, right, preferred_element_type=f32)]
    reduce_scatter x4 -> x3, waiting for transfers between devices: 0.04 us -> 27.5 us  [sum_ctx_parts(): return lax.psum_scatter(whole, 'ctx', scatter_dimension=0, tiled=True)]
    all_to_all x1, waiting for transfers between devices: 16.3 us -> 35.7 us  [exchange(): lax.all_to_all(values, ('shard', 'tp'), 0, 0, tiled=True, axis_index_grou...]
  transfers between devices with their start and end apart: 60 -> 61, of which waited for: 26 -> 25; matrix products, arithmetic and copies ran while one was open for 27% -> 22% of each run, Pallas kernels for 1% -> 8%
where the time goes in v3:
time: 867 us; the launch traced here: 855 us
  waiting for transfers between devices  353 us (41%)
  Pallas kernels  140 us (16%)
  local copies, waits for them, and re-layouts  132 us (15%)
  other arithmetic  68.3 us (8%)
  starting transfers between devices  68.2 us (8%)
  blocking collectives  40.4 us (5%)
  matrix products  35.9 us (4%)
  between operations  16.2 us (2%)
    ppermute x54, waiting for transfers between devices, swap(): return lax.ppermute(values, axis, [(i, i ^ bit) for i in range(count)])  256 us
    unnamed x258, local copies, waits for them, and re-layouts  58.9 us
    ppermute x54, starting transfers between devices, swap(): return lax.ppermute(values, axis, [(i, i ^ bit) for i in range(count)])  56.7 us
    pallas_call x1, Pallas kernels, hidden_units(): pl.pallas_call(functools.partial(hidden_kernel, bounds, 128 if block % 38...  41.7 us
    pallas_call x4, Pallas kernels, rows_dot(): pl.pallas_call(rows_kernel, grid=(width // step,), in_specs=specs, out_sp...  40.8 us
    pallas_call x3, Pallas kernels, units_dot(): pl.pallas_call(functools.partial(units_kernel, used), grid=(width // step...  40.7 us
    all_to_all x1, blocking collectives, exchange(): lax.all_to_all(values, ('shard', 'tp'), 0, 0, tiled=True, axis_index_grou...  40.4 us
    all_to_all x1, waiting for transfers between devices, exchange(): lax.all_to_all(values, ('shard', 'tp'), 0, 0, tiled=True, axis_index_grou...  35.7 us
  transfers between devices with their start and end apart: 61, of which 25 were waited for; matrix products, arithmetic and copies ran while one was open for 22% of the time, Pallas kernels for 8%

profile of v3, /device:TPU:0, one launch (start us, length us, event | category | flops | bytes accessed | tf_op | source)
XLA Modules:
  0.0 855.1 jit_solution(2501074540993295531)
XLA Ops:
  49.0 34.4 %all-gather.3.cloned.1.call-done = bf16[2048,1536]{0,1:T(8,128)(2,1)} async-done(((bf16[512,1536]{0,1:T(8,128)(2,1)}), bf16[2048,1536]{0,1:T(8,128)(2,1)}) %all-gather.3.cloned.1.call-update) | async-done | bytes 6291472 | tf_op jit(solution)/shard_map/all_gather | solution.py:459
  99.2 31.7 %collective-permute-done.3 = bf16[2,2,4,192,128]{4,3,2,1,0:T(8,128)(2,1)S(1)} collective-permute-done((bf16[2,2,4,192,128]{4,3,2,1,0:T(8,128)(2,1)S(1)}, bf16[2,2,4,192,128]{4,3,2,1,0:T(8,128)(2,1)S(1)}, u32[]{:S(2)}, u32[]{:S(2)}) %collective-permute-start.3) | collective-permute-done | bytes 786464 | tf_op jit(solution)/shard_map/ppermute | solution.py:58
  139.0 19.7 %collective-permute-done.5.rows = bf16[2112,512]{1,0:T(8,128)(2,1)} collective-permute-done((bf16[2112,512]{1,0:T(8,128)(2,1)}, bf16[2112,512]{1,0:T(8,128)(2,1)}, u32[]{:S(2)}, u32[]{:S(2)}) %collective-permute-start.5) | collective-permute-done | bytes 2162720 | tf_op jit(solution)/shard_map/ppermute | solution.py:58
  187.4 17.8 %collective-permute-done.8.rows = bf16[2112,512]{1,0:T(8,128)(2,1)S(1)} collective-permute-done((bf16[2112,512]{1,0:T(8,128)(2,1)}, bf16[2112,512]{1,0:T(8,128)(2,1)S(1)}, u32[]{:S(2)}, u32[]{:S(2)}) %collective-permute-start.8) | collective-permute-done | bytes 2162720 | tf_op jit(solution)/shard_map/ppermute | solution.py:58
  214.5 13.8 %collective-permute-done.9.rows = bf16[1056,512]{1,0:T(8,128)(2,1)} collective-permute-done((bf16[1056,512]{1,0:T(8,128)(2,1)}, bf16[1056,512]{1,0:T(8,128)(2,1)}, u32[]{:S(2)}, u32[]{:S(2)}) %collective-permute-start.9) | collective-permute-done | bytes 1081376 | tf_op jit(solution)/shard_map/ppermute | solution.py:58
  228.4 21.8 %collective-permute-done.11.rows = bf16[1056,512]{1,0:T(8,128)(2,1)} collective-permute-done((bf16[1056,512]{1,0:T(8,128)(2,1)}, bf16[1056,512]{1,0:T(8,128)(2,1)}, u32[]{:S(2)}, u32[]{:S(2)}) %collective-permute-start.11) | collective-permute-done | bytes 1081376 | tf_op jit(solution)/shard_map/ppermute | solution.py:58
  255.7 40.4 %all_to_all.19 = bf16[8,96,2048]{2,1,0:T(8,128)(2,1)} all-to-all(bf16[8,96,2048]{2,1,0:T(8,128)(2,1)S(1)} %broadcast_in_dim.152), channel_id=1, replica_groups={{0,2,8,10,16,18,24,26},{1,3,9,11,17,19,25,27},{4,6,12,14,20,22,28,30},{..., dimensions={0} | all-to-all | bytes 6291456 | tf_op jit(solution)/shard_map/all_to_all | solution.py:116
  300.8 35.7 %all-to-all-done.1 = bf16[8,96,2048]{2,1,0:T(8,128)(2,1)} async-done(((bf16[8,96,2048]{2,1,0:T(8,128)(2,1)}), bf16[8,96,2048]{2,1,0:T(8,128)(2,1)}, u32[]{:S(2)}, u32[]{:S(2)}) %all-to-all-start.1) | async-done | bytes 3145760 | tf_op jit(solution)/shard_map/all_to_all | solution.py:116
  354.2 41.7 %shard_map.306 = (bf16[1536,1152]{1,0:T(8,128)(2,1)}, bf16[1536,2304]{1,0:T(8,128)(2,1)}, f32[1536,128]{1,0:T(8,128)}) custom-call(bf16[768,2048]{1,0:T(8,128)(2,1)} %bitcast.364, bf16[768,2048]{1,0:T(8,128)(2,1)} %bitcast.65.values_b, bf16[768,2048]{1,0:T(8,128)(2,1)} %bitcast.66.up_a.values_a, bf16[768,2048]{1,0:T(8,128)(2,1)} %bitcast.67.up_b.values_b, ...), custom_call_target="tpu_custom_call" | custom-call | flops 1000 | bytes 1000 | tf_op jit(solution)/shard_map/pallas_call | solution.py:250
  395.9 13.6 %shard_map.307 = bf16[2,1056,1024]{2,1,0:T(8,128)(2,1)} custom-call(bf16[1536,1152]{1,0:T(8,128)(2,1)} %get-tuple-element.90.units.left, bf16[768,2048]{1,0:T(8,128)(2,1)} %bitcast.66.up_a.values_a, bf16[768,2048]{1,0:T(8,128)(2,1)} %bitcast.67.up_b.values_b), custom_call_target="tpu_custom_call" | custom-call | flops 1000 | bytes 1000 | tf_op jit(solution)/shard_map/pallas_call | solution.py:330
  409.5 11.8 %shard_map.308 = bf16[768,2048]{1,0:T(8,128)(2,1)} custom-call(bf16[1536,2304]{1,0:T(8,128)(2,1)} %get-tuple-element.105.left.units, bf16[2304,2048]{1,0:T(8,128)(2,1)} %copy-done.4), custom_call_target="tpu_custom_call" | custom-call | flops 1000 | bytes 1000 | tf_op jit(solution)/shard_map/pallas_call | solution.py:302
  427.7 12.6 %shard_map.309 = bf16[768,2048]{1,0:T(8,128)(2,1)} custom-call(bf16[1536,2304]{1,0:T(8,128)(2,1)} %get-tuple-element.105.left.units, bf16[2304,2048]{1,0:T(8,128)(2,1)} %copy-done.4, bf16[768,2048]{1,0:T(8,128)(2,1)} %collective-permute-done.14.refs_0_), custom_call_target="tpu_custom_call" | custom-call | flops 1000 | bytes 1000 | tf_op jit(solution)/shard_map/pallas_call | solution.py:302
  442.8 7.9 shard_map.310
  456.8 8.5 shard_map.311
  472.7 17.1 %collective-permute-done.18 = bf16[2,96,2176]{2,1,0:T(8,128)(2,1)} collective-permute-done((bf16[2,96,2176]{2,1,0:T(8,128)(2,1)S(1)}, bf16[2,96,2176]{2,1,0:T(8,128)(2,1)}, u32[]{:S(2)}, u32[]{:S(2)}) %collective-permute-start.18) | collective-permute-done | bytes 835616 | tf_op jit(solution)/shard_map/ppermute | solution.py:58
  493.8 13.6 %shard_map.312 = bf16[2,1056,1024]{2,1,0:T(8,128)(2,1)} custom-call(bf16[1536,2304]{1,0:T(8,128)(2,1)} %get-tuple-element.105.left.units, bf16[768,2048]{1,0:T(8,128)(2,1)} %bitcast.365, bf16[768,2048]{1,0:T(8,128)(2,1)} %bitcast.65.values_b), custom_call_target="tpu_custom_call" | custom-call | flops 1000 | bytes 1000 | tf_op jit(solution)/shard_map/pallas_call | solution.py:330
  519.5 15.3 %collective-permute-done.20 = bf16[96,2176]{1,0:T(8,128)(2,1)} collective-permute-done((bf16[96,2176]{1,0:T(8,128)(2,1)}, bf16[96,2176]{1,0:T(8,128)(2,1)}, u32[]{:S(2)}, u32[]{:S(2)}) %collective-permute-start.20) | collective-permute-done | bytes 417824 | tf_op jit(solution)/shard_map/ppermute | solution.py:58
  544.8 13.6 %shard_map.313 = bf16[2,1056,1024]{2,1,0:T(8,128)(2,1)} custom-call(bf16[1536,2304]{1,0:T(8,128)(2,1)} %get-tuple-element.105.left.units, bf16[768,2048]{1,0:T(8,128)(2,1)} %bitcast.366, bf16[768,2048]{1,0:T(8,128)(2,1)} %bitcast.65.values_b), custom_call_target="tpu_custom_call" | custom-call | flops 1000 | bytes 1000 | tf_op jit(solution)/shard_map/pallas_call | solution.py:330
  582.0 12.4 %collective-permute-done.27.refs_2_ = bf16[1056,256]{1,0:T(8,128)(2,1)S(1)} collective-permute-done((bf16[1056,256]{1,0:T(8,128)(2,1)S(1)}, bf16[1056,256]{1,0:T(8,128)(2,1)S(1)}, u32[]{:S(2)}, u32[]{:S(2)}) %collective-permute-start.27) | collective-permute-done | bytes 540704 | tf_op jit(solution)/shard_map/ppermute | solution.py:58
  617.8 15.5 %collective-permute-done.29 = bf16[96,2048]{1,0:T(8,128)(2,1)S(1)} collective-permute-done((bf16[96,2048]{1,0:T(8,128)(2,1)S(1)}, bf16[96,2048]{1,0:T(8,128)(2,1)S(1)}, u32[]{:S(2)}, u32[]{:S(2)}) %collective-permute-start.29) | collective-permute-done | bytes 393248 | tf_op jit(solution)/shard_map/ppermute | solution.py:58
  637.8 27.5 %reduce-scatter.6.cloned.1.call-done = bf16[1,1056,1024]{2,1,0:T(8,128)(2,1)} async-done(((bf16[2,1056,1024]{2,1,0:T(8,128)(2,1)}), bf16[1,1056,1024]{2,1,0:T(8,128)(2,1)}) %reduce-scatter.6.cloned.1.call-update) | async-done | bytes 2162704 | tf_op jit(solution)/shard_map/reduce_scatter | solution.py:604
  682.2 11.6 %collective-permute-done.37.refs_2_ = bf16[1056,256]{1,0:T(8,128)(2,1)S(1)} collective-permute-done((bf16[1056,256]{1,0:T(8,128)(2,1)S(1)}, bf16[1056,256]{1,0:T(8,128)(2,1)S(1)}, u32[]{:S(2)}, u32[]{:S(2)}) %collective-permute-start.37) | collective-permute-done | bytes 540704 | tf_op jit(solution)/shard_map/ppermute | solution.py:58
  731.8 17.6 %collective-permute-done.40 = bf16[1,96,2048]{2,1,0:T(8,128)(2,1)} collective-permute-done((bf16[1,96,2048]{2,1,0:T(8,128)(2,1)}, bf16[1,96,2048]{2,1,0:T(8,128)(2,1)}, u32[]{:S(2)}, u32[]{:S(2)}) %collective-permute-start.40) | collective-permute-done | bytes 393248 | tf_op jit(solution)/shard_map/ppermute | solution.py:58
  812.8 21.5 %collective-permute-done.50 = bf16[256,1536]{1,0:T(8,128)(2,1)} collective-permute-done((bf16[256,1536]{1,0:T(8,128)(2,1)}, bf16[256,1536]{1,0:T(8,128)(2,1)}, u32[]{:S(2)}, u32[]{:S(2)}) %collective-permute-start.50) | collective-permute-done | bytes 786464 | tf_op jit(solution)/shard_map/ppermute | solution.py:58
  (602 shorter events, 361.7 us)
Async XLA Ops:
  7.2 76.1 %all-gather.3.cloned.1.call-start = ((), (), s32[]{:S(2)}) async-start(), calls=%async_computation.6 | async-start | bytes 7864320 | tf_op jit(solution)/shard_map/all_gather | solution.py:459
  10.0 160.3 %all-gather.5.cloned.1.call-start = ((), (), s32[]{:S(2)}) async-start(), calls=%async_computation.7 | async-start | bytes 2621440 | tf_op jit(solution)/shard_map/all_gather | solution.py:461
  90.3 74.0 %collective-permute-start.4 = (bf16[2112,512]{1,0:T(8,128)(2,1)}, bf16[2112,512]{1,0:T(8,128)(2,1)}, u32[]{:S(2)}, u32[]{:S(2)}) collective-permute-start(bf16[2112,512]{1,0:T(8,128)(2,1)} %pad_maximum_fusion.2), channel_id=1, source_target_pairs={{0,16},{8,24},{16,0},{24,8},{1,17},{9,25},{17,1},{25,9},{2,18},{10... | collective-permute-start | bytes 6488072 | tf_op jit(solution)/shard_map/ppermute | solution.py:58
  91.8 66.9 %collective-permute-start.5 = (bf16[2112,512]{1,0:T(8,128)(2,1)}, bf16[2112,512]{1,0:T(8,128)(2,1)}, u32[]{:S(2)}, u32[]{:S(2)}) collective-permute-start(bf16[2112,512]{1,0:T(8,128)(2,1)} %pad_maximum_fusion.3), channel_id=1, source_target_pairs={{0,8},{8,0},{16,24},{24,16},{1,9},{9,1},{17,25},{25,17},{2,10},{10... | collective-permute-start | bytes 6488072 | tf_op jit(solution)/shard_map/ppermute | solution.py:58
  137.5 67.7 %collective-permute-start.8 = (bf16[2112,512]{1,0:T(8,128)(2,1)}, bf16[2112,512]{1,0:T(8,128)(2,1)S(1)}, u32[]{:S(2)}, u32[]{:S(2)}) collective-permute-start(bf16[2112,512]{1,0:T(8,128)(2,1)} %pad_maximum_fusion.5), channel_id=1, source_target_pairs={{0,24},{8,16},{16,8},{24,0},{1,25},{9,17},{17,9},{25,1},{2,26},{10... | collective-permute-start | bytes 6488072 | tf_op jit(solution)/shard_map/ppermute | solution.py:58
  176.4 51.9 %collective-permute-start.9 = (bf16[1056,512]{1,0:T(8,128)(2,1)}, bf16[1056,512]{1,0:T(8,128)(2,1)}, u32[]{:S(2)}, u32[]{:S(2)}) collective-permute-start(bf16[1056,512]{1,0:T(8,128)(2,1)} %pad_maximum_fusion.9), channel_id=1, source_target_pairs={{0,8},{8,0},{16,24},{24,16},{1,9},{9,1},{17,25},{25,17},{2,10},{10... | collective-permute-start | bytes 3244040 | tf_op jit(solution)/shard_map/ppermute | solution.py:58
  176.7 51.7 %collective-permute-start.10 = (bf16[1056,512]{1,0:T(8,128)(2,1)}, bf16[1056,512]{1,0:T(8,128)(2,1)}, u32[]{:S(2)}, u32[]{:S(2)}) collective-permute-start(bf16[1056,512]{1,0:T(8,128)(2,1)} %pad_maximum_fusion.10), channel_id=1, source_target_pairs={{0,16},{8,24},{16,0},{24,8},{1,17},{9,25},{17,1},{25,9},{2,18},{10... | collective-permute-start | bytes 3244040 | tf_op jit(solution)/shard_map/ppermute | solution.py:58
  178.5 71.7 %collective-permute-start.11 = (bf16[1056,512]{1,0:T(8,128)(2,1)}, bf16[1056,512]{1,0:T(8,128)(2,1)}, u32[]{:S(2)}, u32[]{:S(2)}) collective-permute-start(bf16[1056,512]{1,0:T(8,128)(2,1)} %pad_maximum_fusion.11), channel_id=1, source_target_pairs={{0,24},{8,16},{16,8},{24,0},{1,25},{9,17},{17,9},{25,1},{2,26},{10... | collective-permute-start | bytes 3244040 | tf_op jit(solution)/shard_map/ppermute | solution.py:58
  296.1 40.3 %all-to-all-start.1 = ((bf16[8,96,2048]{2,1,0:T(8,128)(2,1)}), bf16[8,96,2048]{2,1,0:T(8,128)(2,1)}, u32[]{:S(2)}, u32[]{:S(2)}) async-start(bf16[8,96,2048]{2,1,0:T(8,128)(2,1)} %broadcast_in_dim.150), calls=%async_computation.1 | async-start | bytes 6291456 | tf_op jit(solution)/shard_map/all_to_all | solution.py:116
  300.6 264.4 %reduce-scatter.4.cloned.1.call-start = ((), (), s32[]{:S(2)}) async-start(), calls=%async_computation.8 | async-start | bytes 6488064 | tf_op jit(solution)/shard_map/reduce_scatter | solution.py:604
  300.7 49.2 %collective-permute-start.12 = (bf16[8,96,2048]{2,1,0:T(8,128)(2,1)}, bf16[8,96,2048]{2,1,0:T(8,128)(2,1)}, u32[]{:S(2)}, u32[]{:S(2)}) collective-permute-start(bf16[8,96,2048]{2,1,0:T(8,128)(2,1)} %all_to_all.19), channel_id=1, source_target_pairs={{0,1},{1,0},{2,3},{3,2},{4,5},{5,4},{6,7},{7,6},{8,9},{9,8},{10,11... | collective-permute-start | bytes 9437192 | tf_op jit(solution)/shard_map/ppermute | solution.py:58
  421.8 243.4 %reduce-scatter.6.cloned.1.call-start = ((), (), s32[]{:S(2)}) async-start(), calls=%async_computation.9 | async-start | bytes 6488064 | tf_op jit(solution)/shard_map/reduce_scatter | solution.py:604
  507.4 277.5 %reduce-scatter.8.cloned.1.call-start = ((), (), s32[]{:S(2)}) async-start(), calls=%async_computation.10 | async-start | bytes 6488064 | tf_op jit(solution)/shard_map/reduce_scatter | solution.py:604
  515.5 42.9 %collective-permute-start.23 = (bf16[2,96,2048]{2,1,0:T(8,128)(2,1)}, bf16[2,96,2048]{2,1,0:T(8,128)(2,1)}, u32[]{:S(2)}, u32[]{:S(2)}) collective-permute-start(bf16[2,96,2048]{2,1,0:T(8,128)(2,1)} %get-tuple-element.103), channel_id=1, source_target_pairs={{0,24},{8,16},{16,8},{24,0},{1,25},{9,17},{17,9},{25,1},{2,26},{10... | collective-permute-start | bytes 2359304 | tf_op jit(solution)/shard_map/ppermute | solution.py:58
  517.5 41.0 %collective-permute-start.22 = (bf16[2,96,2048]{2,1,0:T(8,128)(2,1)}, bf16[2,96,2048]{2,1,0:T(8,128)(2,1)}, u32[]{:S(2)}, u32[]{:S(2)}) collective-permute-start(bf16[2,96,2048]{2,1,0:T(8,128)(2,1)} %get-tuple-element.101), channel_id=1, source_target_pairs={{0,16},{8,24},{16,0},{24,8},{1,17},{9,25},{17,1},{25,9},{2,18},{10... | collective-permute-start | bytes 2359304 | tf_op jit(solution)/shard_map/ppermute | solution.py:58
  518.9 39.6 %collective-permute-start.21 = (bf16[2,96,2048]{2,1,0:T(8,128)(2,1)}, bf16[2,96,2048]{2,1,0:T(8,128)(2,1)}, u32[]{:S(2)}, u32[]{:S(2)}) collective-permute-start(bf16[2,96,2048]{2,1,0:T(8,128)(2,1)} %get-tuple-element.99), channel_id=1, source_target_pairs={{0,8},{8,0},{16,24},{24,16},{1,9},{9,1},{17,25},{25,17},{2,10},{10... | collective-permute-start | bytes 2359304 | tf_op jit(solution)/shard_map/ppermute | solution.py:58
  606.7 89.3 %collective-permute-start.32 = (bf16[2,2,4,192,128]{4,3,2,1,0:T(8,128)(2,1)}, bf16[2,2,4,192,128]{4,3,2,1,0:T(8,128)(2,1)}, u32[]{:S(2)}, u32[]{:S(2)}) collective-permute-start(bf16[2,2,4,192,128]{4,3,2,1,0:T(8,128)(2,1)} %fusion.4), channel_id=1, source_target_pairs={{0,4},{4,0},{1,5},{5,1},{2,6},{6,2},{3,7},{7,3},{8,12},{12,8},{9,1... | collective-permute-start | bytes 2359304 | tf_op jit(solution)/shard_map/ppermute | solution.py:58
  611.1 57.4 %collective-permute-start.35 = (bf16[512,512]{1,0:T(8,128)(2,1)}, bf16[512,512]{1,0:T(8,128)(2,1)}, u32[]{:S(2)}, u32[]{:S(2)}) collective-permute-start(bf16[512,512]{1,0:T(8,128)(2,1)} %get-tuple-element.245), channel_id=1, source_target_pairs={{0,24},{8,16},{16,8},{24,0},{1,25},{9,17},{17,9},{25,1},{2,26},{10... | collective-permute-start | bytes 1572872 | tf_op jit(solution)/shard_map/ppermute | solution.py:58
  612.4 57.6 %collective-permute-start.34 = (bf16[512,512]{1,0:T(8,128)(2,1)}, bf16[512,512]{1,0:T(8,128)(2,1)}, u32[]{:S(2)}, u32[]{:S(2)}) collective-permute-start(bf16[512,512]{1,0:T(8,128)(2,1)} %get-tuple-element.246), channel_id=1, source_target_pairs={{0,16},{8,24},{16,0},{24,8},{1,17},{9,25},{17,1},{25,9},{2,18},{10... | collective-permute-start | bytes 1572872 | tf_op jit(solution)/shard_map/ppermute | solution.py:58
  613.7 57.7 %collective-permute-start.33 = (bf16[512,512]{1,0:T(8,128)(2,1)}, bf16[512,512]{1,0:T(8,128)(2,1)}, u32[]{:S(2)}, u32[]{:S(2)}) collective-permute-start(bf16[512,512]{1,0:T(8,128)(2,1)} %get-tuple-element.247), channel_id=1, source_target_pairs={{0,8},{8,0},{16,24},{24,16},{1,9},{9,1},{17,25},{25,17},{2,10},{10... | collective-permute-start | bytes 1572872 | tf_op jit(solution)/shard_map/ppermute | solution.py:58
  671.4 42.8 %collective-permute-start.30 = (bf16[1,96,2048]{2,1,0:T(8,128)(2,1)}, bf16[1,96,2048]{2,1,0:T(8,128)(2,1)}, u32[]{:S(2)}, u32[]{:S(2)}) collective-permute-start(bf16[1,96,2048]{2,1,0:T(8,128)(2,1)} %bitcast.104), channel_id=1, source_target_pairs={{0,2},{1,3},{2,0},{3,1},{4,6},{5,7},{6,4},{7,5},{8,10},{9,11},{10,... | collective-permute-start | bytes 1179656 | tf_op jit(solution)/shard_map/ppermute | solution.py:58
  716.6 56.9 %collective-permute-start.31 = (bf16[2,96,2048]{2,1,0:T(8,128)(2,1)}, bf16[2,96,2048]{2,1,0:T(8,128)(2,1)}, u32[]{:S(2)}, u32[]{:S(2)}) collective-permute-start(bf16[2,96,2048]{2,1,0:T(8,128)(2,1)} %maximum_select_fusion.6), channel_id=1, source_target_pairs={{0,1},{1,0},{2,3},{3,2},{4,5},{5,4},{6,7},{7,6},{8,9},{9,8},{10,11... | collective-permute-start | bytes 2359304 | tf_op jit(solution)/shard_map/ppermute | solution.py:58
  720.3 39.5 %collective-permute-start.42 = (bf16[2,512,768]{2,1,0:T(8,128)(2,1)}, bf16[2,512,768]{2,1,0:T(8,128)(2,1)}, u32[]{:S(2)}, u32[]{:S(2)}) collective-permute-start(bf16[2,512,768]{2,1,0:T(8,128)(2,1)} %dynamic-slice_bitcast_fusion), channel_id=1, source_target_pairs={{0,16},{8,24},{16,0},{24,8},{1,17},{9,25},{17,1},{25,9},{2,18},{10... | collective-permute-start | bytes 4718600 | tf_op jit(solution)/shard_map/ppermute | solution.py:58
  724.2 41.7 %collective-permute-start.43 = (bf16[512,256]{1,0:T(8,128)(2,1)}, bf16[512,256]{1,0:T(8,128)(2,1)}, u32[]{:S(2)}, u32[]{:S(2)}) collective-permute-start(bf16[512,256]{1,0:T(8,128)(2,1)} %bitcast.358), channel_id=1, source_target_pairs={{0,4},{4,0},{1,5},{5,1},{2,6},{6,2},{3,7},{7,3},{8,12},{12,8},{9,1... | collective-permute-start | bytes 786440 | tf_op jit(solution)/shard_map/ppermute | solution.py:58
  (159 other events, 1730.0 us)
Sparse Core Ops, SparseCore 0:
  10.5 72.8 all-gather.2
  85.2 52.2 all-gather.4
  422.0 105.2 reduce-scatter.3
  529.5 135.7 reduce-scatter.5
  667.4 115.3 reduce-scatter.7

commit v4 on v3

--- a/solution.py
+++ b/solution.py
@@ -578,10 +578,10 @@
     bounds.append(used)
     gates = pad_to(jnp.stack(gates + names, axis=1), 1, 128)
 
-    up_all = both_cores(up_core)
     down = None
     for k in range(n_sh):
         down = place_columns(down_pieces[k], 1, down, my_sh ^ k, parts)
+    up_all = both_cores(tie(up_core, gates, down))
     act_low, pre_grad, gate_terms = hidden_units(
         normed_two, up_all, gate_up, down, gates, tuple(bounds)
     )
@@ -603,8 +603,11 @@
     def sum_ctx_parts(whole):
         return lax.psum_scatter(whole, "ctx", scatter_dimension=0, tiled=True)
 
-    def sum_core(left, right, urgent):
-        arrived = swap(rows_dot(left, 1, right, None, urgent), "tp", 1)
+    def sum_core(left, right, urgent, between=None):
+        sent = rows_dot(left, 1, right, None, urgent)
+        arrived = swap(sent, "tp", 1)
+        if between is not None:
+            left = tie(left, between(sent))
         return rows_dot(left, 0, right, arrived, urgent)
 
     def by_shard(own):
@@ -613,9 +616,14 @@
 
     gate_terms = gate_terms.reshape(2, half, gate_terms.shape[-1])
     gate_terms = (gate_terms[0] + swap(gate_terms[1], "tp", 1)).astype(bf16)
-    down_whole = grad_whole(act_low, 0, up_all)
-    down_piece = sum_ctx_parts(down_whole)
-    own_grad = sum_core(tie(pre_grad, down_whole), gate_up, True)
+    down_whole = []
+
+    def down_dot(after):
+        down_whole.append(grad_whole(tie(act_low, after), 0, up_all))
+        return down_whole[0]
+
+    own_grad = sum_core(pre_grad, gate_up, True, down_dot)
+    down_piece = sum_ctx_parts(down_whole[0])
     own_grad = by_shard(jnp.concatenate([own_grad, gate_terms], axis=1))
     own_mixed = sum_core(tie(act_low, *own_grad), down, False)
     own_grad = [tie(v, own_mixed) for v in others(own_grad, "shard")]
@@ -672,7 +680,8 @@
     up_piece = sum_ctx_parts(up_whole)
     down_terms = others(owned(down_piece), "shard")
     mixed_kept, mixed_sent = sum_shard([tie(v, my_branch) for v in mixed])
-    branch_low = tie(gather_tp(my_branch), up_whole, mixed_sent, *down_terms)
+    mixed_got = swap(mixed_sent, "tp", 2)
+    branch_low = tie(gather_tp(my_branch), up_whole, mixed_got, *down_terms)
     out_weight_grad = dot_rows(head_rows, branch_low).astype(bf16)
     out_terms = [
         lax.dynamic_slice_in_dim(out_weight_grad, (my_sh ^ k) * n_ctx * own, n_ctx * own, 1)
@@ -695,10 +704,7 @@
     shared_down_grad = down_parts[1].reshape(shared_hidden, own)
     out_summed = sum_pieces(out_terms, pair_sent)
     gate_parts = settle(others(owned(gate_piece), "shard"), pair_sent)
-    mixed_sum = mixed_kept + swap_z(tie(mixed_sent, pair_sent))
-    my_out = (hidden_res + from_parts(mixed_sum)).astype(bf16)
-    layer_out = gather_tp(my_out)
-    arrived = tie(arrived, my_out, *down_parts, out_summed, *gate_parts)
+    arrived = tie(arrived, *down_parts, out_summed, *gate_parts)
     key_grad, value_grad = pair_grad[..., :rows, :] + arrived.astype(f32)
     proj_grad = jnp.concatenate(
         [
@@ -737,6 +743,8 @@
         axis=1,
     )
     expert_gate_grad, shared_gate_grad = turned(*gate_parts)
+    mixed_sum = mixed_kept + tie(mixed_got, one_terms).astype(f32)
+    my_out = (hidden_res + from_parts(mixed_sum)).astype(bf16)
     out_summed = tie(out_summed, one_terms).reshape(-1, n_ctx, own).transpose(1, 0, 2)
     out_got = swap(for_other(out_summed), "ctx", 1)
     out_weight_grad = pick(out_summed, my_ctx, 0) + out_got.astype(f32)
@@ -749,34 +757,38 @@
             pick(one_half, 1 - my_y, 0).astype(bf16),
             pick(two_half, 1 - my_x, 0).astype(bf16),
         ]
-        normed_one_grad = tie(normed_one_grad, *qkv_terms)
+        qkv_terms = [swap(qkv_terms[0], "shard", 2), swap(qkv_terms[1], "shard", 1)]
     _, first_pull = jax.vjp(lambda v: rms_scale(v, first_gain), my_inputs)
     (input_norm_grad,) = first_pull(normed_one_grad)
-    my_tokens_grad = tie((hidden_grad + input_norm_grad).astype(bf16), out_got)
+    my_tokens_grad = tie((hidden_grad + input_norm_grad).astype(bf16), out_got, *(qkv_terms if in_square else []))
     tokens_grad = gather_tp(my_tokens_grad).astype(f32)
-    late_rows = lax.all_to_all(tie(late, my_tokens_grad), ("shard", "ctx"), 0, 0, tiled=True)
-    late = jnp.sum(late_rows, axis=0)
-    bias_grad = late[(experts + 3) * own :].reshape(3, local_heads, bias_own)
-    late = sum_tp_small(late[: (experts + 3) * own]).reshape(experts + 3, own)
-    up_terms = owned(tie(up_piece, my_tokens_grad, late_rows))
+    late = jnp.broadcast_to(tie(late, my_tokens_grad)[:, None], (count, n_tp, late.shape[1]))
+    late_rows = lax.all_to_all(
+        late.reshape(count * n_tp, -1), ("shard", "ctx", "tp"), 0, 0, tiled=True
+    ).reshape(late.shape)
+    at = (experts + 3) * own
+    late_sum = jnp.sum(late_rows[:, :, :at], axis=(0, 1))
+    bias_grad = jnp.sum(pick(late_rows[:, :, at:], my_tp, 1), axis=0)
+    bias_grad = bias_grad.reshape(3, local_heads, bias_own)
+    late = late_sum.reshape(experts + 3, own)
     if in_square:
-        qkv_got = [swap(qkv_terms[0], "shard", 2), swap(qkv_terms[1], "shard", 1)]
         qkv_summed = jnp.concatenate(
             [
-                kept + tie(got, my_tokens_grad, *up_terms).astype(f32)
-                for kept, got in zip(kept_terms, qkv_got)
+                kept + tie(got, my_tokens_grad).astype(f32)
+                for kept, got in zip(kept_terms, qkv_terms)
             ],
             axis=1,
         )
     else:
-        qkv_summed = sum_pieces(qkv_terms, my_tokens_grad, *up_terms)
-    up_terms = others(up_terms, "shard")
+        qkv_summed = sum_pieces(qkv_terms, my_tokens_grad)
     qkv_summed = qkv_summed.reshape(n_ctx, own, -1)
     qkv_sent = for_other(qkv_summed)
+    up_terms = others(owned(tie(up_piece, qkv_sent)), "shard")
     qkv_got = swap(qkv_sent, "ctx", 1)
     qkv_grad = pick(qkv_summed, my_ctx, 0) + qkv_got.astype(f32)
     qkv_grad = qkv_grad.reshape(own, 3, heads_width).transpose(1, 0, 2)
 
+    layer_out = gather_tp(tie(my_out, qkv_sent))
     expert_up_grad, shared_up_grad = turned(*settle(up_terms, qkv_got))
     shape = (micro, 1, rows, width)
     return (

time: 867 us -> 862 us (level)
    reduce_scatter x3, waiting for transfers between devices: 27.5 us -> 81.1 us  [sum_ctx_parts(): return lax.psum_scatter(whole, 'ctx', scatter_dimension=0, tiled=True)]
    ppermute x54 -> x52, waiting for transfers between devices: 256 us -> 216 us  [swap(): return lax.ppermute(values, axis, [(i, i ^ bit) for i in range(count)])]
    all_to_all x1, waiting for transfers between devices: 35.7 us -> 17.8 us  [exchange(): lax.all_to_all(values, ('shard', 'tp'), 0, 0, tiled=True, axis_index_grou...]
    unnamed x258 -> x254, local copies, waits for them, and re-layouts: 58.9 us -> 62.2 us
    ppermute x54 -> x52, starting transfers between devices: 56.7 us -> 56.4 us  [swap(): return lax.ppermute(values, axis, [(i, i ^ bit) for i in range(count)])]
  transfers between devices with their start and end apart: 61 -> 59, of which waited for: 25 -> 26; matrix products, arithmetic and copies ran while one was open for 22% -> 21% of each run, Pallas kernels for 8% -> 10%
where the time goes in v4:
time: 862 us; the launch traced here: 850 us
  waiting for transfers between devices  349 us (40%)
  local copies, waits for them, and re-layouts  140 us (16%)
  Pallas kernels  140 us (16%)
  other arithmetic  64.4 us (7%)
  starting transfers between devices  64.2 us (7%)
  blocking collectives  40.4 us (5%)
  matrix products  36.1 us (4%)
  between operations  16.4 us (2%)
    ppermute x52, waiting for transfers between devices, swap(): return lax.ppermute(values, axis, [(i, i ^ bit) for i in range(count)])  216 us
    reduce_scatter x3, waiting for transfers between devices, sum_ctx_parts(): return lax.psum_scatter(whole, 'ctx', scatter_dimension=0, tiled=True)  81.1 us
    unnamed x254, local copies, waits for them, and re-layouts  62.2 us
    ppermute x52, starting transfers between devices, swap(): return lax.ppermute(values, axis, [(i, i ^ bit) for i in range(count)])  56.4 us
    pallas_call x1, Pallas kernels, hidden_units(): pl.pallas_call(functools.partial(hidden_kernel, bounds, 128 if block % 38...  41.7 us
    pallas_call x3, Pallas kernels, units_dot(): pl.pallas_call(functools.partial(units_kernel, used), grid=(width // step...  41 us
    all_to_all x1, blocking collectives, exchange(): lax.all_to_all(values, ('shard', 'tp'), 0, 0, tiled=True, axis_index_grou...  40.4 us
    pallas_call x4, Pallas kernels, rows_dot(): pl.pallas_call(rows_kernel, grid=(width // step,), in_specs=specs, out_sp...  40.2 us
  transfers between devices with their start and end apart: 59, of which 26 were waited for; matrix products, arithmetic and copies ran while one was open for 21% of the time, Pallas kernels for 10%

profile of v4, /device:TPU:0, one launch (start us, length us, event | category | flops | bytes accessed | tf_op | source)
XLA Modules:
  0.0 850.1 jit_solution(4893128569206830393)
XLA Ops:
  49.1 34.2 %all-gather.3.cloned.1.call-done = bf16[2048,1536]{0,1:T(8,128)(2,1)} async-done(((bf16[512,1536]{0,1:T(8,128)(2,1)}), bf16[2048,1536]{0,1:T(8,128)(2,1)}) %all-gather.3.cloned.1.call-update) | async-done | bytes 6291472 | tf_op jit(solution)/shard_map/all_gather | solution.py:459
  98.3 31.8 %collective-permute-done.3 = bf16[2,2,4,192,128]{4,3,2,1,0:T(8,128)(2,1)S(1)} collective-permute-done((bf16[2,2,4,192,128]{4,3,2,1,0:T(8,128)(2,1)S(1)}, bf16[2,2,4,192,128]{4,3,2,1,0:T(8,128)(2,1)S(1)}, u32[]{:S(2)}, u32[]{:S(2)}) %collective-permute-start.3) | collective-permute-done | bytes 786464 | tf_op jit(solution)/shard_map/ppermute | solution.py:58
  137.7 21.0 %collective-permute-done.5.rows = bf16[2112,512]{1,0:T(8,128)(2,1)} collective-permute-done((bf16[2112,512]{1,0:T(8,128)(2,1)}, bf16[2112,512]{1,0:T(8,128)(2,1)}, u32[]{:S(2)}, u32[]{:S(2)}) %collective-permute-start.5) | collective-permute-done | bytes 2162720 | tf_op jit(solution)/shard_map/ppermute | solution.py:58
  187.4 17.8 %collective-permute-done.8.rows = bf16[2112,512]{1,0:T(8,128)(2,1)S(1)} collective-permute-done((bf16[2112,512]{1,0:T(8,128)(2,1)}, bf16[2112,512]{1,0:T(8,128)(2,1)S(1)}, u32[]{:S(2)}, u32[]{:S(2)}) %collective-permute-start.8) | collective-permute-done | bytes 2162720 | tf_op jit(solution)/shard_map/ppermute | solution.py:58
  214.5 13.8 %collective-permute-done.9.rows = bf16[1056,512]{1,0:T(8,128)(2,1)} collective-permute-done((bf16[1056,512]{1,0:T(8,128)(2,1)}, bf16[1056,512]{1,0:T(8,128)(2,1)}, u32[]{:S(2)}, u32[]{:S(2)}) %collective-permute-start.9) | collective-permute-done | bytes 1081376 | tf_op jit(solution)/shard_map/ppermute | solution.py:58
  228.4 21.8 %collective-permute-done.11.rows = bf16[1056,512]{1,0:T(8,128)(2,1)} collective-permute-done((bf16[1056,512]{1,0:T(8,128)(2,1)}, bf16[1056,512]{1,0:T(8,128)(2,1)}, u32[]{:S(2)}, u32[]{:S(2)}) %collective-permute-start.11) | collective-permute-done | bytes 1081376 | tf_op jit(solution)/shard_map/ppermute | solution.py:58
  255.7 40.4 %all_to_all.19 = bf16[8,96,2048]{2,1,0:T(8,128)(2,1)} all-to-all(bf16[8,96,2048]{2,1,0:T(8,128)(2,1)S(1)} %broadcast_in_dim.158), channel_id=1, replica_groups={{0,2,8,10,16,18,24,26},{1,3,9,11,17,19,25,27},{4,6,12,14,20,22,28,30},{..., dimensions={0} | all-to-all | bytes 6291456 | tf_op jit(solution)/shard_map/all_to_all | solution.py:116
  318.6 17.8 %all-to-all-done.1 = bf16[8,96,2048]{2,1,0:T(8,128)(2,1)} async-done(((bf16[8,96,2048]{2,1,0:T(8,128)(2,1)}), bf16[8,96,2048]{2,1,0:T(8,128)(2,1)}, u32[]{:S(2)}, u32[]{:S(2)}) %all-to-all-start.1) | async-done | bytes 3145760 | tf_op jit(solution)/shard_map/all_to_all | solution.py:116
  343.9 41.7 %shard_map.306 = (bf16[1536,1152]{1,0:T(8,128)(2,1)}, bf16[1536,2304]{1,0:T(8,128)(2,1)}, f32[1536,128]{1,0:T(8,128)}) custom-call(bf16[768,2048]{1,0:T(8,128)(2,1)} %bitcast.367, bf16[768,2048]{1,0:T(8,128)(2,1)} %bitcast.65.values_b, bf16[768,2048]{1,0:T(8,128)(2,1)} %bitcast.72.up_a.values_a, bf16[768,2048]{1,0:T(8,128)(2,1)} %bitcast.373, ...), custom_call_target="tpu_custom_call" | custom-call | flops 1000 | bytes 1000 | tf_op jit(solution)/shard_map/pallas_call | solution.py:250
  385.6 11.7 %shard_map.307 = bf16[768,2048]{1,0:T(8,128)(2,1)} custom-call(bf16[1536,2304]{1,0:T(8,128)(2,1)} %get-tuple-element.109.left.units, bf16[2304,2048]{1,0:T(8,128)(2,1)} %copy-done.4), custom_call_target="tpu_custom_call" | custom-call | flops 1000 | bytes 1000 | tf_op jit(solution)/shard_map/pallas_call | solution.py:302
  397.5 13.7 %shard_map.308 = bf16[2,1056,1024]{2,1,0:T(8,128)(2,1)} custom-call(bf16[1536,1152]{1,0:T(8,128)(2,1)} %get-tuple-element.94.units.left, bf16[768,2048]{1,0:T(8,128)(2,1)} %bitcast.72.up_a.values_a, bf16[768,2048]{1,0:T(8,128)(2,1)} %bitcast.374), custom_call_target="tpu_custom_call" | custom-call | flops 1000 | bytes 1000 | tf_op jit(solution)/shard_map/pallas_call | solution.py:330
  416.0 12.1 %shard_map.309 = bf16[768,2048]{1,0:T(8,128)(2,1)} custom-call(bf16[1536,2304]{1,0:T(8,128)(2,1)} %get-tuple-element.109.left.units, bf16[2304,2048]{1,0:T(8,128)(2,1)} %copy-done.4, bf16[768,2048]{1,0:T(8,128)(2,1)} %collective-permute-done.14.refs_0_), custom_call_target="tpu_custom_call" | custom-call | flops 1000 | bytes 1000 | tf_op jit(solution)/shard_map/pallas_call | solution.py:302
  431.4 7.9 shard_map.310
  445.3 8.5 shard_map.311
  453.8 8.6 %collective-permute-done.19 = bf16[2,96,2176]{2,1,0:T(8,128)(2,1)} collective-permute-done((bf16[2,96,2176]{2,1,0:T(8,128)(2,1)}, bf16[2,96,2176]{2,1,0:T(8,128)(2,1)}, u32[]{:S(2)}, u32[]{:S(2)}) %collective-permute-start.19) | collective-permute-done | bytes 835616 | tf_op jit(solution)/shard_map/ppermute | solution.py:58
  462.4 16.8 %collective-permute-done.18 = bf16[2,96,2176]{2,1,0:T(8,128)(2,1)} collective-permute-done((bf16[2,96,2176]{2,1,0:T(8,128)(2,1)S(1)}, bf16[2,96,2176]{2,1,0:T(8,128)(2,1)}, u32[]{:S(2)}, u32[]{:S(2)}) %collective-permute-start.18) | collective-permute-done | bytes 835616 | tf_op jit(solution)/shard_map/ppermute | solution.py:58
  483.2 13.6 %shard_map.312 = bf16[2,1056,1024]{2,1,0:T(8,128)(2,1)} custom-call(bf16[1536,2304]{1,0:T(8,128)(2,1)} %get-tuple-element.109.left.units, bf16[768,2048]{1,0:T(8,128)(2,1)} %bitcast.368, bf16[768,2048]{1,0:T(8,128)(2,1)} %bitcast.65.values_b), custom_call_target="tpu_custom_call" | custom-call | flops 1000 | bytes 1000 | tf_op jit(solution)/shard_map/pallas_call | solution.py:330
  512.3 11.7 %collective-permute-done.20 = bf16[96,2176]{1,0:T(8,128)(2,1)} collective-permute-done((bf16[96,2176]{1,0:T(8,128)(2,1)}, bf16[96,2176]{1,0:T(8,128)(2,1)}, u32[]{:S(2)}, u32[]{:S(2)}) %collective-permute-start.20) | collective-permute-done | bytes 417824 | tf_op jit(solution)/shard_map/ppermute | solution.py:58
  534.1 13.6 %shard_map.313 = bf16[2,1056,1024]{2,1,0:T(8,128)(2,1)} custom-call(bf16[1536,2304]{1,0:T(8,128)(2,1)} %get-tuple-element.109.left.units, bf16[768,2048]{1,0:T(8,128)(2,1)} %bitcast.369, bf16[768,2048]{1,0:T(8,128)(2,1)} %bitcast.65.values_b), custom_call_target="tpu_custom_call" | custom-call | flops 1000 | bytes 1000 | tf_op jit(solution)/shard_map/pallas_call | solution.py:330
  565.9 14.2 %collective-permute-done.24 = bf16[96,2048]{1,0:T(8,128)(2,1)S(1)} collective-permute-done((bf16[96,2048]{1,0:T(8,128)(2,1)S(1)}, bf16[96,2048]{1,0:T(8,128)(2,1)S(1)}, u32[]{:S(2)}, u32[]{:S(2)}) %collective-permute-start.24) | collective-permute-done | bytes 393248 | tf_op jit(solution)/shard_map/ppermute | solution.py:58
  605.6 48.2 %reduce-scatter.6.cloned.1.call-done = bf16[1,1056,1024]{2,1,0:T(8,128)(2,1)} async-done(((bf16[2,1056,1024]{2,1,0:T(8,128)(2,1)}), bf16[1,1056,1024]{2,1,0:T(8,128)(2,1)}) %reduce-scatter.6.cloned.1.call-update) | async-done | bytes 2162704 | tf_op jit(solution)/shard_map/reduce_scatter | solution.py:604
  661.5 9.3 %collective-permute-done.34.refs_1_ = bf16[1056,256]{1,0:T(8,128)(2,1)S(1)} collective-permute-done((bf16[1056,256]{1,0:T(8,128)(2,1)S(1)}, bf16[1056,256]{1,0:T(8,128)(2,1)S(1)}, u32[]{:S(2)}, u32[]{:S(2)}) %collective-permute-start.34) | collective-permute-done | bytes 540704 | tf_op jit(solution)/shard_map/ppermute | solution.py:58
  670.8 12.0 %collective-permute-done.35.refs_2_ = bf16[1056,256]{1,0:T(8,128)(2,1)S(1)} collective-permute-done((bf16[1056,256]{1,0:T(8,128)(2,1)S(1)}, bf16[1056,256]{1,0:T(8,128)(2,1)S(1)}, u32[]{:S(2)}, u32[]{:S(2)}) %collective-permute-start.35) | collective-permute-done | bytes 540704 | tf_op jit(solution)/shard_map/ppermute | solution.py:58
  766.1 32.9 %reduce-scatter.8.cloned.1.call-done = bf16[1,1056,1024]{2,1,0:T(8,128)(2,1)} async-done(((bf16[2,1056,1024]{2,1,0:T(8,128)(2,1)}), bf16[1,1056,1024]{2,1,0:T(8,128)(2,1)}) %reduce-scatter.8.cloned.1.call-update) | async-done | bytes 2162704 | tf_op jit(solution)/shard_map/reduce_scatter | solution.py:604
  (593 shorter events, 358.7 us)
Async XLA Ops:
  7.2 76.1 %all-gather.3.cloned.1.call-start = ((), (), s32[]{:S(2)}) async-start(), calls=%async_computation.6 | async-start | bytes 7864320 | tf_op jit(solution)/shard_map/all_gather | solution.py:459
  10.0 160.2 %all-gather.5.cloned.1.call-start = ((), (), s32[]{:S(2)}) async-start(), calls=%async_computation.7 | async-start | bytes 2621440 | tf_op jit(solution)/shard_map/all_gather | solution.py:461
  90.3 74.0 %collective-permute-start.4 = (bf16[2112,512]{1,0:T(8,128)(2,1)}, bf16[2112,512]{1,0:T(8,128)(2,1)}, u32[]{:S(2)}, u32[]{:S(2)}) collective-permute-start(bf16[2112,512]{1,0:T(8,128)(2,1)} %pad_maximum_fusion.2), channel_id=1, source_target_pairs={{0,16},{8,24},{16,0},{24,8},{1,17},{9,25},{17,1},{25,9},{2,18},{10... | collective-permute-start | bytes 6488072 | tf_op jit(solution)/shard_map/ppermute | solution.py:58
  91.8 66.9 %collective-permute-start.5 = (bf16[2112,512]{1,0:T(8,128)(2,1)}, bf16[2112,512]{1,0:T(8,128)(2,1)}, u32[]{:S(2)}, u32[]{:S(2)}) collective-permute-start(bf16[2112,512]{1,0:T(8,128)(2,1)} %pad_maximum_fusion.3), channel_id=1, source_target_pairs={{0,8},{8,0},{16,24},{24,16},{1,9},{9,1},{17,25},{25,17},{2,10},{10... | collective-permute-start | bytes 6488072 | tf_op jit(solution)/shard_map/ppermute | solution.py:58
  136.3 69.0 %collective-permute-start.8 = (bf16[2112,512]{1,0:T(8,128)(2,1)}, bf16[2112,512]{1,0:T(8,128)(2,1)S(1)}, u32[]{:S(2)}, u32[]{:S(2)}) collective-permute-start(bf16[2112,512]{1,0:T(8,128)(2,1)} %pad_maximum_fusion.5), channel_id=1, source_target_pairs={{0,24},{8,16},{16,8},{24,0},{1,25},{9,17},{17,9},{25,1},{2,26},{10... | collective-permute-start | bytes 6488072 | tf_op jit(solution)/shard_map/ppermute | solution.py:58
  176.5 51.9 %collective-permute-start.9 = (bf16[1056,512]{1,0:T(8,128)(2,1)}, bf16[1056,512]{1,0:T(8,128)(2,1)}, u32[]{:S(2)}, u32[]{:S(2)}) collective-permute-start(bf16[1056,512]{1,0:T(8,128)(2,1)} %pad_maximum_fusion.9), channel_id=1, source_target_pairs={{0,8},{8,0},{16,24},{24,16},{1,9},{9,1},{17,25},{25,17},{2,10},{10... | collective-permute-start | bytes 3244040 | tf_op jit(solution)/shard_map/ppermute | solution.py:58
  176.7 51.7 %collective-permute-start.10 = (bf16[1056,512]{1,0:T(8,128)(2,1)}, bf16[1056,512]{1,0:T(8,128)(2,1)}, u32[]{:S(2)}, u32[]{:S(2)}) collective-permute-start(bf16[1056,512]{1,0:T(8,128)(2,1)} %pad_maximum_fusion.10), channel_id=1, source_target_pairs={{0,16},{8,24},{16,0},{24,8},{1,17},{9,25},{17,1},{25,9},{2,18},{10... | collective-permute-start | bytes 3244040 | tf_op jit(solution)/shard_map/ppermute | solution.py:58
  178.5 71.7 %collective-permute-start.11 = (bf16[1056,512]{1,0:T(8,128)(2,1)}, bf16[1056,512]{1,0:T(8,128)(2,1)}, u32[]{:S(2)}, u32[]{:S(2)}) collective-permute-start(bf16[1056,512]{1,0:T(8,128)(2,1)} %pad_maximum_fusion.11), channel_id=1, source_target_pairs={{0,24},{8,16},{16,8},{24,0},{1,25},{9,17},{17,9},{25,1},{2,26},{10... | collective-permute-start | bytes 3244040 | tf_op jit(solution)/shard_map/ppermute | solution.py:58
  296.1 40.3 %all-to-all-start.1 = ((bf16[8,96,2048]{2,1,0:T(8,128)(2,1)}), bf16[8,96,2048]{2,1,0:T(8,128)(2,1)}, u32[]{:S(2)}, u32[]{:S(2)}) async-start(bf16[8,96,2048]{2,1,0:T(8,128)(2,1)} %broadcast_in_dim.156), calls=%async_computation.1 | async-start | bytes 6291456 | tf_op jit(solution)/shard_map/all_to_all | solution.py:116
  300.6 253.8 %reduce-scatter.4.cloned.1.call-start = ((), (), s32[]{:S(2)}) async-start(), calls=%async_computation.8 | async-start | bytes 6488064 | tf_op jit(solution)/shard_map/reduce_scatter | solution.py:604
  411.2 242.6 %reduce-scatter.6.cloned.1.call-start = ((), (), s32[]{:S(2)}) async-start(), calls=%async_computation.9 | async-start | bytes 6488064 | tf_op jit(solution)/shard_map/reduce_scatter | solution.py:604
  440.7 38.4 %collective-permute-start.18 = (bf16[2,96,2176]{2,1,0:T(8,128)(2,1)S(1)}, bf16[2,96,2176]{2,1,0:T(8,128)(2,1)}, u32[]{:S(2)}, u32[]{:S(2)}) collective-permute-start(bf16[2,96,2176]{2,1,0:T(8,128)(2,1)S(1)} %get-tuple-element.217), channel_id=1, source_target_pairs={{0,16},{8,24},{16,0},{24,8},{1,17},{9,25},{17,1},{25,9},{2,18},{10... | collective-permute-start | bytes 2506760 | tf_op jit(solution)/shard_map/ppermute | solution.py:58
  441.3 37.9 %collective-permute-start.17 = (bf16[2,96,2176]{2,1,0:T(8,128)(2,1)S(1)}, bf16[2,96,2176]{2,1,0:T(8,128)(2,1)}, u32[]{:S(2)}, u32[]{:S(2)}) collective-permute-start(bf16[2,96,2176]{2,1,0:T(8,128)(2,1)S(1)} %get-tuple-element.218), channel_id=1, source_target_pairs={{0,8},{8,0},{16,24},{24,16},{1,9},{9,1},{17,25},{25,17},{2,10},{10... | collective-permute-start | bytes 2506760 | tf_op jit(solution)/shard_map/ppermute | solution.py:58
  496.8 302.2 %reduce-scatter.8.cloned.1.call-start = ((), (), s32[]{:S(2)}) async-start(), calls=%async_computation.10 | async-start | bytes 6488064 | tf_op jit(solution)/shard_map/reduce_scatter | solution.py:604
  508.8 39.9 %collective-permute-start.23 = (bf16[2,96,2048]{2,1,0:T(8,128)(2,1)}, bf16[2,96,2048]{2,1,0:T(8,128)(2,1)}, u32[]{:S(2)}, u32[]{:S(2)}) collective-permute-start(bf16[2,96,2048]{2,1,0:T(8,128)(2,1)} %get-tuple-element.107), channel_id=1, source_target_pairs={{0,24},{8,16},{16,8},{24,0},{1,25},{9,17},{17,9},{25,1},{2,26},{10... | collective-permute-start | bytes 2359304 | tf_op jit(solution)/shard_map/ppermute | solution.py:58
  510.4 38.3 %collective-permute-start.22 = (bf16[2,96,2048]{2,1,0:T(8,128)(2,1)}, bf16[2,96,2048]{2,1,0:T(8,128)(2,1)}, u32[]{:S(2)}, u32[]{:S(2)}) collective-permute-start(bf16[2,96,2048]{2,1,0:T(8,128)(2,1)} %get-tuple-element.105), channel_id=1, source_target_pairs={{0,16},{8,24},{16,0},{24,8},{1,17},{9,25},{17,1},{25,9},{2,18},{10... | collective-permute-start | bytes 2359304 | tf_op jit(solution)/shard_map/ppermute | solution.py:58
  593.4 64.3 %collective-permute-start.33 = (bf16[512,512]{1,0:T(8,128)(2,1)}, bf16[512,512]{1,0:T(8,128)(2,1)}, u32[]{:S(2)}, u32[]{:S(2)}) collective-permute-start(bf16[512,512]{1,0:T(8,128)(2,1)} %get-tuple-element.249), channel_id=1, source_target_pairs={{0,24},{8,16},{16,8},{24,0},{1,25},{9,17},{17,9},{25,1},{2,26},{10... | collective-permute-start | bytes 1572872 | tf_op jit(solution)/shard_map/ppermute | solution.py:58
  594.9 64.3 %collective-permute-start.32 = (bf16[512,512]{1,0:T(8,128)(2,1)}, bf16[512,512]{1,0:T(8,128)(2,1)}, u32[]{:S(2)}, u32[]{:S(2)}) collective-permute-start(bf16[512,512]{1,0:T(8,128)(2,1)} %get-tuple-element.250), channel_id=1, source_target_pairs={{0,16},{8,24},{16,0},{24,8},{1,17},{9,25},{17,1},{25,9},{2,18},{10... | collective-permute-start | bytes 1572872 | tf_op jit(solution)/shard_map/ppermute | solution.py:58
  600.2 84.7 %collective-permute-start.30 = (bf16[2,2,4,192,128]{4,3,2,1,0:T(8,128)(2,1)}, bf16[2,2,4,192,128]{4,3,2,1,0:T(8,128)(2,1)}, u32[]{:S(2)}, u32[]{:S(2)}) collective-permute-start(bf16[2,2,4,192,128]{4,3,2,1,0:T(8,128)(2,1)} %fusion.5), channel_id=1, source_target_pairs={{0,4},{4,0},{1,5},{5,1},{2,6},{6,2},{3,7},{7,3},{8,12},{12,8},{9,1... | collective-permute-start | bytes 2359304 | tf_op jit(solution)/shard_map/ppermute | solution.py:58
  601.9 57.8 %collective-permute-start.31 = (bf16[512,512]{1,0:T(8,128)(2,1)}, bf16[512,512]{1,0:T(8,128)(2,1)}, u32[]{:S(2)}, u32[]{:S(2)}) collective-permute-start(bf16[512,512]{1,0:T(8,128)(2,1)} %get-tuple-element.251), channel_id=1, source_target_pairs={{0,8},{8,0},{16,24},{24,16},{1,9},{9,1},{17,25},{25,17},{2,10},{10... | collective-permute-start | bytes 1572872 | tf_op jit(solution)/shard_map/ppermute | solution.py:58
  756.4 49.9 %collective-permute-start.44 = (bf16[1,96,2048]{2,1,0:T(8,128)(2,1)S(1)}, bf16[1,96,2048]{2,1,0:T(8,128)(2,1)S(1)}, u32[]{:S(2)}, u32[]{:S(2)}) collective-permute-start(bf16[1,96,2048]{2,1,0:T(8,128)(2,1)S(1)} %bitcast.398), channel_id=1, source_target_pairs={{0,2},{1,3},{2,0},{3,1},{4,6},{5,7},{6,4},{7,5},{8,10},{9,11},{10,... | collective-permute-start | bytes 1179656 | tf_op jit(solution)/shard_map/ppermute | solution.py:58
  758.3 60.4 %collective-permute-start.48 = (bf16[256,1536]{1,0:T(8,128)(2,1)}, bf16[256,1536]{1,0:T(8,128)(2,1)}, u32[]{:S(2)}, u32[]{:S(2)}) collective-permute-start(bf16[256,1536]{1,0:T(8,128)(2,1)} %fusion.18), channel_id=1, source_target_pairs={{0,4},{4,0},{1,5},{5,1},{2,6},{6,2},{3,7},{7,3},{8,12},{12,8},{9,1... | collective-permute-start | bytes 2359304 | tf_op jit(solution)/shard_map/ppermute | solution.py:58
  761.6 49.8 %collective-permute-start.46 = (bf16[1,96,2048]{2,1,0:T(8,128)(2,1)S(1)}, bf16[1,96,2048]{2,1,0:T(8,128)(2,1)}, u32[]{:S(2)}, u32[]{:S(2)}) collective-permute-start(bf16[1,96,2048]{2,1,0:T(8,128)(2,1)S(1)} %bitcast.395), channel_id=1, source_target_pairs={{0,2},{1,3},{2,0},{3,1},{4,6},{5,7},{6,4},{7,5},{8,10},{9,11},{10,... | collective-permute-start | bytes 1179656 | tf_op jit(solution)/shard_map/ppermute | solution.py:58
  762.9 52.7 %all-to-all-start.2 = ((f32[32,1,3008]{2,1,0:T(1,128)}), f32[32,1,3008]{2,1,0:T(1,128)S(1)}, u32[]{:S(2)}, u32[]{:S(2)}) async-start(f32[32,1,3008]{2,1,0:T(1,128)} %all_to_all.14), calls=%async_computation.4 | async-start | bytes 786432 | tf_op jit(solution)/shard_map/all_to_all | solution.py:766
  (155 other events, 1613.3 us)
Sparse Core Ops, SparseCore 0:
  10.5 72.8 all-gather.2
  85.2 52.2 all-gather.4
  411.3 105.1 reduce-scatter.3
  518.8 134.9 reduce-scatter.5
  656.0 142.9 reduce-scatter.7
